TPU v7x, 512 devices: a whole 4x4x16 slice. The times are simulated.
512 devices in a mesh: xy: 32 (over z, x_lo), gz: 16 (over x_hi, y, core).
Axes of the slice: x: 4 (x_hi: 2, x_lo: 2; x = x_hi * 2 + x_lo), y: 4, z: 16, core: 2. Of those that a mesh axis runs over, the one named last changes fastest.
Arguments:
- e_check: float32 [3, 512, 384, 128], P(None, 'xy', 'gz'), may hold values from -6 to 6
- h_check: float32 [3, 512, 384, 128], P(None, 'xy', 'gz'), may hold values from -6 to 6
- adj_e_end: float32 [3, 512, 384, 128], P(None, 'xy', 'gz'), may hold values from -6 to 6
- adj_h_end: float32 [3, 512, 384, 128], P(None, 'xy', 'gz'), may hold values from -6 to 6
- background: float32 [512, 384, 128], P('xy', 'gz'), may hold values from 1 to 12
- conductivity: float32 [512, 384, 128], P('xy', 'gz'), may hold values from 0.02 to 0.5
- pattern: float32 [512, 128], P('xy'), may hold values from 0 to 8
- design_box: int32 [6], replicated, may hold values from 0 to 512, as said below
- pml_width: int32 [3], replicated, may hold values from 8 to 16
Outputs:
- adjoint_e: float32 [3, 512, 384, 128], P(None, 'xy', 'gz')
- adjoint_h: float32 [3, 512, 384, 128], P(None, 'xy', 'gz')
- pattern_grad: float32 [512, 128], P('xy', 'gz')
Inputs may be any that keep to these rules, and one draw needn't show every extreme that they name: `design_box`: x_lo < 65, x_hi > 447, likewise for y with 128 and z with 384; z_lo = 0, and along the longest grid dimension the upper end equals that dimension's cell count.
All inputs are finite; a program needn't handle non-finite values.
Results may differ from a plain program's by a relative error of at most 0.0001.
Values sent between devices are 32-bit elements; how exact they have to be, the bound alone decides.
No kernel may reach another device: no remote copies, remote signals or barrier semaphores. Data moves between devices by JAX's collectives and lax.ppermute only.
A program may use at most 64 MiB of HBM per device.

v0:
```python
import jax
import jax.numpy as jnp
from jax import lax
from jax.sharding import PartitionSpec as P

STEPS = 2


TIME_STEP = 0.5
SIGMA_PEAK = 1.0


def shifted(shard, axis, by):
    size = lax.axis_size(axis)
    pairs = [(i, i + by) for i in range(size) if 0 <= i + by < size]
    return lax.ppermute(shard, axis, pairs)


def ahead_diff(values, plane, axis):
    rest = lax.slice_in_dim(values, 1, values.shape[axis], axis=axis)
    return jnp.concatenate([rest, plane], axis) - values


def behind_diff(values, plane, axis):
    first = lax.slice_in_dim(values, 0, values.shape[axis] - 1, axis=axis)
    return values - jnp.concatenate([plane, first], axis)


def curl_plus(vector):
    front_whole = shifted(vector[:, :1], "xy", -1)
    upper_whole = shifted(vector[:, :, :1], "gz", -1)
    front_planes = front_whole[1:3]
    upper_planes = upper_whole[0:2]
    comp_x, comp_y, comp_z = (vector[0], vector[1], vector[2])
    zero_y = jnp.zeros_like(comp_x[:, :, :1])
    return jnp.stack(
        [
            ahead_diff(comp_z, zero_y, 2) - ahead_diff(comp_y, upper_planes[1], 1),
            ahead_diff(comp_x, upper_planes[0], 1) - ahead_diff(comp_z, front_planes[1], 0),
            ahead_diff(comp_y, front_planes[0], 0) - ahead_diff(comp_x, zero_y, 2),
        ]
    )


def curl_minus(vector):
    back_whole = shifted(vector[:, -1:], "xy", 1)
    lower_whole = shifted(vector[:, :, -1:], "gz", 1)
    back_planes = back_whole[1:3]
    lower_planes = lower_whole[0:2]
    comp_x, comp_y, comp_z = (vector[0], vector[1], vector[2])
    zero_y = jnp.zeros_like(comp_x[:, :, :1])
    return jnp.stack(
        [
            behind_diff(comp_z, zero_y, 2) - behind_diff(comp_y, lower_planes[1], 1),
            behind_diff(comp_x, lower_planes[0], 1) - behind_diff(comp_z, back_planes[1], 0),
            behind_diff(comp_y, back_planes[0], 0) - behind_diff(comp_x, zero_y, 2),
        ]
    )


def depth_cube(index, total, width):
    place = index.astype(jnp.float32)
    layer = width.astype(jnp.float32)
    low_side = layer - place
    high_side = place - (total - 1 - layer)
    depth = jnp.maximum(jnp.maximum(low_side, high_side), 0.0) / layer
    return depth * depth * depth


def inside_range(index, lower, upper):
    return ((index >= lower) & (index < upper)).astype(jnp.float32)


def layer_sigma(pml_width, x_index, z_index, y_index, total_x, total_z, total_y):
    return SIGMA_PEAK * (
        depth_cube(x_index, total_x, pml_width[0])[:, None, None]
        + depth_cube(z_index, total_z, pml_width[2])[None, :, None]
        + depth_cube(y_index, total_y, pml_width[1])[None, None, :]
    )


def from_permittivity(permittivity, conductivity, sigma):
    loss = (conductivity + sigma) * (TIME_STEP / 2)
    denom = permittivity + loss
    coef_a = (permittivity - loss) / denom
    coef_b = TIME_STEP / denom
    slope_a = 2.0 * loss / (denom * denom)
    slope_b = -TIME_STEP / (denom * denom)
    mag_loss = sigma * (TIME_STEP / 2)
    coef_c = (1.0 - mag_loss) / (1.0 + mag_loss)
    coef_d = TIME_STEP / (1.0 + mag_loss)
    return (coef_a, coef_b, slope_a, slope_b, coef_c, coef_d)


def march(electric, magnetic, back_e, back_h, coefs, plus_fn, minus_fn):
    coef_a, coef_b, slope_a, slope_b, coef_c, coef_d = coefs
    saved_e = []
    saved_curl = []
    for turn in range(STEPS):
        magnetic = coef_c * magnetic - coef_d * plus_fn(electric)
        curl_now = minus_fn(magnetic)
        saved_e.append(electric)
        saved_curl.append(curl_now)
        if turn + 1 < STEPS:
            electric = coef_a * electric + coef_b * curl_now
    term_list = []
    for turn in range(STEPS - 1, -1, -1):
        combined = back_h + plus_fn(coef_b * back_e)
        term_list.append(
            jnp.sum(back_e * (slope_a * saved_e[turn] + slope_b * saved_curl[turn]), axis=0)
        )
        back_h = coef_c * combined
        back_e = coef_a * back_e - minus_fn(coef_d * combined)
    return (back_e, back_h, term_list)


def shards(
    e_check, h_check, adj_e_end, adj_h_end, background, conductivity, pattern, design_box, pml_width
):
    rows_x = background.shape[0]
    rows_z = background.shape[1]
    cols_y = background.shape[2]
    x_index = lax.axis_index("xy") * rows_x + jnp.arange(rows_x)
    z_index = lax.axis_index("gz") * rows_z + jnp.arange(rows_z)
    y_index = jnp.arange(cols_y)
    total_x = rows_x * lax.axis_size("xy")
    total_z = rows_z * lax.axis_size("gz")
    mask = (
        inside_range(x_index, design_box[0], design_box[1])[:, None, None]
        * inside_range(z_index, design_box[4], design_box[5])[None, :, None]
        * inside_range(y_index, design_box[2], design_box[3])[None, None, :]
    )
    permittivity = background + mask * pattern[:, None, :]
    sigma = layer_sigma(pml_width, x_index, z_index, y_index, total_x, total_z, cols_y)
    coefs = from_permittivity(permittivity, conductivity, sigma)
    back_e, back_h, term_list = march(
        e_check, h_check, adj_e_end, adj_h_end, coefs, curl_plus, curl_minus
    )
    share_width = cols_y // lax.axis_size("gz")
    share_start = lax.axis_index("gz") * share_width
    gathered = jnp.zeros((rows_x, cols_y), jnp.float32)
    for terms in term_list:
        local_sum = jnp.sum(mask * terms, axis=1)
        gathered = gathered + lax.psum(local_sum, "gz")
    pattern_grad = lax.dynamic_slice_in_dim(gathered, share_start, share_width, 1)
    return (back_e, back_h, pattern_grad)


def solution(mesh):
    return jax.shard_map(
        shards,
        mesh=mesh,
        in_specs=(
            P(None, "xy", "gz", None),
            P(None, "xy", "gz", None),
            P(None, "xy", "gz", None),
            P(None, "xy", "gz", None),
            P("xy", "gz", None),
            P("xy", "gz", None),
            P("xy", None),
            P(),
            P(),
        ),
        out_specs=(P(None, "xy", "gz", None), P(None, "xy", "gz", None), P("xy", "gz")),
        check_vma=False,
    )
```

profile of v0, /device:TPU:409, one launch (start us, length us, event | category | flops | bytes accessed | tf_op | source)
XLA Modules:
  0.0 143.3 jit_solution(11546660920887328540)
XLA Ops:
  0.6 1.6 %slice.560 = f32[3,16,1,128]{3,2,1,0:T(1,128)} slice(f32[3,16,24,128]{3,2,1,0:T(8,128)} %param.9), slice={[0:3], [0:16], [0:1], [0:128]} | slice | bytes 49152 | tf_op jit(solution)/shard_map/slice | solution.py:31
  2.2 2.6 %collective-permute-start.8 = (f32[3,16,1,128]{3,1,2,0:T(8,128)}, f32[3,16,1,128]{3,1,2,0:T(8,128)}, u32[]{:S(2)}, u32[]{:S(2)}) collective-permute-start(f32[3,16,1,128]{3,1,2,0:T(8,128)} %bitcast.92), channel_id=1, source_target_pairs={{1,0},{2,1},{3,2},{4,3},{5,4},{6,5},{7,6},{8,7},{9,8},{10,9},{11,1... | collective-permute-start | bytes 73736 | tf_op jit(solution)/shard_map/ppermute | solution.py:16
  4.8 1.4 slice.566
  6.2 4.8 %collective-permute-start.9 = (f32[3,1,24,128]{3,2,1,0:T(8,128)}, f32[3,1,24,128]{3,2,1,0:T(8,128)}, u32[]{:S(2)}, u32[]{:S(2)}) collective-permute-start(f32[3,1,24,128]{3,2,1,0:T(8,128)} %slice.566), channel_id=1, source_target_pairs={{16,0},{32,16},{48,32},{64,48},{80,64},{96,80},{112,96},{128,112},... | collective-permute-start | bytes 110600 | tf_op jit(solution)/shard_map/ppermute | solution.py:16
  11.0 1.4 fusion.76
  14.3 1.5 %fusion.75 = (s32[1]{0:T(128)}, s32[1]{0:T(128)}, s32[1]{0:T(128)}, s32[1]{0:T(128)}, s32[1]{0:T(128)}, /*index=5*/s32[1]{0:T(128)}) fusion(s32[6]{0:T(128)} %param.16), kind=kLoop, calls=%fused_computation.192 | loop fusion | bytes 48 | tf_op jit(solution)/shard_map/slice | solution.py:129
  15.8 1.3 and_convert_fusion.2
  17.1 1.3 and_convert_fusion.1
  18.4 1.3 and_convert_fusion
  20.4 1.9 %subtract_divide_fusion = (f32[16,24,128]{2,1,0:T(8,128)S(1)}, f32[16,24,128]{2,1,0:T(8,128)}, f32[16,24,128]{2,1,0:T(8,128)}, f32[16,24,128]{2,1,0:T(8,128)S(1)...) fusion(f32[16,24,128]{2,1,0:T(8,128)S(1)} %copy-done.14, f32[16,24,128]{2,1,0:T(8,128)} %param.14, ...), kind=kLoop, calls=%fused_computation.121 | loop fusion | flops 933888 | bytes 1585152 | tf_op jit(solution)/shard_map/div | solution.py:85
  23.0 2.4 %collective-permute-start = (f32[3,16,1,128]{3,2,1,0:T(1,128)}, f32[3,16,1,128]{3,2,1,0:T(1,128)}, u32[]{:S(2)}, u32[]{:S(2)}) collective-permute-start(f32[3,16,1,128]{3,2,1,0:T(1,128)} %slice.624), channel_id=1, source_target_pairs={{1,0},{2,1},{3,2},{4,3},{5,4},{6,5},{7,6},{8,7},{9,8},{10,9},{11,1... | collective-permute-start | bytes 73736 | tf_op jit(solution)/shard_map/ppermute | solution.py:16
  26.0 2.2 %collective-permute-start.1 = (f32[3,1,24,128]{3,2,1,0:T(8,128)}, f32[3,1,24,128]{3,2,1,0:T(8,128)}, u32[]{:S(2)}, u32[]{:S(2)}) collective-permute-start(f32[3,1,24,128]{3,2,1,0:T(8,128)} %slice.630), channel_id=1, source_target_pairs={{16,0},{32,16},{48,32},{64,48},{80,64},{96,80},{112,96},{128,112},... | collective-permute-start | bytes 110600 | tf_op jit(solution)/shard_map/ppermute | solution.py:16
  28.2 0.7 fusion.59
  29.0 0.8 fusion.55
  29.9 0.8 slice.634
  30.7 0.7 fusion.74
  31.4 0.9 collective-permute-done
  32.3 0.7 slice_bitcast_fusion.48
  33.0 0.7 fusion.67
  34.0 0.8 fusion.63
  35.2 0.8 copy-done.7
  36.2 1.0 copy-done.2
  37.8 6.8 %collective-permute-start.10 = (f32[3,16,1,128]{3,1,2,0:T(8,128)S(1)}, f32[3,16,1,128]{3,1,2,0:T(8,128)S(1)}, u32[]{:S(2)}, u32[]{:S(2)}) collective-permute-start(f32[3,16,1,128]{3,1,2,0:T(8,128)S(1)} %bitcast.266), channel_id=1, source_target_pairs={{0,1},{1,2},{2,3},{3,4},{4,5},{5,6},{6,7},{7,8},{8,9},{9,10},{10,1... | collective-permute-start | bytes 73736 | tf_op jit(solution)/shard_map/ppermute | solution.py:16
  44.6 2.1 %collective-permute-start.11 = (f32[3,1,24,128]{3,2,1,0:T(8,128)S(1)}, f32[3,1,24,128]{3,2,1,0:T(8,128)S(1)}, u32[]{:S(2)}, u32[]{:S(2)}) collective-permute-start(f32[3,1,24,128]{3,2,1,0:T(8,128)S(1)} %slice.697), channel_id=1, source_target_pairs={{0,16},{16,32},{32,48},{48,64},{64,80},{80,96},{96,112},{112,128},... | collective-permute-start | bytes 110600 | tf_op jit(solution)/shard_map/ppermute | solution.py:16
  46.7 2.4 %collective-permute-start.3 = (f32[3,1,24,128]{3,2,1,0:T(8,128)S(1)}, f32[3,1,24,128]{3,2,1,0:T(8,128)S(1)}, u32[]{:S(2)}, u32[]{:S(2)}) collective-permute-start(f32[3,1,24,128]{3,2,1,0:T(8,128)S(1)} %slice.644), channel_id=1, source_target_pairs={{0,16},{16,32},{32,48},{48,64},{64,80},{80,96},{96,112},{112,128},... | collective-permute-start | bytes 110600 | tf_op jit(solution)/shard_map/ppermute | solution.py:16
  49.2 2.5 %collective-permute-start.2 = (f32[3,16,1,128]{3,1,2,0:T(8,128)S(1)}, f32[3,16,1,128]{3,1,2,0:T(8,128)S(1)}, u32[]{:S(2)}, u32[]{:S(2)}) collective-permute-start(f32[3,16,1,128]{3,1,2,0:T(8,128)S(1)} %bitcast.269), channel_id=1, source_target_pairs={{0,1},{1,2},{2,3},{3,4},{4,5},{5,6},{6,7},{7,8},{8,9},{9,10},{10,1... | collective-permute-start | bytes 73736 | tf_op jit(solution)/shard_map/ppermute | solution.py:16
  51.8 0.9 collective-permute-done.2
  53.1 1.9 %collective-permute-start.12 = (f32[3,16,1,128]{3,1,2,0:T(8,128)S(1)}, f32[3,16,1,128]{3,1,2,0:T(8,128)S(1)}, u32[]{:S(2)}, u32[]{:S(2)}) collective-permute-start(f32[3,16,1,128]{3,1,2,0:T(8,128)S(1)} %bitcast.264), channel_id=1, source_target_pairs={{1,0},{2,1},{3,2},{4,3},{5,4},{6,5},{7,6},{8,7},{9,8},{10,9},{11,1... | collective-permute-start | bytes 73736 | tf_op jit(solution)/shard_map/ppermute | solution.py:16
  55.6 5.1 %collective-permute-start.13 = (f32[3,1,24,128]{3,2,1,0:T(8,128)S(1)}, f32[3,1,24,128]{3,2,1,0:T(8,128)S(1)}, u32[]{:S(2)}, u32[]{:S(2)}) collective-permute-start(f32[3,1,24,128]{3,2,1,0:T(8,128)S(1)} %slice.713), channel_id=1, source_target_pairs={{16,0},{32,16},{48,32},{64,48},{80,64},{96,80},{112,96},{128,112},... | collective-permute-start | bytes 110600 | tf_op jit(solution)/shard_map/ppermute | solution.py:16
  60.7 1.8 %collective-permute-done.12 = f32[3,16,1,128]{3,1,2,0:T(8,128)S(1)} collective-permute-done((f32[3,16,1,128]{3,1,2,0:T(8,128)S(1)}, f32[3,16,1,128]{3,1,2,0:T(8,128)S(1)}, u32[]{:S(2)}, u32[]{:S(2)}) %collective-permute-start.12) | collective-permute-done | bytes 24608 | tf_op jit(solution)/shard_map/ppermute | solution.py:16
  63.0 8.6 %collective-permute-start.14 = (f32[3,16,1,128]{3,1,2,0:T(8,128)S(1)}, f32[3,16,1,128]{3,1,2,0:T(8,128)S(1)}, u32[]{:S(2)}, u32[]{:S(2)}) collective-permute-start(f32[3,16,1,128]{3,1,2,0:T(8,128)S(1)} %bitcast.267), channel_id=1, source_target_pairs={{0,1},{1,2},{2,3},{3,4},{4,5},{5,6},{6,7},{7,8},{8,9},{9,10},{10,1... | collective-permute-start | bytes 73736 | tf_op jit(solution)/shard_map/ppermute | solution.py:16
  71.6 1.9 %collective-permute-start.15 = (f32[3,1,24,128]{3,2,1,0:T(8,128)S(1)}, f32[3,1,24,128]{3,2,1,0:T(8,128)S(1)}, u32[]{:S(2)}, u32[]{:S(2)}) collective-permute-start(f32[3,1,24,128]{3,2,1,0:T(8,128)S(1)} %slice.727), channel_id=1, source_target_pairs={{0,16},{16,32},{32,48},{48,64},{64,80},{80,96},{96,112},{112,128},... | collective-permute-start | bytes 110600 | tf_op jit(solution)/shard_map/ppermute | solution.py:16
  73.6 4.9 %collective-permute-done.15 = f32[3,1,24,128]{3,2,1,0:T(8,128)S(1)} collective-permute-done((f32[3,1,24,128]{3,2,1,0:T(8,128)S(1)}, f32[3,1,24,128]{3,2,1,0:T(8,128)S(1)}, u32[]{:S(2)}, u32[]{:S(2)}) %collective-permute-start.15) | collective-permute-done | bytes 36896 | tf_op jit(solution)/shard_map/ppermute | solution.py:16
  78.7 0.7 copy-done.5
  80.0 0.8 fusion.53
  80.9 33.1 %psum.16 = f32[16,128]{1,0:T(8,128)S(1)} all-reduce(f32[16,128]{1,0:T(8,128)S(1)} %add.160), channel_id=1, replica_groups=mesh['xy'=32,'gz'=16] {'gz'}, use_global_device_ids=true, to_apply=%region_2.0 | all-reduce | flops 2048 | bytes 16384 | tf_op jit(solution)/shard_map/psum | solution.py:144
  114.0 1.9 %collective-permute-start.4 = (f32[3,16,1,128]{3,1,2,0:T(8,128)S(1)}, f32[3,16,1,128]{3,1,2,0:T(8,128)S(1)}, u32[]{:S(2)}, u32[]{:S(2)}) collective-permute-start(f32[3,16,1,128]{3,1,2,0:T(8,128)S(1)} %bitcast.265), channel_id=1, source_target_pairs={{1,0},{2,1},{3,2},{4,3},{5,4},{6,5},{7,6},{8,7},{9,8},{10,9},{11,1... | collective-permute-start | bytes 73736 | tf_op jit(solution)/shard_map/ppermute | solution.py:16
  116.1 0.8 slice.664
  117.5 3.3 %collective-permute-start.5 = (f32[3,1,24,128]{3,2,1,0:T(8,128)S(1)}, f32[3,1,24,128]{3,2,1,0:T(8,128)S(1)}, u32[]{:S(2)}, u32[]{:S(2)}) collective-permute-start(f32[3,1,24,128]{3,2,1,0:T(8,128)S(1)} %slice.660), channel_id=1, source_target_pairs={{16,0},{32,16},{48,32},{64,48},{80,64},{96,80},{112,96},{128,112},... | collective-permute-start | bytes 110600 | tf_op jit(solution)/shard_map/ppermute | solution.py:16
  120.9 2.5 %collective-permute-done.4 = f32[3,16,1,128]{3,1,2,0:T(8,128)S(1)} collective-permute-done((f32[3,16,1,128]{3,1,2,0:T(8,128)S(1)}, f32[3,16,1,128]{3,1,2,0:T(8,128)S(1)}, u32[]{:S(2)}, u32[]{:S(2)}) %collective-permute-start.4) | collective-permute-done | bytes 24608 | tf_op jit(solution)/shard_map/ppermute | solution.py:16
  123.4 1.0 slice_bitcast_fusion.25
  124.5 0.9 copy-done.8
  125.6 0.8 copy-done.4
  126.4 1.0 broadcast_multiply_fusion
  127.5 7.8 %collective-permute-start.6 = (f32[3,16,1,128]{3,1,2,0:T(8,128)S(1)}, f32[3,16,1,128]{3,1,2,0:T(8,128)S(1)}, u32[]{:S(2)}, u32[]{:S(2)}) collective-permute-start(f32[3,16,1,128]{3,1,2,0:T(8,128)S(1)} %bitcast.268), channel_id=1, source_target_pairs={{0,1},{1,2},{2,3},{3,4},{4,5},{5,6},{6,7},{7,8},{8,9},{9,10},{10,1... | collective-permute-start | bytes 73736 | tf_op jit(solution)/shard_map/ppermute | solution.py:16
  135.4 1.9 %collective-permute-start.7 = (f32[3,1,24,128]{3,2,1,0:T(8,128)S(1)}, f32[3,1,24,128]{3,2,1,0:T(8,128)S(1)}, u32[]{:S(2)}, u32[]{:S(2)}) collective-permute-start(f32[3,1,24,128]{3,2,1,0:T(8,128)S(1)} %slice.674), channel_id=1, source_target_pairs={{0,16},{16,32},{32,48},{48,64},{64,80},{80,96},{96,112},{112,128},... | collective-permute-start | bytes 110600 | tf_op jit(solution)/shard_map/ppermute | solution.py:16
  137.3 4.9 %collective-permute-done.7 = f32[3,1,24,128]{3,2,1,0:T(8,128)S(1)} collective-permute-done((f32[3,1,24,128]{3,2,1,0:T(8,128)S(1)}, f32[3,1,24,128]{3,2,1,0:T(8,128)S(1)}, u32[]{:S(2)}, u32[]{:S(2)}) %collective-permute-start.7) | collective-permute-done | bytes 36896 | tf_op jit(solution)/shard_map/ppermute | solution.py:16
  142.4 0.9 maximum_subtract_fusion.1
  (123 shorter events, 7.3 us)
Async XLA Ops:
  0.6 19.2 %copy-start.14 = (f32[16,24,128]{2,1,0:T(8,128)S(1)}, f32[16,24,128]{2,1,0:T(8,128)}, u32[]{:S(2)}) copy-start(f32[16,24,128]{2,1,0:T(8,128)} %param.13) | copy-start | bytes 589828
  2.2 28.5 %collective-permute-start.8 = (f32[3,16,1,128]{3,1,2,0:T(8,128)}, f32[3,16,1,128]{3,1,2,0:T(8,128)}, u32[]{:S(2)}, u32[]{:S(2)}) collective-permute-start(f32[3,16,1,128]{3,1,2,0:T(8,128)} %bitcast.92), channel_id=1, source_target_pairs={{1,0},{2,1},{3,2},{4,3},{5,4},{6,5},{7,6},{8,7},{9,8},{10,9},{11,1... | collective-permute-start | bytes 73736 | tf_op jit(solution)/shard_map/ppermute | solution.py:16
  6.2 26.8 %collective-permute-start.9 = (f32[3,1,24,128]{3,2,1,0:T(8,128)}, f32[3,1,24,128]{3,2,1,0:T(8,128)}, u32[]{:S(2)}, u32[]{:S(2)}) collective-permute-start(f32[3,1,24,128]{3,2,1,0:T(8,128)} %slice.566), channel_id=1, source_target_pairs={{16,0},{32,16},{48,32},{64,48},{80,64},{96,80},{112,96},{128,112},... | collective-permute-start | bytes 110600 | tf_op jit(solution)/shard_map/ppermute | solution.py:16
  19.7 0.7 copy-start.15
  20.4 2.0 %copy-start.1 = (f32[3,16,24,128]{3,2,1,0:T(8,128)S(1)}, f32[3,16,24,128]{3,2,1,0:T(8,128)}, u32[]{:S(2)}) copy-start(f32[3,16,24,128]{3,2,1,0:T(8,128)} %param.11) | copy-start | bytes 1769476
  22.4 5.8 %copy-start = (f32[3,16,24,128]{3,2,1,0:T(8,128)S(1)}, f32[3,16,24,128]{3,2,1,0:T(8,128)}, u32[]{:S(2)}) copy-start(f32[3,16,24,128]{3,2,1,0:T(8,128)} %param.9) | copy-start | bytes 1769476
  23.0 9.3 %collective-permute-start = (f32[3,16,1,128]{3,2,1,0:T(1,128)}, f32[3,16,1,128]{3,2,1,0:T(1,128)}, u32[]{:S(2)}, u32[]{:S(2)}) collective-permute-start(f32[3,16,1,128]{3,2,1,0:T(1,128)} %slice.624), channel_id=1, source_target_pairs={{1,0},{2,1},{3,2},{4,3},{5,4},{6,5},{7,6},{8,7},{9,8},{10,9},{11,1... | collective-permute-start | bytes 73736 | tf_op jit(solution)/shard_map/ppermute | solution.py:16
  26.0 8.0 %collective-permute-start.1 = (f32[3,1,24,128]{3,2,1,0:T(8,128)}, f32[3,1,24,128]{3,2,1,0:T(8,128)}, u32[]{:S(2)}, u32[]{:S(2)}) collective-permute-start(f32[3,1,24,128]{3,2,1,0:T(8,128)} %slice.630), channel_id=1, source_target_pairs={{16,0},{32,16},{48,32},{64,48},{80,64},{96,80},{112,96},{128,112},... | collective-permute-start | bytes 110600 | tf_op jit(solution)/shard_map/ppermute | solution.py:16
  29.9 3.9 %copy-start.12 = (f32[1,15,24,128]{3,2,1,0:T(8,128)S(1)}, f32[1,15,24,128]{3,2,1,0:T(8,128)}, u32[]{:S(2)}) copy-start(f32[1,15,24,128]{3,2,1,0:T(8,128)} %get-tuple-element.67) | copy-start | bytes 552964
  33.9 0.9 copy-start.10
  35.1 0.9 copy-start.7
  35.1 1.0 copy-start.9
  36.1 1.1 copy-start.2
  36.1 1.3 copy-start.13
  36.2 1.4 %copy-start.3 = (f32[1,16,24,128]{3,2,1,0:T(8,128)}, f32[1,16,24,128]{3,2,1,0:T(8,128)S(1)}, u32[]{:S(2)}) copy-start(f32[1,16,24,128]{3,2,1,0:T(8,128)S(1)} %get-tuple-element.35) | copy-start | bytes 589828
  37.8 14.0 %collective-permute-start.10 = (f32[3,16,1,128]{3,1,2,0:T(8,128)S(1)}, f32[3,16,1,128]{3,1,2,0:T(8,128)S(1)}, u32[]{:S(2)}, u32[]{:S(2)}) collective-permute-start(f32[3,16,1,128]{3,1,2,0:T(8,128)S(1)} %bitcast.266), channel_id=1, source_target_pairs={{0,1},{1,2},{2,3},{3,4},{4,5},{5,6},{6,7},{7,8},{8,9},{9,10},{10,1... | collective-permute-start | bytes 73736 | tf_op jit(solution)/shard_map/ppermute | solution.py:16
  44.6 8.1 %collective-permute-start.11 = (f32[3,1,24,128]{3,2,1,0:T(8,128)S(1)}, f32[3,1,24,128]{3,2,1,0:T(8,128)S(1)}, u32[]{:S(2)}, u32[]{:S(2)}) collective-permute-start(f32[3,1,24,128]{3,2,1,0:T(8,128)S(1)} %slice.697), channel_id=1, source_target_pairs={{0,16},{16,32},{32,48},{48,64},{64,80},{80,96},{96,112},{112,128},... | collective-permute-start | bytes 110600 | tf_op jit(solution)/shard_map/ppermute | solution.py:16
  46.7 8.4 %collective-permute-start.3 = (f32[3,1,24,128]{3,2,1,0:T(8,128)S(1)}, f32[3,1,24,128]{3,2,1,0:T(8,128)S(1)}, u32[]{:S(2)}, u32[]{:S(2)}) collective-permute-start(f32[3,1,24,128]{3,2,1,0:T(8,128)S(1)} %slice.644), channel_id=1, source_target_pairs={{0,16},{16,32},{32,48},{48,64},{64,80},{80,96},{96,112},{112,128},... | collective-permute-start | bytes 110600 | tf_op jit(solution)/shard_map/ppermute | solution.py:16
  49.2 3.5 %collective-permute-start.2 = (f32[3,16,1,128]{3,1,2,0:T(8,128)S(1)}, f32[3,16,1,128]{3,1,2,0:T(8,128)S(1)}, u32[]{:S(2)}, u32[]{:S(2)}) collective-permute-start(f32[3,16,1,128]{3,1,2,0:T(8,128)S(1)} %bitcast.269), channel_id=1, source_target_pairs={{0,1},{1,2},{2,3},{3,4},{4,5},{5,6},{6,7},{7,8},{8,9},{9,10},{10,1... | collective-permute-start | bytes 73736 | tf_op jit(solution)/shard_map/ppermute | solution.py:16
  53.1 9.3 %collective-permute-start.12 = (f32[3,16,1,128]{3,1,2,0:T(8,128)S(1)}, f32[3,16,1,128]{3,1,2,0:T(8,128)S(1)}, u32[]{:S(2)}, u32[]{:S(2)}) collective-permute-start(f32[3,16,1,128]{3,1,2,0:T(8,128)S(1)} %bitcast.264), channel_id=1, source_target_pairs={{1,0},{2,1},{3,2},{4,3},{5,4},{6,5},{7,6},{8,7},{9,8},{10,9},{11,1... | collective-permute-start | bytes 73736 | tf_op jit(solution)/shard_map/ppermute | solution.py:16
  55.6 6.9 %collective-permute-start.13 = (f32[3,1,24,128]{3,2,1,0:T(8,128)S(1)}, f32[3,1,24,128]{3,2,1,0:T(8,128)S(1)}, u32[]{:S(2)}, u32[]{:S(2)}) collective-permute-start(f32[3,1,24,128]{3,2,1,0:T(8,128)S(1)} %slice.713), channel_id=1, source_target_pairs={{16,0},{32,16},{48,32},{64,48},{80,64},{96,80},{112,96},{128,112},... | collective-permute-start | bytes 110600 | tf_op jit(solution)/shard_map/ppermute | solution.py:16
  63.0 10.6 %collective-permute-start.14 = (f32[3,16,1,128]{3,1,2,0:T(8,128)S(1)}, f32[3,16,1,128]{3,1,2,0:T(8,128)S(1)}, u32[]{:S(2)}, u32[]{:S(2)}) collective-permute-start(f32[3,16,1,128]{3,1,2,0:T(8,128)S(1)} %bitcast.267), channel_id=1, source_target_pairs={{0,1},{1,2},{2,3},{3,4},{4,5},{5,6},{6,7},{7,8},{8,9},{9,10},{10,1... | collective-permute-start | bytes 73736 | tf_op jit(solution)/shard_map/ppermute | solution.py:16
  71.6 6.8 %collective-permute-start.15 = (f32[3,1,24,128]{3,2,1,0:T(8,128)S(1)}, f32[3,1,24,128]{3,2,1,0:T(8,128)S(1)}, u32[]{:S(2)}, u32[]{:S(2)}) collective-permute-start(f32[3,1,24,128]{3,2,1,0:T(8,128)S(1)} %slice.727), channel_id=1, source_target_pairs={{0,16},{16,32},{32,48},{48,64},{64,80},{80,96},{96,112},{112,128},... | collective-permute-start | bytes 110600 | tf_op jit(solution)/shard_map/ppermute | solution.py:16
  78.5 0.9 copy-start.5
  78.5 1.0 copy-start.6
  114.0 9.3 %collective-permute-start.4 = (f32[3,16,1,128]{3,1,2,0:T(8,128)S(1)}, f32[3,16,1,128]{3,1,2,0:T(8,128)S(1)}, u32[]{:S(2)}, u32[]{:S(2)}) collective-permute-start(f32[3,16,1,128]{3,1,2,0:T(8,128)S(1)} %bitcast.265), channel_id=1, source_target_pairs={{1,0},{2,1},{3,2},{4,3},{5,4},{6,5},{7,6},{8,7},{9,8},{10,9},{11,1... | collective-permute-start | bytes 73736 | tf_op jit(solution)/shard_map/ppermute | solution.py:16
  117.5 5.8 %collective-permute-start.5 = (f32[3,1,24,128]{3,2,1,0:T(8,128)S(1)}, f32[3,1,24,128]{3,2,1,0:T(8,128)S(1)}, u32[]{:S(2)}, u32[]{:S(2)}) collective-permute-start(f32[3,1,24,128]{3,2,1,0:T(8,128)S(1)} %slice.660), channel_id=1, source_target_pairs={{16,0},{32,16},{48,32},{64,48},{80,64},{96,80},{112,96},{128,112},... | collective-permute-start | bytes 110600 | tf_op jit(solution)/shard_map/ppermute | solution.py:16
  124.5 0.9 copy-start.8
  124.5 1.0 copy-start.11
  125.5 0.9 copy-start.4
  127.5 9.8 %collective-permute-start.6 = (f32[3,16,1,128]{3,1,2,0:T(8,128)S(1)}, f32[3,16,1,128]{3,1,2,0:T(8,128)S(1)}, u32[]{:S(2)}, u32[]{:S(2)}) collective-permute-start(f32[3,16,1,128]{3,1,2,0:T(8,128)S(1)} %bitcast.268), channel_id=1, source_target_pairs={{0,1},{1,2},{2,3},{3,4},{4,5},{5,6},{6,7},{7,8},{8,9},{9,10},{10,1... | collective-permute-start | bytes 73736 | tf_op jit(solution)/shard_map/ppermute | solution.py:16
  135.4 6.8 %collective-permute-start.7 = (f32[3,1,24,128]{3,2,1,0:T(8,128)S(1)}, f32[3,1,24,128]{3,2,1,0:T(8,128)S(1)}, u32[]{:S(2)}, u32[]{:S(2)}) collective-permute-start(f32[3,1,24,128]{3,2,1,0:T(8,128)S(1)} %slice.674), channel_id=1, source_target_pairs={{0,16},{16,32},{32,48},{48,64},{64,80},{80,96},{96,112},{112,128},... | collective-permute-start | bytes 110600 | tf_op jit(solution)/shard_map/ppermute | solution.py:16
where the time goes:
time: 144 us; the launch traced here: 143 us
  starting transfers between devices  58.2 us (40%)
  blocking collectives  33.1 us (23%)
  local copies, waits for them, and re-layouts  21.4 us (15%)
  waiting for transfers between devices  15.8 us (11%)
  other arithmetic  11.4 us (8%)
  between operations  3.36 us (2%)
    ppermute x16, starting transfers between devices, shifted(): return lax.ppermute(shard, axis, pairs)  58.2 us
    psum x1, blocking collectives, shards(): gathered = gathered + lax.psum(local_sum, 'gz')  33.1 us
    ppermute x16, waiting for transfers between devices, shifted(): return lax.ppermute(shard, axis, pairs)  15.8 us
    unnamed x33, local copies, waits for them, and re-layouts  6.17 us
    slice x16, local copies, waits for them, and re-layouts, ahead_diff(): rest = lax.slice_in_dim(values, 1, values.shape[axis], axis=axis)  4.59 us
    convert_element_type x3, other arithmetic, inside_range(): return ((index >= lower) & (index < upper)).astype(jnp.float32)  3.84 us
  transfers between devices with their start and end apart: 16, of which 6 were waited for; matrix products, arithmetic and copies ran while one was open for 13% of the time, Pallas kernels for 0%

commit v1 on v0

v1 whole, which is shorter than its diff:
```python
import functools

import jax
import jax.numpy as jnp
from jax import lax
from jax.experimental import pallas as pl
from jax.experimental.pallas import tpu as pltpu
from jax.sharding import PartitionSpec as P

TIME_STEP = 0.5
SIGMA_PEAK = 1.0
HALF = TIME_STEP / 2
EXT = 8
VMEM_LIMIT = 32 * 1024 * 1024

FIRST_ROWS = (2, 2, 1, 1, 1, 1, 2, 2, 1, 1, 1, 1, 2, 2)
LAST_ROWS = (2, 2, 2, 2, 2, 1, 2, 2, 2, 2, 2, 1, 2, 2)
FIRST_AT = tuple(sum(FIRST_ROWS[:k]) for k in range(14))
LAST_AT = tuple(sum(LAST_ROWS[:k]) for k in range(14))
FIRST_SIZE = -(-sum(FIRST_ROWS) // 8) * 8
LAST_SIZE = -(-sum(LAST_ROWS) // 8) * 8
SLOTS = 14
BACK_PLANES = 11
FRONT_PLANES = 9

ANY = pl.BlockSpec(memory_space=pl.ANY)
VMEM = pl.BlockSpec(memory_space=pltpu.VMEM)
SMEM = pl.BlockSpec(memory_space=pltpu.SMEM)


def shifted(shard, axis, by):
    size = lax.axis_size(axis)
    pairs = [(i, i + by) for i in range(size) if 0 <= i + by < size]
    return lax.ppermute(shard, axis, pairs)


def slot(refs, k):
    return refs[k // 3].at[k % 3] if k < 12 else refs[k - 8]


def edge_rows(*refs):
    fields, outs, scratch = refs[:6], refs[6:8], refs[8:]
    first_out, last_out = outs
    tiles, sems = scratch[:12], scratch[12]
    rows_z = fields[4].shape[1]
    copies = []
    for k, ref in enumerate(fields):
        for side, start in enumerate((0, rows_z - EXT)):
            src = ref.at[:, :, pl.ds(start, EXT), :] if k < 4 else ref.at[:, pl.ds(start, EXT), :]
            copy = pltpu.make_async_copy(src, tiles[2 * k + side], sems.at[2 * k + side])
            copy.start()
            copies.append(copy)
    for copy in copies:
        copy.wait()

    def plane(x, carry):
        for k in range(SLOTS):
            pair = (tiles[2 * (k // 3)], tiles[2 * (k // 3) + 1]) if k < 12 else (
                tiles[2 * (k - 8)], tiles[2 * (k - 8) + 1])
            low = pair[0].at[k % 3, x] if k < 12 else pair[0].at[x]
            high = pair[1].at[k % 3, x] if k < 12 else pair[1].at[x]
            count = FIRST_ROWS[k]
            first_out[x, pl.ds(FIRST_AT[k], count), :] = low[pl.ds(0, count), :]
            count = LAST_ROWS[k]
            last_out[x, pl.ds(LAST_AT[k], count), :] = high[pl.ds(EXT - count, count), :]
        return carry

    lax.fori_loop(0, fields[4].shape[0], plane, 0)


def lane_index(shape):
    return lax.broadcasted_iota(jnp.int32, shape, 1)


def y_ahead(v):
    cols = v.shape[1]
    moved = pltpu.roll(v, cols - 1, 1)
    return jnp.where(lane_index(v.shape) == cols - 1, 0.0, moved) - v


def y_behind(v):
    moved = pltpu.roll(v, 1, 1)
    return v - jnp.where(lane_index(v.shape) == 0, 0.0, moved)


def z_ahead(v):
    return pltpu.roll(v, v.shape[0] - 1, 0) - v


def z_behind(v):
    return v - pltpu.roll(v, 1, 0)


def plus_x(v):
    return y_ahead(v[2]) - z_ahead(v[1])


def plus_y(v, next_z):
    return z_ahead(v[0]) - (next_z - v[2])


def plus_z(v, next_y):
    return (next_y - v[1]) - y_ahead(v[0])


def plus(v, next_y, next_z):
    return plus_x(v), plus_y(v, next_z), plus_z(v, next_y)


def minus(v, prev_y, prev_z):
    return (
        y_behind(v[2]) - z_behind(v[1]),
        z_behind(v[0]) - (v[2] - prev_z),
        (v[1] - prev_y) - y_behind(v[0]),
    )


def minus_first(v_x, prev_y, prev_z):
    return None, z_behind(v_x) + prev_z, -prev_y - y_behind(v_x)


def depth_cube(place, total, layer):
    depth = jnp.maximum(jnp.maximum(layer - place, place - (total - 1 - layer)), 0.0) / layer
    return depth * depth * depth


class Grid:
    def __init__(self, box, pml, pos, rows_x, rows_z, cols, total_x, total_z):
        rows = rows_z + EXT
        self.shape = (rows, cols)
        self.box = box
        self.width_x = pml[0].astype(jnp.float32)
        self.total_x = total_x
        self.x_start = pos[0] * rows_x
        self.rows_z = rows_z
        row = lax.broadcasted_iota(jnp.int32, self.shape, 0)
        z = pos[1] * rows_z + jnp.where(row < rows_z + EXT // 2, row, row - rows)
        y = lane_index(self.shape)
        self.inside = (z >= 0) & (z < total_z)
        self.sigma_zy = depth_cube(
            z.astype(jnp.float32), total_z, pml[2].astype(jnp.float32)
        ) + depth_cube(y.astype(jnp.float32), cols, pml[1].astype(jnp.float32))
        picked = (z >= box[4]) & (z < box[5]) & (y >= box[2]) & (y < box[3])
        self.mask_zy = jnp.where(picked, 1.0, 0.0)

    def sigma(self, x):
        place = jnp.full((1, self.shape[1]), (self.x_start + x).astype(jnp.float32))
        return SIGMA_PEAK * (self.sigma_zy + depth_cube(place, self.total_x, self.width_x))

    def mask_x(self, x):
        at = self.x_start + x
        return jnp.where((at >= self.box[0]) & (at < self.box[1]), 1.0, 0.0)

    def magnetic(self, sigma, x_inside=None):
        inside = self.inside if x_inside is None else self.inside & x_inside
        inverse = 1.0 / (1.0 + HALF * sigma)
        return (
            jnp.where(inside, 2.0 * inverse - 1.0, 0.0),
            jnp.where(inside, TIME_STEP * inverse, 0.0),
        )

    def electric(self, x, background, conductivity, pattern_row, sigma):
        permittivity = background + self.mask_zy * (pattern_row * self.mask_x(x))
        loss = HALF * (conductivity + sigma)
        inverse = jnp.where(self.inside, 1.0 / (permittivity + loss), 0.0)
        return (permittivity - loss) * inverse, TIME_STEP * inverse, loss, inverse


def full_plane(ref, tile_ref, k, x):
    own = ref[k % 3, x] if k < 12 else ref[x]
    return jnp.concatenate([own, tile_ref[k, x]], axis=0)


def fill_tile(tile_ref, above, below, k, x):
    count = FIRST_ROWS[k]
    tile_ref[k, x, pl.ds(0, count), :] = above[x, pl.ds(FIRST_AT[k], count), :]
    count = LAST_ROWS[k]
    tile_ref[k, x, pl.ds(EXT - count, count), :] = below[x, pl.ds(LAST_AT[k], count), :]


def field_ref(fields, k):
    return fields[k // 3] if k < 12 else fields[k - 8]


def triple(fields, tile_ref, group, x):
    return tuple(full_plane(fields[group], tile_ref, 3 * group + c, x) for c in range(3))


def edge_planes(geometry, pos, box, pml, pattern, *refs):
    fields, (above, below), (to_next, to_prev, tile) = refs[:6], refs[6:8], refs[8:]
    rows_x = geometry[0]
    grid = Grid(box, pml, (pos[0], pos[1]), *geometry)

    def fill(x, carry):
        for k in range(SLOTS):
            tile[k, x] = jnp.zeros(tile.shape[2:], jnp.float32)
            fill_tile(tile, above, below, k, x)
        return carry

    lax.fori_loop(0, rows_x, fill, 0)

    def coefs(x):
        sigma = grid.sigma(x)
        coef_a, coef_b, _, _ = grid.electric(
            x,
            full_plane(fields[4], tile, 12, x),
            full_plane(fields[5], tile, 13, x),
            pattern[pl.ds(x, 1), :],
            sigma,
        )
        return (coef_a, coef_b) + grid.magnetic(sigma)

    def load(x):
        return [triple(fields, tile, g, x) for g in range(4)]

    one, two = rows_x - 2, rows_x - 1
    e1, h1, p1, q1 = load(one)
    e2, h2, p2, q2 = load(two)
    _, cb1, da1, db1 = coefs(one)
    ca2, cb2, da2, db2 = coefs(two)
    before = (
        da1 * h1[1] - db1 * plus_y(e1, e2[2]),
        da1 * h1[2] - db1 * plus_z(e1, e2[1]),
    )
    partial = [da2 * h - db2 * c for h, c in zip(h2, plus(e2, 0.0, 0.0))]
    curl = minus_first(partial[0], before[0], before[1])
    to_next[0], to_next[1] = partial[1], partial[2]
    to_next[2] = ca2 * e2[0]
    to_next[3] = ca2 * e2[1] + cb2 * curl[1]
    to_next[4] = ca2 * e2[2] + cb2 * curl[2]
    to_next[5] = cb2
    u1 = [cb1 * v for v in p1]
    u2 = [cb2 * v for v in p2]
    before = (
        db1 * (q1[1] + plus_y(u1, u2[2])),
        db1 * (q1[2] + plus_z(u1, u2[1])),
    )
    partial = [q + c for q, c in zip(q2, plus(u2, 0.0, 0.0))]
    curl = minus_first(db2 * partial[0], before[0], before[1])
    to_next[6], to_next[7] = partial[1], partial[2]
    to_next[8] = ca2 * p2[0]
    to_next[9] = ca2 * p2[1] - curl[1]
    to_next[10] = ca2 * p2[2] - curl[2]

    e1, h1, p1, q1 = load(0)
    e2, _, p2, _ = load(1)
    ca1, cb1, da1, db1 = coefs(0)
    _, cb2, _, _ = coefs(1)
    whole = [da1 * h - db1 * c for h, c in zip(h1, plus(e1, e2[1], e2[2]))]
    curl = minus(whole, 0.0, 0.0)
    to_prev[0], to_prev[1] = e1[1], e1[2]
    to_prev[2] = ca1 * e1[1] + cb1 * curl[1]
    to_prev[3] = ca1 * e1[2] + cb1 * curl[2]
    to_prev[4] = cb1
    u1 = [cb1 * v for v in p1]
    whole = [db1 * (q + c) for q, c in zip(q1, plus(u1, cb2 * p2[1], cb2 * p2[2]))]
    curl = minus(whole, 0.0, 0.0)
    to_prev[5], to_prev[6] = u1[1], u1[2]
    to_prev[7] = ca1 * p1[1] - curl[1]
    to_prev[8] = ca1 * p1[2] - curl[2]


def sweep(geometry, pos, box, pml, pattern, *refs):
    fields, (tile, back, front) = refs[:6], refs[6:9]
    out_e, out_h, out_sum = refs[9:12]
    mag, adj_mag, ele, adj_ele, ca, cb, da, db, loss_at, inv_at, sums = refs[12:]
    rows_x, rows_z, cols = geometry[:3]
    grid = Grid(box, pml, (pos[0], pos[1]), *geometry)
    last = rows_x - 1

    def coefs(x, carry):
        sigma = grid.sigma(x)
        ca[x + 1], cb[x + 1], loss_at[x], inv_at[x] = grid.electric(
            x,
            full_plane(fields[4], tile, 12, x),
            full_plane(fields[5], tile, 13, x),
            pattern[pl.ds(x, 1), :],
            sigma,
        )
        da[x + 1], db[x + 1] = grid.magnetic(sigma)
        return carry

    lax.fori_loop(0, rows_x, coefs, 0)
    cb[rows_x + 1] = front[4]

    at = jnp.full(grid.shape, grid.x_start)
    da0, db0 = grid.magnetic(grid.sigma(-1), at > 0)
    cb0 = back[5]
    e_y, e_z = full_plane(fields[0], tile, 1, 0), full_plane(fields[0], tile, 2, 0)
    h_y, h_z = back[0] + db0 * e_z, back[1] - db0 * e_y
    ele[0, 0] = back[2] + cb0 * (y_behind(h_z) - z_behind(h_y))
    ele[1, 0] = back[3] - cb0 * h_z
    ele[2, 0] = back[4] + cb0 * h_y
    p_y, p_z = full_plane(fields[2], tile, 7, 0), full_plane(fields[2], tile, 8, 0)
    m_y, m_z = back[6] - cb[1] * p_z, back[7] + cb[1] * p_y
    n_y, n_z = db0 * m_y, db0 * m_z
    adj_ele[0, 0] = back[8] - (y_behind(n_z) - z_behind(n_y))
    adj_ele[1, 0] = back[9] + n_z
    adj_ele[2, 0] = back[10] - n_y
    da[0], db[0], cb[0] = da0, db0, cb0

    def first(x, carry):
        at_last = jnp.full(grid.shape, x) == last
        ahead = jnp.minimum(x + 1, last)
        e, h, p, q = [triple(fields, tile, g, x) for g in range(4)]
        a, b, c, d = ca[x + 1], cb[x + 1], da[x + 1], db[x + 1]
        e_y = jnp.where(at_last, front[0], full_plane(fields[0], tile, 1, ahead))
        e_z = jnp.where(at_last, front[1], full_plane(fields[0], tile, 2, ahead))
        new_h = [c * v - d * w for v, w in zip(h, plus(e, e_y, e_z))]
        prev_h, prev_m = carry
        curl = minus(new_h, *prev_h)
        b_ahead = cb[ahead + 1]
        u_y = jnp.where(at_last, front[5], b_ahead * full_plane(fields[2], tile, 7, ahead))
        u_z = jnp.where(at_last, front[6], b_ahead * full_plane(fields[2], tile, 8, ahead))
        new_m = [v + w for v, w in zip(q, plus([b * v for v in p], u_y, u_z))]
        scaled = [d * v for v in new_m]
        adj_curl = minus(scaled, *prev_m)
        dot_e, dot_r = 0.0, 0.0
        for k in range(3):
            mag[k, x + 1] = new_h[k]
            adj_mag[k, x + 1] = new_m[k]
            ele[k, x + 1] = a * e[k] + b * curl[k]
            new_p = a * p[k] - adj_curl[k]
            adj_ele[k, x + 1] = new_p
            dot_e = dot_e + new_p[:rows_z] * e[k][:rows_z]
            dot_r = dot_r + new_p[:rows_z] * curl[k][:rows_z]
        inverse = inv_at[x, pl.ds(0, rows_z), :]
        sums[x] = inverse * inverse * (
            2.0 * loss_at[x, pl.ds(0, rows_z), :] * dot_e - TIME_STEP * dot_r
        )
        return new_h[1:], scaled[1:]

    lax.fori_loop(0, rows_x, first, ([h_y, h_z], [n_y, n_z]))

    cb_after = front[4]
    ele[1, rows_x + 1] = front[2] + cb_after * mag[2, rows_x]
    ele[2, rows_x + 1] = front[3] - cb_after * mag[1, rows_x]
    d_last = db[rows_x]
    adj_ele[1, rows_x + 1] = front[7] - d_last * adj_mag[2, rows_x]
    adj_ele[2, rows_x + 1] = front[8] + d_last * adj_mag[1, rows_x]

    e = [ele[k, 0] for k in range(3)]
    before_h = [da0 * h_y - db0 * plus_y(e, ele[2, 1]), da0 * h_z - db0 * plus_z(e, ele[1, 1])]
    u = [cb0 * adj_ele[k, 0] for k in range(3)]
    before_m = [
        db0 * (da0 * m_y + plus_y(u, cb[1] * adj_ele[2, 1])),
        db0 * (da0 * m_z + plus_z(u, cb[1] * adj_ele[1, 1])),
    ]

    mask_own = grid.mask_zy[:rows_z]

    def second(x, carry):
        e = [ele[k, x + 1] for k in range(3)]
        p1 = [adj_ele[k, x + 1] for k in range(3)]
        a, b, c, d = ca[x + 1], cb[x + 1], da[x + 1], db[x + 1]
        new_h = [
            c * mag[k, x + 1] - d * w
            for k, w in enumerate(plus(e, ele[1, x + 2], ele[2, x + 2]))
        ]
        prev_h, prev_m = carry
        curl = minus(new_h, *prev_h)
        b_ahead = cb[x + 2]
        u = [b * v for v in p1]
        new_m = [
            c * adj_mag[k, x + 1] + w
            for k, w in enumerate(plus(u, b_ahead * adj_ele[1, x + 2], b_ahead * adj_ele[2, x + 2]))
        ]
        scaled = [d * v for v in new_m]
        adj_curl = minus(scaled, *prev_m)
        dot_e, dot_r = 0.0, 0.0
        for k in range(3):
            out_h[k, x] = c[:rows_z] * new_m[k][:rows_z]
            out_e[k, x] = a[:rows_z] * p1[k][:rows_z] - adj_curl[k][:rows_z]
            p = fields[2][k, x]
            dot_e = dot_e + p * e[k][:rows_z]
            dot_r = dot_r + p * curl[k][:rows_z]
        inverse = inv_at[x, pl.ds(0, rows_z), :]
        terms = sums[x] + inverse * inverse * (
            2.0 * loss_at[x, pl.ds(0, rows_z), :] * dot_e - TIME_STEP * dot_r
        )
        picked = terms * (mask_own * grid.mask_x(x))
        total = picked[0:8]
        for start in range(8, rows_z, 8):
            total = total + picked[start : start + 8]
        out_sum[pl.ds(x, 1), :] = jnp.sum(total, axis=0, keepdims=True)
        return new_h[1:], scaled[1:]

    lax.fori_loop(0, rows_x, second, (before_h, before_m))


def shards(
    e_check, h_check, adj_e_end, adj_h_end, background, conductivity, pattern, design_box, pml_width
):
    rows_x, rows_z, cols = background.shape
    size_x, size_z = lax.axis_size("xy"), lax.axis_size("gz")
    geometry = (rows_x, rows_z, cols, rows_x * size_x, rows_z * size_z)
    pos = jnp.stack([lax.axis_index("xy"), lax.axis_index("gz")]).astype(jnp.int32)
    fields = (e_check, h_check, adj_e_end, adj_h_end, background, conductivity)
    f32 = jnp.float32
    params = pltpu.CompilerParams(vmem_limit_bytes=VMEM_LIMIT)

    def tiles(ref):
        return pltpu.VMEM(ref.shape[:-2] + (EXT, cols), f32)

    first_rows, last_rows = pl.pallas_call(
        edge_rows,
        out_shape=(
            jax.ShapeDtypeStruct((rows_x, FIRST_SIZE, cols), f32),
            jax.ShapeDtypeStruct((rows_x, LAST_SIZE, cols), f32),
        ),
        in_specs=[ANY] * 6,
        out_specs=[VMEM] * 2,
        scratch_shapes=[tiles(ref) for ref in fields for _ in range(2)]
        + [pltpu.SemaphoreType.DMA((12,))],
        compiler_params=params,
        name="edge_rows",
    )(*fields)
    above = shifted(first_rows, "gz", -1)
    below = shifted(last_rows, "gz", 1)

    plane = (rows_z + EXT, cols)
    to_next, to_prev, tile = pl.pallas_call(
        functools.partial(edge_planes, geometry),
        out_shape=(
            jax.ShapeDtypeStruct((BACK_PLANES,) + plane, f32),
            jax.ShapeDtypeStruct((FRONT_PLANES,) + plane, f32),
            jax.ShapeDtypeStruct((SLOTS, rows_x, EXT, cols), f32),
        ),
        in_specs=[SMEM] * 3 + [VMEM] * 9,
        out_specs=[VMEM] * 3,
        compiler_params=params,
        name="edge_planes",
    )(pos, design_box, pml_width, pattern, *fields, above, below)
    back = shifted(to_next, "xy", 1)
    front = shifted(to_prev, "xy", -1)

    def planes(*lead):
        return pltpu.VMEM(lead + plane, f32)

    count = rows_x + 2
    back_e, back_h, local_sum = pl.pallas_call(
        functools.partial(sweep, geometry),
        out_shape=(
            jax.ShapeDtypeStruct(e_check.shape, f32),
            jax.ShapeDtypeStruct(e_check.shape, f32),
            jax.ShapeDtypeStruct((rows_x, cols), f32),
        ),
        in_specs=[SMEM] * 3 + [VMEM] * 10,
        out_specs=[VMEM] * 3,
        scratch_shapes=[planes(3, count)] * 4
        + [planes(count)] * 4
        + [planes(rows_x)] * 2
        + [pltpu.VMEM((rows_x, rows_z, cols), f32)],
        compiler_params=params,
        name="sweep",
    )(pos, design_box, pml_width, pattern, *fields, tile, back, front)

    share = cols // size_z
    parts = lax.all_to_all(local_sum.T, "gz", split_axis=0, concat_axis=0, tiled=True)
    pattern_grad = jnp.sum(parts.reshape(size_z, share, rows_x), axis=0).T
    return (back_e, back_h, pattern_grad)


def solution(mesh):
    field = P(None, "xy", "gz", None)
    cell = P("xy", "gz", None)
    return jax.shard_map(
        shards,
        mesh=mesh,
        in_specs=(field, field, field, field, cell, cell, P("xy", None), P(), P()),
        out_specs=(field, field, P("xy", "gz")),
        check_vma=False,
    )
```

time: 144 us -> 58.8 us (0.41)
  the two profiles are of different devices: /device:TPU:409 before, /device:TPU:227 now
where the time goes in v1:
time: 58.8 us; the launch traced here: 58.4 us
  blocking collectives  15.9 us (27%)
  starting transfers between devices  12.3 us (21%)
  waiting for transfers between devices  11.2 us (19%)
  Pallas kernels  9.8 us (17%)
  local copies, waits for them, and re-layouts  6.92 us (12%)
  other arithmetic  1.36 us (2%)
  between operations  0.82 us (1%)
    all_to_all x1, blocking collectives, shards(): lax.all_to_all(local_sum.T, 'gz', split_axis=0, concat_axis=0, tiled=True)  15.9 us
    ppermute x4, starting transfers between devices, shifted(): return lax.ppermute(shard, axis, pairs)  12.3 us
    ppermute x4, waiting for transfers between devices, shifted(): return lax.ppermute(shard, axis, pairs)  11.2 us
    pallas_call x1, Pallas kernels, shards(): pl.pallas_call(functools.partial(sweep, geometry), out_shape=(jax.ShapeDt...  7.56 us
    unnamed x32, local copies, waits for them, and re-layouts  6.31 us
    pallas_call x1, Pallas kernels, shards(): pl.pallas_call(edge_rows, out_shape=(jax.ShapeDtypeStruct((rows_x, FIRST_...  1.21 us
  transfers between devices with their start and end apart: 4, of which 2 were waited for; matrix products, arithmetic and copies ran while one was open for 0% of the time, Pallas kernels for 0%

profile of v1, /device:TPU:227, one launch (start us, length us, event | category | flops | bytes accessed | tf_op | source)
XLA Modules:
  0.0 58.4 jit_solution(2032668989279438669)
XLA Ops:
  0.6 0.0 copy-start
  0.6 1.1 %copy-done = f32[3,16,24,128]{3,2,1,0:T(8,128)S(1)} copy-done((f32[3,16,24,128]{3,2,1,0:T(8,128)S(1)}, f32[3,16,24,128]{3,2,1,0:T(8,128)}, u32[]{:S(2)}) %copy-start) | copy-done | bytes 589848
  1.7 0.0 copy-start.2
  1.7 1.1 %copy-done.2 = f32[3,16,24,128]{3,2,1,0:T(8,128)S(1)} copy-done((f32[3,16,24,128]{3,2,1,0:T(8,128)S(1)}, f32[3,16,24,128]{3,2,1,0:T(8,128)}, u32[]{:S(2)}) %copy-start.2) | copy-done | bytes 589848
  2.8 0.0 copy-start.4
  2.8 1.1 %copy-done.4 = f32[3,16,24,128]{3,2,1,0:T(8,128)S(1)} copy-done((f32[3,16,24,128]{3,2,1,0:T(8,128)S(1)}, f32[3,16,24,128]{3,2,1,0:T(8,128)}, u32[]{:S(2)}) %copy-start.4) | copy-done | bytes 589848
  3.8 0.0 copy-start.6
  3.8 1.1 %copy-done.6 = f32[3,16,24,128]{3,2,1,0:T(8,128)S(1)} copy-done((f32[3,16,24,128]{3,2,1,0:T(8,128)S(1)}, f32[3,16,24,128]{3,2,1,0:T(8,128)}, u32[]{:S(2)}) %copy-start.6) | copy-done | bytes 589848
  4.9 0.0 copy-start.8
  4.9 0.9 %copy-done.8 = f32[16,24,128]{2,1,0:T(8,128)S(1)} copy-done((f32[16,24,128]{2,1,0:T(8,128)S(1)}, f32[16,24,128]{2,1,0:T(8,128)}, u32[]{:S(2)}) %copy-start.8) | copy-done | bytes 196632
  5.8 0.0 copy-start.10
  5.8 0.9 %copy-done.10 = f32[16,24,128]{2,1,0:T(8,128)S(1)} copy-done((f32[16,24,128]{2,1,0:T(8,128)S(1)}, f32[16,24,128]{2,1,0:T(8,128)}, u32[]{:S(2)}) %copy-start.10) | copy-done | bytes 196632
  6.7 0.0 copy-start.1
  6.7 0.0 copy-start.3
  6.8 0.0 copy-start.5
  6.8 0.0 copy-start.9
  6.8 0.0 copy-start.11
  6.8 1.2 %edge_rows.1 = (f32[16,24,128]{2,1,0:T(8,128)}, f32[16,32,128]{2,1,0:T(8,128)S(1)}) custom-call(f32[3,16,24,128]{3,2,1,0:T(8,128)S(1)} %copy-done, f32[3,16,24,128]{3,2,1,0:T(8,128)S(1)} %copy-done.2, f32[3,16,24,128]{3,2,1,0:T(8,128)S(1)} %copy-done.4, f32[3,16,24,128]{3,2,1,0:T(8,128)S(1)} %copy-done.6, f32[16,24,128]{2,1,0:T(8,128)S(1)} %copy-done.8, ...), custom_call_target="tpu_custom_call" | custom-call | tf_op jit(solution)/shard_map/edge_rows/pallas_call | solution.py:405
  8.0 3.8 %collective-permute-start.1 = (f32[16,32,128]{2,1,0:T(8,128)S(1)}, f32[16,32,128]{2,1,0:T(8,128)S(1)}, u32[]{:S(2)}, u32[]{:S(2)}) collective-permute-start(f32[16,32,128]{2,1,0:T(8,128)S(1)} %get-tuple-element.12), channel_id=1, source_target_pairs={{0,1},{1,2},{2,3},{3,4},{4,5},{5,6},{6,7},{7,8},{8,9},{9,10},{10,1... | collective-permute-start | bytes 786440 | tf_op jit(solution)/shard_map/ppermute | solution.py:34
  11.8 1.9 %collective-permute-start = (f32[16,24,128]{2,1,0:T(8,128)}, f32[16,24,128]{2,1,0:T(8,128)S(1)}, u32[]{:S(2)}, u32[]{:S(2)}) collective-permute-start(f32[16,24,128]{2,1,0:T(8,128)} %get-tuple-element.11), channel_id=1, source_target_pairs={{1,0},{2,1},{3,2},{4,3},{5,4},{6,5},{7,6},{8,7},{9,8},{10,9},{11,1... | collective-permute-start | bytes 589832 | tf_op jit(solution)/shard_map/ppermute | solution.py:34
  13.7 0.0 copy-start.12
  13.7 0.0 copy-start.13
  13.7 0.0 copy-start.14
  13.7 0.1 pad_add_fusion.pos
  13.8 5.2 %collective-permute-done.refs_6_ = f32[16,24,128]{2,1,0:T(8,128)S(1)} collective-permute-done((f32[16,24,128]{2,1,0:T(8,128)}, f32[16,24,128]{2,1,0:T(8,128)S(1)}, u32[]{:S(2)}, u32[]{:S(2)}) %collective-permute-start) | collective-permute-done | bytes 196640 | tf_op jit(solution)/shard_map/ppermute | solution.py:34
  19.0 0.0 collective-permute-done.1.refs_7_
  19.0 0.0 copy-done.1
  19.0 0.0 copy-done.3
  19.0 0.0 copy-done.5
  19.0 0.0 copy-done.7
  19.0 0.0 copy-done.9
  19.0 0.0 copy-done.11
  19.0 0.0 copy-done.12
  19.0 0.0 copy-done.13
  19.0 0.0 copy-done.14
  19.1 1.0 %edge_planes.1 = (f32[11,32,128]{2,1,0:T(8,128)S(1)}, f32[9,32,128]{2,1,0:T(8,128)S(1)}, f32[14,16,8,128]{3,2,1,0:T(8,128)S(1)}) custom-call(s32[2]{0:T(128)S(1)} %pad_add_fusion.pos, s32[6]{0:T(128)S(1)} %copy-done.13, s32[3]{0:T(128)S(1)} %copy-done.14, f32[16,128]{1,0:T(8,128)S(1)} %copy-done.12, f32[3,16,24,128]{3,2,1,0:T(8,128)S(1)} %copy-done.1, ...), custom_call_target="tpu_custom_call" | custom-call | tf_op jit(solution)/shard_map/edge_planes/pallas_call | solution.py:422
  20.1 4.7 %collective-permute-start.2 = (f32[11,32,128]{2,1,0:T(8,128)S(1)}, f32[11,32,128]{2,1,0:T(8,128)S(1)}, u32[]{:S(2)}, u32[]{:S(2)}) collective-permute-start(f32[11,32,128]{2,1,0:T(8,128)S(1)} %get-tuple-element.14), channel_id=1, source_target_pairs={{0,16},{16,32},{32,48},{48,64},{64,80},{80,96},{96,112},{112,128},... | collective-permute-start | bytes 540680 | tf_op jit(solution)/shard_map/ppermute | solution.py:34
  24.8 1.9 %collective-permute-start.3 = (f32[9,32,128]{2,1,0:T(8,128)S(1)}, f32[9,32,128]{2,1,0:T(8,128)S(1)}, u32[]{:S(2)}, u32[]{:S(2)}) collective-permute-start(f32[9,32,128]{2,1,0:T(8,128)S(1)} %get-tuple-element.15), channel_id=1, source_target_pairs={{16,0},{32,16},{48,32},{64,48},{80,64},{96,80},{112,96},{128,112},... | collective-permute-start | bytes 442376 | tf_op jit(solution)/shard_map/ppermute | solution.py:34
  26.8 6.1 %collective-permute-done.3.refs_8_ = f32[9,32,128]{2,1,0:T(8,128)S(1)} collective-permute-done((f32[9,32,128]{2,1,0:T(8,128)S(1)}, f32[9,32,128]{2,1,0:T(8,128)S(1)}, u32[]{:S(2)}, u32[]{:S(2)}) %collective-permute-start.3) | collective-permute-done | bytes 147488 | tf_op jit(solution)/shard_map/ppermute | solution.py:34
  32.8 0.0 collective-permute-done.2.refs_7_
  32.8 7.6 %sweep.1 = (f32[3,16,24,128]{3,2,1,0:T(8,128)}, f32[3,16,24,128]{3,2,1,0:T(8,128)}, f32[16,128]{1,0:T(8,128)S(1)}) custom-call(s32[2]{0:T(128)S(1)} %pad_add_fusion.pos, s32[6]{0:T(128)S(1)} %copy-done.13, s32[3]{0:T(128)S(1)} %copy-done.14, f32[16,128]{1,0:T(8,128)S(1)} %copy-done.12, f32[3,16,24,128]{3,2,1,0:T(8,128)S(1)} %copy-done.1, ...), custom_call_target="tpu_custom_call" | custom-call | tf_op jit(solution)/shard_map/sweep/pallas_call | solution.py:441
  40.4 0.1 copy.12
  40.5 0.1 reshape.10
  40.6 15.9 %all_to_all.9 = f32[16,1,128]{2,1,0:T(1,128)S(1)} all-to-all(f32[16,1,128]{2,1,0:T(1,128)S(1)} %reshape.10), channel_id=1, replica_groups=mesh['xy'=32,'gz'=16] {'gz'}, dimensions={0} | all-to-all | bytes 16384 | tf_op jit(solution)/shard_map/all_to_all | solution.py:459
  56.5 0.5 broadcast
  57.0 0.7 %reduce.1 = f32[16,128]{1,0:T(8,128)S(1)} reduce(f32[16,1,128]{2,1,0:T(1,128)S(1)} %all_to_all.9, f32[]{:T(128)} %broadcast), dimensions={1}, to_apply=%all_to_all.7.reduce_sub_computation | reduce | bytes 16388 | tf_op jit(solution)/shard_map/all_to_all | solution.py:459
  57.7 0.1 reshape.11
  57.8 0.6 %reduce_sum.9 = f32[8,16]{1,0:T(8,128)} reduce(f32[16,8,16]{2,1,0:T(8,128)S(1)} %reshape.11, f32[]{:T(128)} %constant.10.clone.1), dimensions={0}, to_apply=%region_0.0 | reduce | flops 1920 | bytes 8708 | tf_op jit(solution)/shard_map/reduce_sum | solution.py:460
  (1 shorter events, 0.0 us)
Async XLA Ops:
  0.6 1.1 %copy-start = (f32[3,16,24,128]{3,2,1,0:T(8,128)S(1)}, f32[3,16,24,128]{3,2,1,0:T(8,128)}, u32[]{:S(2)}) copy-start(f32[3,16,24,128]{3,2,1,0:T(8,128)} %refs_0_.5) | copy-start | bytes 1769476
  1.7 1.1 %copy-start.2 = (f32[3,16,24,128]{3,2,1,0:T(8,128)S(1)}, f32[3,16,24,128]{3,2,1,0:T(8,128)}, u32[]{:S(2)}) copy-start(f32[3,16,24,128]{3,2,1,0:T(8,128)} %refs_1_.5) | copy-start | bytes 1769476
  2.8 1.1 %copy-start.4 = (f32[3,16,24,128]{3,2,1,0:T(8,128)S(1)}, f32[3,16,24,128]{3,2,1,0:T(8,128)}, u32[]{:S(2)}) copy-start(f32[3,16,24,128]{3,2,1,0:T(8,128)} %refs_2_.5) | copy-start | bytes 1769476
  3.8 1.1 %copy-start.6 = (f32[3,16,24,128]{3,2,1,0:T(8,128)S(1)}, f32[3,16,24,128]{3,2,1,0:T(8,128)}, u32[]{:S(2)}) copy-start(f32[3,16,24,128]{3,2,1,0:T(8,128)} %refs_3_.5) | copy-start | bytes 1769476
  4.9 0.9 %copy-start.8 = (f32[16,24,128]{2,1,0:T(8,128)S(1)}, f32[16,24,128]{2,1,0:T(8,128)}, u32[]{:S(2)}) copy-start(f32[16,24,128]{2,1,0:T(8,128)} %refs_4_.5) | copy-start | bytes 589828
  5.8 0.9 %copy-start.10 = (f32[16,24,128]{2,1,0:T(8,128)S(1)}, f32[16,24,128]{2,1,0:T(8,128)}, u32[]{:S(2)}) copy-start(f32[16,24,128]{2,1,0:T(8,128)} %refs_5_.5) | copy-start | bytes 589828
  6.7 12.2 %copy-start.1 = (f32[3,16,24,128]{3,2,1,0:T(8,128)S(1)}, f32[3,16,24,128]{3,2,1,0:T(8,128)}, u32[]{:S(2)}) copy-start(f32[3,16,24,128]{3,2,1,0:T(8,128)} %refs_0_.5) | copy-start | bytes 1769476
  6.7 12.2 %copy-start.3 = (f32[3,16,24,128]{3,2,1,0:T(8,128)S(1)}, f32[3,16,24,128]{3,2,1,0:T(8,128)}, u32[]{:S(2)}) copy-start(f32[3,16,24,128]{3,2,1,0:T(8,128)} %refs_1_.5) | copy-start | bytes 1769476
  6.8 12.2 %copy-start.5 = (f32[3,16,24,128]{3,2,1,0:T(8,128)S(1)}, f32[3,16,24,128]{3,2,1,0:T(8,128)}, u32[]{:S(2)}) copy-start(f32[3,16,24,128]{3,2,1,0:T(8,128)} %refs_2_.5) | copy-start | bytes 1769476
  6.8 12.2 %copy-start.7 = (f32[3,16,24,128]{3,2,1,0:T(8,128)S(1)}, f32[3,16,24,128]{3,2,1,0:T(8,128)}, u32[]{:S(2)}) copy-start(f32[3,16,24,128]{3,2,1,0:T(8,128)} %refs_3_.5) | copy-start | bytes 1769476
  6.8 12.2 %copy-start.9 = (f32[16,24,128]{2,1,0:T(8,128)S(1)}, f32[16,24,128]{2,1,0:T(8,128)}, u32[]{:S(2)}) copy-start(f32[16,24,128]{2,1,0:T(8,128)} %refs_4_.5) | copy-start | bytes 589828
  6.8 12.2 %copy-start.11 = (f32[16,24,128]{2,1,0:T(8,128)S(1)}, f32[16,24,128]{2,1,0:T(8,128)}, u32[]{:S(2)}) copy-start(f32[16,24,128]{2,1,0:T(8,128)} %refs_5_.5) | copy-start | bytes 589828
  8.0 11.0 %collective-permute-start.1 = (f32[16,32,128]{2,1,0:T(8,128)S(1)}, f32[16,32,128]{2,1,0:T(8,128)S(1)}, u32[]{:S(2)}, u32[]{:S(2)}) collective-permute-start(f32[16,32,128]{2,1,0:T(8,128)S(1)} %get-tuple-element.12), channel_id=1, source_target_pairs={{0,1},{1,2},{2,3},{3,4},{4,5},{5,6},{6,7},{7,8},{8,9},{9,10},{10,1... | collective-permute-start | bytes 786440 | tf_op jit(solution)/shard_map/ppermute | solution.py:34
  11.8 7.2 %collective-permute-start = (f32[16,24,128]{2,1,0:T(8,128)}, f32[16,24,128]{2,1,0:T(8,128)S(1)}, u32[]{:S(2)}, u32[]{:S(2)}) collective-permute-start(f32[16,24,128]{2,1,0:T(8,128)} %get-tuple-element.11), channel_id=1, source_target_pairs={{1,0},{2,1},{3,2},{4,3},{5,4},{6,5},{7,6},{8,7},{9,8},{10,9},{11,1... | collective-permute-start | bytes 589832 | tf_op jit(solution)/shard_map/ppermute | solution.py:34
  13.7 5.3 %copy-start.12 = (f32[16,128]{1,0:T(8,128)S(1)}, f32[16,128]{1,0:T(8,128)}, u32[]{:S(2)}) copy-start(f32[16,128]{1,0:T(8,128)} %pattern.3) | copy-start | bytes 24580
  13.7 5.3 %copy-start.13 = (s32[6]{0:T(128)S(1)}, s32[6]{0:T(128)}, u32[]{:S(2)}) copy-start(s32[6]{0:T(128)} %box.3) | copy-start | bytes 76
  13.7 5.3 %copy-start.14 = (s32[3]{0:T(128)S(1)}, s32[3]{0:T(128)}, u32[]{:S(2)}) copy-start(s32[3]{0:T(128)} %pml.3) | copy-start | bytes 40
  20.1 12.7 %collective-permute-start.2 = (f32[11,32,128]{2,1,0:T(8,128)S(1)}, f32[11,32,128]{2,1,0:T(8,128)S(1)}, u32[]{:S(2)}, u32[]{:S(2)}) collective-permute-start(f32[11,32,128]{2,1,0:T(8,128)S(1)} %get-tuple-element.14), channel_id=1, source_target_pairs={{0,16},{16,32},{32,48},{48,64},{64,80},{80,96},{96,112},{112,128},... | collective-permute-start | bytes 540680 | tf_op jit(solution)/shard_map/ppermute | solution.py:34
  24.8 8.0 %collective-permute-start.3 = (f32[9,32,128]{2,1,0:T(8,128)S(1)}, f32[9,32,128]{2,1,0:T(8,128)S(1)}, u32[]{:S(2)}, u32[]{:S(2)}) collective-permute-start(f32[9,32,128]{2,1,0:T(8,128)S(1)} %get-tuple-element.15), channel_id=1, source_target_pairs={{16,0},{32,16},{48,32},{64,48},{80,64},{96,80},{112,96},{128,112},... | collective-permute-start | bytes 442376 | tf_op jit(solution)/shard_map/ppermute | solution.py:34

commit v2 on v1

--- a/solution.py
+++ b/solution.py
@@ -11,6 +11,7 @@
 SIGMA_PEAK = 1.0
 HALF = TIME_STEP / 2
 EXT = 8
+UNROLL = 4
 VMEM_LIMIT = 32 * 1024 * 1024
 
 FIRST_ROWS = (2, 2, 1, 1, 1, 1, 2, 2, 1, 1, 1, 1, 2, 2)
@@ -23,7 +24,7 @@
 BACK_PLANES = 11
 FRONT_PLANES = 9
 
-ANY = pl.BlockSpec(memory_space=pl.ANY)
+HBM = pl.BlockSpec(memory_space=pltpu.HBM)
 VMEM = pl.BlockSpec(memory_space=pltpu.VMEM)
 SMEM = pl.BlockSpec(memory_space=pltpu.SMEM)
 
@@ -263,7 +264,7 @@
 def sweep(geometry, pos, box, pml, pattern, *refs):
     fields, (tile, back, front) = refs[:6], refs[6:9]
     out_e, out_h, out_sum = refs[9:12]
-    mag, adj_mag, ele, adj_ele, ca, cb, da, db, loss_at, inv_at, sums = refs[12:]
+    mag, adj_mag, ele, adj_ele, ca, cb, da, db, loss_at, inv_at, sums, grad = refs[12:]
     rows_x, rows_z, cols = geometry[:3]
     grid = Grid(box, pml, (pos[0], pos[1]), *geometry)
     last = rows_x - 1
@@ -280,7 +281,8 @@
         da[x + 1], db[x + 1] = grid.magnetic(sigma)
         return carry
 
-    lax.fori_loop(0, rows_x, coefs, 0)
+    lax.fori_loop(0, rows_x, coefs, 0, unroll=UNROLL)
+    grad[...] = jnp.zeros(grad.shape, jnp.float32)
     cb[rows_x + 1] = front[4]
 
     at = jnp.full(grid.shape, grid.x_start)
@@ -330,7 +332,7 @@
         )
         return new_h[1:], scaled[1:]
 
-    lax.fori_loop(0, rows_x, first, ([h_y, h_z], [n_y, n_z]))
+    lax.fori_loop(0, rows_x, first, ([h_y, h_z], [n_y, n_z]), unroll=UNROLL)
 
     cb_after = front[4]
     ele[1, rows_x + 1] = front[2] + cb_after * mag[2, rows_x]
@@ -382,10 +384,20 @@
         total = picked[0:8]
         for start in range(8, rows_z, 8):
             total = total + picked[start : start + 8]
-        out_sum[pl.ds(x, 1), :] = jnp.sum(total, axis=0, keepdims=True)
+        grad[pl.ds(x, 1), :] = jnp.sum(total, axis=0, keepdims=True)
         return new_h[1:], scaled[1:]
 
-    lax.fori_loop(0, rows_x, second, (before_h, before_m))
+    lax.fori_loop(0, rows_x, second, (before_h, before_m), unroll=UNROLL)
+
+    out_sum[...] = jnp.transpose(grad[...])
+
+
+def add_shares(parts, out):
+    share, rows_x = out.shape
+    total = parts[pl.ds(0, share), :]
+    for j in range(1, parts.shape[0] // share):
+        total = total + parts[pl.ds(j * share, share), :]
+    out[...] = total[:, :rows_x]
 
 
 def shards(
@@ -408,11 +420,11 @@
             jax.ShapeDtypeStruct((rows_x, FIRST_SIZE, cols), f32),
             jax.ShapeDtypeStruct((rows_x, LAST_SIZE, cols), f32),
         ),
-        in_specs=[ANY] * 6,
+        in_specs=[HBM] * 6,
         out_specs=[VMEM] * 2,
         scratch_shapes=[tiles(ref) for ref in fields for _ in range(2)]
         + [pltpu.SemaphoreType.DMA((12,))],
-        compiler_params=params,
+        compiler_params=pltpu.CompilerParams(vmem_limit_bytes=60 * 1024 * 1024),
         name="edge_rows",
     )(*fields)
     above = shifted(first_rows, "gz", -1)
@@ -443,21 +455,26 @@
         out_shape=(
             jax.ShapeDtypeStruct(e_check.shape, f32),
             jax.ShapeDtypeStruct(e_check.shape, f32),
-            jax.ShapeDtypeStruct((rows_x, cols), f32),
+            jax.ShapeDtypeStruct((cols, cols), f32),
         ),
         in_specs=[SMEM] * 3 + [VMEM] * 10,
         out_specs=[VMEM] * 3,
         scratch_shapes=[planes(3, count)] * 4
         + [planes(count)] * 4
         + [planes(rows_x)] * 2
-        + [pltpu.VMEM((rows_x, rows_z, cols), f32)],
+        + [pltpu.VMEM((rows_x, rows_z, cols), f32), pltpu.VMEM((cols, cols), f32)],
         compiler_params=params,
         name="sweep",
     )(pos, design_box, pml_width, pattern, *fields, tile, back, front)
 
-    share = cols // size_z
-    parts = lax.all_to_all(local_sum.T, "gz", split_axis=0, concat_axis=0, tiled=True)
-    pattern_grad = jnp.sum(parts.reshape(size_z, share, rows_x), axis=0).T
+    parts = lax.all_to_all(local_sum, "gz", split_axis=0, concat_axis=0, tiled=True)
+    pattern_grad = pl.pallas_call(
+        add_shares,
+        out_shape=jax.ShapeDtypeStruct((cols // size_z, rows_x), f32),
+        in_specs=[VMEM],
+        out_specs=VMEM,
+        name="add_shares",
+    )(parts).T
     return (back_e, back_h, pattern_grad)
 
 

time: 58.8 us -> 50.8 us (0.86)
  local copies, waits for them, and re-layouts: 6.92 us -> 0.04 us
  other arithmetic: 1.36 us -> 0.08 us
    unnamed x32 -> x18, local copies, waits for them, and re-layouts: 6.31 us -> 0.04 us
    pallas_call x1, Pallas kernels: 7.56 us -> 4.39 us  [shards(): pl.pallas_call(functools.partial(sweep, geometry), out_shape=(jax.ShapeDt...]
    pallas_call x1, Pallas kernels: 1.21 us -> 2.8 us  [shards(): pl.pallas_call(edge_rows, out_shape=(jax.ShapeDtypeStruct((rows_x, FIRST_...]
    pallas_call x0 -> x1, Pallas kernels: none -> 1.45 us  [shards(): pl.pallas_call(add_shares, out_shape=jax.ShapeDtypeStruct((cols // size_z...]
    all_to_all x1 -> x0, other arithmetic: 0.67 us -> none  [shards(): lax.all_to_all(local_sum.T, 'gz', split_axis=0, concat_axis=0, tiled=True)]
    reduce_sum x1 -> x0, other arithmetic: 0.62 us -> none  [shards(): pattern_grad = jnp.sum(parts.reshape(size_z, share, rows_x), axis=0).T]
where the time goes in v2:
time: 50.8 us; the launch traced here: 50.5 us
  blocking collectives  16.4 us (32%)
  starting transfers between devices  12.3 us (24%)
  waiting for transfers between devices  11.2 us (22%)
  Pallas kernels  9.66 us (19%)
  between operations  0.81 us (2%)
    all_to_all x1, blocking collectives, shards(): lax.all_to_all(local_sum, 'gz', split_axis=0, concat_axis=0, tiled=True)  16.4 us
    ppermute x4, starting transfers between devices, shifted(): return lax.ppermute(shard, axis, pairs)  12.3 us
    ppermute x4, waiting for transfers between devices, shifted(): return lax.ppermute(shard, axis, pairs)  11.2 us
    pallas_call x1, Pallas kernels, shards(): pl.pallas_call(functools.partial(sweep, geometry), out_shape=(jax.ShapeDt...  4.39 us
    pallas_call x1, Pallas kernels, shards(): pl.pallas_call(edge_rows, out_shape=(jax.ShapeDtypeStruct((rows_x, FIRST_...  2.8 us
    pallas_call x1, Pallas kernels, shards(): pl.pallas_call(add_shares, out_shape=jax.ShapeDtypeStruct((cols // size_z...  1.45 us
    pallas_call x1, Pallas kernels, shards(): pl.pallas_call(functools.partial(edge_planes, geometry), out_shape=(jax.S...  1.03 us
  transfers between devices with their start and end apart: 4, of which 2 were waited for; matrix products, arithmetic and copies ran while one was open for 0% of the time, Pallas kernels for 0%

profile of v2, /device:TPU:227, one launch (start us, length us, event | category | flops | bytes accessed | tf_op | source)
XLA Modules:
  0.0 50.5 jit_solution(470663098699142607)
XLA Ops:
  0.6 0.0 copy-start.5
  0.6 0.0 copy-start.4
  0.7 0.0 copy-start.3
  0.7 0.0 copy-start.2
  0.7 0.0 copy-start.1
  0.7 0.0 copy-start
  0.7 2.8 %edge_rows.1 = (f32[16,24,128]{2,1,0:T(8,128)}, f32[16,32,128]{2,1,0:T(8,128)}) custom-call(f32[3,16,24,128]{3,2,1,0:T(8,128)} %refs_0_.5, f32[3,16,24,128]{3,2,1,0:T(8,128)} %refs_1_.5, f32[3,16,24,128]{3,2,1,0:T(8,128)} %refs_2_.5, f32[3,16,24,128]{3,2,1,0:T(8,128)} %refs_3_.5, f32[16,24,128]{2,1,0:T(8,128)} %refs_4_.5, f32[16,24,128]{2,1,0:T(8,128)} %refs_5_.5), custom_call_target="tpu_custom_call" | custom-call | tf_op jit(solution)/shard_map/edge_rows/pallas_call | solution.py:417
  3.5 3.8 %collective-permute-start.1 = (f32[16,32,128]{2,1,0:T(8,128)}, f32[16,32,128]{2,1,0:T(8,128)S(1)}, u32[]{:S(2)}, u32[]{:S(2)}) collective-permute-start(f32[16,32,128]{2,1,0:T(8,128)} %get-tuple-element.12), channel_id=1, source_target_pairs={{0,1},{1,2},{2,3},{3,4},{4,5},{5,6},{6,7},{7,8},{8,9},{9,10},{10,1... | collective-permute-start | bytes 786440 | tf_op jit(solution)/shard_map/ppermute | solution.py:35
  7.3 1.9 %collective-permute-start = (f32[16,24,128]{2,1,0:T(8,128)}, f32[16,24,128]{2,1,0:T(8,128)S(1)}, u32[]{:S(2)}, u32[]{:S(2)}) collective-permute-start(f32[16,24,128]{2,1,0:T(8,128)} %get-tuple-element.11), channel_id=1, source_target_pairs={{1,0},{2,1},{3,2},{4,3},{5,4},{6,5},{7,6},{8,7},{9,8},{10,9},{11,1... | collective-permute-start | bytes 589832 | tf_op jit(solution)/shard_map/ppermute | solution.py:35
  9.2 0.0 copy-start.6
  9.2 0.0 copy-start.7
  9.2 0.0 copy-start.8
  9.2 0.1 pad_add_fusion.pos
  9.3 5.2 %collective-permute-done.refs_6_ = f32[16,24,128]{2,1,0:T(8,128)S(1)} collective-permute-done((f32[16,24,128]{2,1,0:T(8,128)}, f32[16,24,128]{2,1,0:T(8,128)S(1)}, u32[]{:S(2)}, u32[]{:S(2)}) %collective-permute-start) | collective-permute-done | bytes 196640 | tf_op jit(solution)/shard_map/ppermute | solution.py:35
  14.5 0.0 collective-permute-done.1.refs_7_
  14.5 0.0 copy-done.5
  14.5 0.0 copy-done.4
  14.5 0.0 copy-done.3
  14.5 0.0 copy-done.2
  14.5 0.0 copy-done.1
  14.5 0.0 copy-done
  14.5 0.0 copy-done.6
  14.5 0.0 copy-done.7
  14.5 0.0 copy-done.8
  14.5 1.0 %edge_planes.1 = (f32[11,32,128]{2,1,0:T(8,128)S(1)}, f32[9,32,128]{2,1,0:T(8,128)S(1)}, f32[14,16,8,128]{3,2,1,0:T(8,128)S(1)}) custom-call(s32[2]{0:T(128)S(1)} %pad_add_fusion.pos, s32[6]{0:T(128)S(1)} %copy-done.7, s32[3]{0:T(128)S(1)} %copy-done.8, f32[16,128]{1,0:T(8,128)S(1)} %copy-done.6, f32[3,16,24,128]{3,2,1,0:T(8,128)S(1)} %copy-done, ...), custom_call_target="tpu_custom_call" | custom-call | tf_op jit(solution)/shard_map/edge_planes/pallas_call | solution.py:434
  15.6 4.7 %collective-permute-start.2 = (f32[11,32,128]{2,1,0:T(8,128)S(1)}, f32[11,32,128]{2,1,0:T(8,128)S(1)}, u32[]{:S(2)}, u32[]{:S(2)}) collective-permute-start(f32[11,32,128]{2,1,0:T(8,128)S(1)} %get-tuple-element.14), channel_id=1, source_target_pairs={{0,16},{16,32},{32,48},{48,64},{64,80},{80,96},{96,112},{112,128},... | collective-permute-start | bytes 540680 | tf_op jit(solution)/shard_map/ppermute | solution.py:35
  20.3 1.9 %collective-permute-start.3 = (f32[9,32,128]{2,1,0:T(8,128)S(1)}, f32[9,32,128]{2,1,0:T(8,128)S(1)}, u32[]{:S(2)}, u32[]{:S(2)}) collective-permute-start(f32[9,32,128]{2,1,0:T(8,128)S(1)} %get-tuple-element.15), channel_id=1, source_target_pairs={{16,0},{32,16},{48,32},{64,48},{80,64},{96,80},{112,96},{128,112},... | collective-permute-start | bytes 442376 | tf_op jit(solution)/shard_map/ppermute | solution.py:35
  22.2 6.1 %collective-permute-done.3.refs_8_ = f32[9,32,128]{2,1,0:T(8,128)S(1)} collective-permute-done((f32[9,32,128]{2,1,0:T(8,128)S(1)}, f32[9,32,128]{2,1,0:T(8,128)S(1)}, u32[]{:S(2)}, u32[]{:S(2)}) %collective-permute-start.3) | collective-permute-done | bytes 147488 | tf_op jit(solution)/shard_map/ppermute | solution.py:35
  28.3 0.0 collective-permute-done.2.refs_7_
  28.3 4.4 %sweep.1 = (f32[3,16,24,128]{3,2,1,0:T(8,128)}, f32[3,16,24,128]{3,2,1,0:T(8,128)}, f32[128,128]{1,0:T(8,128)S(1)}) custom-call(s32[2]{0:T(128)S(1)} %pad_add_fusion.pos, s32[6]{0:T(128)S(1)} %copy-done.7, s32[3]{0:T(128)S(1)} %copy-done.8, f32[16,128]{1,0:T(8,128)S(1)} %copy-done.6, f32[3,16,24,128]{3,2,1,0:T(8,128)S(1)} %copy-done, ...), custom_call_target="tpu_custom_call" | custom-call | tf_op jit(solution)/shard_map/sweep/pallas_call | solution.py:453
  32.7 16.4 %all_to_all.11 = f32[16,8,128]{2,1,0:T(8,128)} all-to-all(f32[16,8,128]{2,1,0:T(8,128)S(1)} %bitcast.5), channel_id=1, replica_groups=mesh['xy'=32,'gz'=16] {'gz'}, dimensions={0} | all-to-all | bytes 131072 | tf_op jit(solution)/shard_map/all_to_all | solution.py:470
  49.1 1.4 %add_shares.1 = f32[8,16]{1,0:T(8,128)} custom-call(f32[128,128]{1,0:T(8,128)} %bitcast.6), custom_call_target="tpu_custom_call" | custom-call | tf_op jit(solution)/shard_map/add_shares/pallas_call | solution.py:471
Async XLA Ops:
  0.6 13.8 %copy-start.5 = (f32[16,24,128]{2,1,0:T(8,128)S(1)}, f32[16,24,128]{2,1,0:T(8,128)}, u32[]{:S(2)}) copy-start(f32[16,24,128]{2,1,0:T(8,128)} %refs_5_.5) | copy-start | bytes 589828
  0.6 13.8 %copy-start.4 = (f32[16,24,128]{2,1,0:T(8,128)S(1)}, f32[16,24,128]{2,1,0:T(8,128)}, u32[]{:S(2)}) copy-start(f32[16,24,128]{2,1,0:T(8,128)} %refs_4_.5) | copy-start | bytes 589828
  0.7 13.8 %copy-start.3 = (f32[3,16,24,128]{3,2,1,0:T(8,128)S(1)}, f32[3,16,24,128]{3,2,1,0:T(8,128)}, u32[]{:S(2)}) copy-start(f32[3,16,24,128]{3,2,1,0:T(8,128)} %refs_3_.5) | copy-start | bytes 1769476
  0.7 13.8 %copy-start.2 = (f32[3,16,24,128]{3,2,1,0:T(8,128)S(1)}, f32[3,16,24,128]{3,2,1,0:T(8,128)}, u32[]{:S(2)}) copy-start(f32[3,16,24,128]{3,2,1,0:T(8,128)} %refs_2_.5) | copy-start | bytes 1769476
  0.7 13.8 %copy-start.1 = (f32[3,16,24,128]{3,2,1,0:T(8,128)S(1)}, f32[3,16,24,128]{3,2,1,0:T(8,128)}, u32[]{:S(2)}) copy-start(f32[3,16,24,128]{3,2,1,0:T(8,128)} %refs_1_.5) | copy-start | bytes 1769476
  0.7 13.8 %copy-start = (f32[3,16,24,128]{3,2,1,0:T(8,128)S(1)}, f32[3,16,24,128]{3,2,1,0:T(8,128)}, u32[]{:S(2)}) copy-start(f32[3,16,24,128]{3,2,1,0:T(8,128)} %refs_0_.5) | copy-start | bytes 1769476
  3.5 11.0 %collective-permute-start.1 = (f32[16,32,128]{2,1,0:T(8,128)}, f32[16,32,128]{2,1,0:T(8,128)S(1)}, u32[]{:S(2)}, u32[]{:S(2)}) collective-permute-start(f32[16,32,128]{2,1,0:T(8,128)} %get-tuple-element.12), channel_id=1, source_target_pairs={{0,1},{1,2},{2,3},{3,4},{4,5},{5,6},{6,7},{7,8},{8,9},{9,10},{10,1... | collective-permute-start | bytes 786440 | tf_op jit(solution)/shard_map/ppermute | solution.py:35
  7.3 7.2 %collective-permute-start = (f32[16,24,128]{2,1,0:T(8,128)}, f32[16,24,128]{2,1,0:T(8,128)S(1)}, u32[]{:S(2)}, u32[]{:S(2)}) collective-permute-start(f32[16,24,128]{2,1,0:T(8,128)} %get-tuple-element.11), channel_id=1, source_target_pairs={{1,0},{2,1},{3,2},{4,3},{5,4},{6,5},{7,6},{8,7},{9,8},{10,9},{11,1... | collective-permute-start | bytes 589832 | tf_op jit(solution)/shard_map/ppermute | solution.py:35
  9.2 5.3 %copy-start.6 = (f32[16,128]{1,0:T(8,128)S(1)}, f32[16,128]{1,0:T(8,128)}, u32[]{:S(2)}) copy-start(f32[16,128]{1,0:T(8,128)} %pattern.3) | copy-start | bytes 24580
  9.2 5.3 %copy-start.7 = (s32[6]{0:T(128)S(1)}, s32[6]{0:T(128)}, u32[]{:S(2)}) copy-start(s32[6]{0:T(128)} %box.3) | copy-start | bytes 76
  9.2 5.3 %copy-start.8 = (s32[3]{0:T(128)S(1)}, s32[3]{0:T(128)}, u32[]{:S(2)}) copy-start(s32[3]{0:T(128)} %pml.3) | copy-start | bytes 40
  15.6 12.7 %collective-permute-start.2 = (f32[11,32,128]{2,1,0:T(8,128)S(1)}, f32[11,32,128]{2,1,0:T(8,128)S(1)}, u32[]{:S(2)}, u32[]{:S(2)}) collective-permute-start(f32[11,32,128]{2,1,0:T(8,128)S(1)} %get-tuple-element.14), channel_id=1, source_target_pairs={{0,16},{16,32},{32,48},{48,64},{64,80},{80,96},{96,112},{112,128},... | collective-permute-start | bytes 540680 | tf_op jit(solution)/shard_map/ppermute | solution.py:35
  20.3 8.0 %collective-permute-start.3 = (f32[9,32,128]{2,1,0:T(8,128)S(1)}, f32[9,32,128]{2,1,0:T(8,128)S(1)}, u32[]{:S(2)}, u32[]{:S(2)}) collective-permute-start(f32[9,32,128]{2,1,0:T(8,128)S(1)} %get-tuple-element.15), channel_id=1, source_target_pairs={{16,0},{32,16},{48,32},{64,48},{80,64},{96,80},{112,96},{128,112},... | collective-permute-start | bytes 442376 | tf_op jit(solution)/shard_map/ppermute | solution.py:35

commit v3 on v2

v3 whole, which is shorter than its diff:
```python
import functools

import jax
import jax.numpy as jnp
from jax import lax
from jax.experimental import pallas as pl
from jax.experimental.pallas import tpu as pltpu
from jax.sharding import PartitionSpec as P

TIME_STEP = 0.5
SIGMA_PEAK = 1.0
HALF = TIME_STEP / 2
EXT = 8
UNROLL = 4
VMEM_LIMIT = 32 * 1024 * 1024
FIRST_VMEM_LIMIT = 60 * 1024 * 1024

FIRST_ROWS = (2, 2, 1, 1, 1, 1, 2, 2, 1, 1, 1, 1, 2, 2)
LAST_ROWS = (2, 2, 2, 2, 2, 1, 2, 2, 2, 2, 2, 1, 2, 2)
FIRST_AT = tuple(sum(FIRST_ROWS[:k]) for k in range(14))
LAST_AT = tuple(sum(LAST_ROWS[:k]) for k in range(14))
ROWS = max(sum(FIRST_ROWS), sum(LAST_ROWS))
SLOTS = 14
PLANES = 9
NEXT_ROWS = tuple((k, r) for k in (0, 1, 5, 6) for r in (0, -1)) + ((4, 0),)
PREV_ROWS = tuple(
    (k, r) for k, rs in ((0, (0, -1)), (1, (0, -2, -1)), (5, (0, -1)), (6, (0, -2, -1)))
    for r in rs
) + ((3, -1), (8, -1), (4, -1))
SINGLE_ROWS = 16
EDGE_PLANES = 38

HBM = pl.BlockSpec(memory_space=pltpu.HBM)
VMEM = pl.BlockSpec(memory_space=pltpu.VMEM)
SMEM = pl.BlockSpec(memory_space=pltpu.SMEM)


def swapped(shard, axis, first):
    size = lax.axis_size(axis)
    pairs = [(i, j) for k in range(first, size - 1, 2) for i, j in ((k, k + 1), (k + 1, k))]
    return lax.ppermute(shard, axis, pairs)


def swap_both(far, near, axis):
    far, near = swapped(far, axis, 1), swapped(near, axis, 0)
    return far, near


def is_even(axis):
    return lax.rem(lax.axis_index(axis), 2) == 0


def edge_rows(*refs):
    fields, pattern, outs, scratch = refs[:6], refs[6], refs[7:9], refs[9:]
    far_out, near_out = outs
    tiles, sems = scratch[:12], scratch[12]
    rows_z = fields[4].shape[1]
    copies = []
    for k, ref in enumerate(fields):
        for side, start in enumerate((0, rows_z - EXT)):
            src = ref.at[:, :, pl.ds(start, EXT), :] if k < 4 else ref.at[:, pl.ds(start, EXT), :]
            copy = pltpu.make_async_copy(src, tiles[2 * k + side], sems.at[2 * k + side])
            copy.start()
            copies.append(copy)
    rows_x = fields[4].shape[0]
    copy = pltpu.make_async_copy(pattern, near_out.at[pl.ds(rows_x * ROWS, rows_x)], sems.at[12])
    copy.start()
    copies.append(copy)
    for copy in copies:
        copy.wait()

    def write(first_out, last_out):
        for x in range(rows_x):
            for k in range(SLOTS):
                group = k // 3 if k < 12 else k - 8
                at = (k % 3, x) if k < 12 else (x,)
                low, high = tiles[2 * group], tiles[2 * group + 1]
                count, start = FIRST_ROWS[k], x * ROWS + FIRST_AT[k]
                first_out[start : start + count, :] = low[(*at, slice(0, count), slice(None))]
                count, start = LAST_ROWS[k], x * ROWS + LAST_AT[k]
                last_out[start : start + count, :] = high[(*at, slice(EXT - count, EXT), slice(None))]

    @pl.when(is_even("gz"))
    def _():
        write(far_out, near_out)

    @pl.when(~is_even("gz"))
    def _():
        write(near_out, far_out)


def lane_index(shape):
    return lax.broadcasted_iota(jnp.int32, shape, 1)


def y_ahead(v):
    cols = v.shape[1]
    moved = pltpu.roll(v, cols - 1, 1)
    return jnp.where(lane_index(v.shape) == cols - 1, 0.0, moved) - v


def y_behind(v):
    moved = pltpu.roll(v, 1, 1)
    return v - jnp.where(lane_index(v.shape) == 0, 0.0, moved)


def z_ahead(v):
    return pltpu.roll(v, v.shape[0] - 1, 0) - v


def z_behind(v):
    return v - pltpu.roll(v, 1, 0)


def plus_x(v):
    return y_ahead(v[2]) - z_ahead(v[1])


def plus_y(v, next_z):
    return z_ahead(v[0]) - (next_z - v[2])


def plus_z(v, next_y):
    return (next_y - v[1]) - y_ahead(v[0])


def plus(v, next_y, next_z):
    return plus_x(v), plus_y(v, next_z), plus_z(v, next_y)


def minus(v, prev_y, prev_z):
    return (
        y_behind(v[2]) - z_behind(v[1]),
        z_behind(v[0]) - (v[2] - prev_z),
        (v[1] - prev_y) - y_behind(v[0]),
    )


def plus_yz(v_y, v_z):
    return y_ahead(v_z) - z_ahead(v_y), v_z, -v_y


def minus_yz(v_y, v_z):
    return y_behind(v_z) - z_behind(v_y), -v_z, v_y


def dot(left, right):
    return sum(a * b for a, b in zip(left, right))


def depth_cube(place, total, layer):
    depth = jnp.maximum(jnp.maximum(layer - place, place - (total - 1 - layer)), 0.0) / layer
    return depth * depth * depth


class Grid:
    def __init__(self, box, pml, rows_x, rows_z, cols, total_x, total_z):
        rows = rows_z + EXT
        self.shape = (rows, cols)
        self.box = box
        self.width_x = pml[0].astype(jnp.float32)
        self.total_x = total_x
        self.x_start = lax.axis_index("xy") * rows_x
        self.rows_z = rows_z
        row = lax.broadcasted_iota(jnp.int32, self.shape, 0)
        z = lax.axis_index("gz") * rows_z + jnp.where(row < rows_z + EXT // 2, row, row - rows)
        y = lane_index(self.shape)
        self.inside = (z >= 0) & (z < total_z)
        self.sigma_zy = depth_cube(
            z.astype(jnp.float32), total_z, pml[2].astype(jnp.float32)
        ) + depth_cube(y.astype(jnp.float32), cols, pml[1].astype(jnp.float32))
        picked = (z >= box[4]) & (z < box[5]) & (y >= box[2]) & (y < box[3])
        self.mask_zy = jnp.where(picked, 1.0, 0.0)

    def sigma(self, x):
        place = jnp.full((1, self.shape[1]), (self.x_start + x).astype(jnp.float32))
        return SIGMA_PEAK * (self.sigma_zy + depth_cube(place, self.total_x, self.width_x))

    def mask_x(self, x):
        at = self.x_start + x
        return jnp.where((at >= self.box[0]) & (at < self.box[1]), 1.0, 0.0)

    def magnetic(self, sigma, x_inside=None):
        inside = self.inside if x_inside is None else self.inside & x_inside
        inverse = 1.0 / (1.0 + HALF * sigma)
        return (
            jnp.where(inside, 2.0 * inverse - 1.0, 0.0),
            jnp.where(inside, TIME_STEP * inverse, 0.0),
        )

    def electric(self, x, background, conductivity, pattern_row, sigma):
        permittivity = background + self.mask_zy * (pattern_row * self.mask_x(x))
        loss = HALF * (conductivity + sigma)
        inverse = jnp.where(self.inside, 1.0 / (permittivity + loss), 0.0)
        return (permittivity - loss) * inverse, TIME_STEP * inverse, loss, inverse


def full_plane(ref, tile_ref, k, x):
    own = ref[k % 3, x] if k < 12 else ref[x]
    return jnp.concatenate([own, tile_ref[k, x]], axis=0)


def fill_tile(tile_ref, far, near, even, k, x):
    for count, at, start in (
        (FIRST_ROWS[k], FIRST_AT[k], 0),
        (LAST_ROWS[k], LAST_AT[k], EXT - LAST_ROWS[k]),
    ):
        rows = pl.ds(x * ROWS + at, count)
        own, other = (near, far) if start == 0 else (far, near)
        tile_ref[k, x, pl.ds(start, count), :] = jnp.where(even, own[rows, :], other[rows, :])


def field_ref(fields, k):
    return fields[k // 3] if k < 12 else fields[k - 8]


def triple(fields, tile_ref, group, x):
    return tuple(full_plane(fields[group], tile_ref, 3 * group + c, x) for c in range(3))


def edge_planes(geometry, box, pml, *refs):
    fields, (rows_far, rows_near), (far, near) = refs[:6], refs[6:8], refs[8:10]
    tile, buffers, planes = refs[10], refs[11:13], refs[13]
    rows_x, rows_z = geometry[:2]
    grid = Grid(box, pml, *geometry)
    even = is_even("gz")
    for x in (0, 1, rows_x - 2, rows_x - 1):
        for k in range(SLOTS):
            tile[k, x] = jnp.zeros(tile.shape[2:], jnp.float32)
            fill_tile(tile, rows_far, rows_near, even, k, x)

    def coefs(x):
        sigma = grid.sigma(x)
        coef_a, coef_b, _, _ = grid.electric(
            x,
            full_plane(fields[4], tile, 12, x),
            full_plane(fields[5], tile, 13, x),
            rows_near[pl.ds(rows_x * ROWS + x, 1), :],
            sigma,
        )
        return (coef_a, coef_b) + grid.magnetic(sigma)

    def load(x):
        return [triple(fields, tile, g, x) for g in range(4)]

    def pack(buffer, values, rows):
        for k, value in enumerate(values):
            buffer[pl.ds(k * rows_z, rows_z), :] = value[:rows_z]
            planes[k] = value
        start = PLANES * rows_z
        buffer[pl.ds(start, SINGLE_ROWS), :] = jnp.zeros((SINGLE_ROWS, value.shape[1]), jnp.float32)
        for i, (k, r) in enumerate(rows):
            at = rows_z + r if r >= 0 else rows_z + EXT + r
            buffer[pl.ds(start + i, 1), :] = planes[k, pl.ds(at, 1), :]

    one, two = rows_x - 2, rows_x - 1
    e1, h1, p1, q1 = load(one)
    e2, h2, p2, q2 = load(two)
    _, cb1, da1, db1 = coefs(one)
    ca2, cb2, da2, db2 = coefs(two)
    before = (
        da1 * h1[1] - db1 * plus_y(e1, e2[2]),
        da1 * h1[2] - db1 * plus_z(e1, e2[1]),
    )
    mag = [da2 * h - db2 * c for h, c in zip(h2, plus(e2, 0.0, 0.0))]
    ele = [ca2 * e + cb2 * c for e, c in zip(e2, minus(mag, *before))]
    mag2 = (
        da2 * mag[1] - db2 * plus_y(ele, 0.0),
        da2 * mag[2] - db2 * plus_z(ele, 0.0),
    )
    u1 = [cb1 * v for v in p1]
    u2 = [cb2 * v for v in p2]
    before = (
        db1 * (q1[1] + plus_y(u1, u2[2])),
        db1 * (q1[2] + plus_z(u1, u2[1])),
    )
    adj = [q + c for q, c in zip(q2, plus(u2, 0.0, 0.0))]
    curl = minus([db2 * v for v in adj], *before)
    u2 = [cb2 * (ca2 * p - c) for p, c in zip(p2, curl)]
    adj2 = (da2 * adj[1] + plus_y(u2, 0.0), da2 * adj[2] + plus_z(u2, 0.0))
    pack(buffers[0], (mag[1], mag[2]) + mag2 + (cb2, adj[1], adj[2]) + adj2, NEXT_ROWS)

    e1, h1, p1, q1 = load(0)
    e2, _, p2, _ = load(1)
    ca1, cb1, da1, db1 = coefs(0)
    _, cb2, _, _ = coefs(1)
    mag = [da1 * h - db1 * c for h, c in zip(h1, plus(e1, e2[1], e2[2]))]
    curl = minus(mag, 0.0, 0.0)
    ele = (ca1 * e1[1] + cb1 * curl[1], ca1 * e1[2] + cb1 * curl[2])
    u1 = [cb1 * v for v in p1]
    adj = [db1 * (q + c) for q, c in zip(q1, plus(u1, cb2 * p2[1], cb2 * p2[2]))]
    curl = minus(adj, 0.0, 0.0)
    adj_ele = (ca1 * p1[1] - curl[1], ca1 * p1[2] - curl[2])
    pack(buffers[1], e1[1:] + ele + (cb1, u1[1], u1[2]) + adj_ele, PREV_ROWS)

    even = is_even("xy")
    to_next, to_prev = buffers[0][...], buffers[1][...]
    far[...] = jnp.where(even, to_prev, to_next)
    near[...] = jnp.where(even, to_next, to_prev)


def sweep(geometry, box, pml, *refs):
    fields, (rows_far, rows_near) = refs[:6], refs[6:8]
    full_e, full_h, grad, edge, edge_e, edge_h = refs[8:14]
    tile, mag, adj_mag, ele, adj_ele, ca, cb, da, db = refs[14:23]
    by_e, by_r, sums, out_e, out_h, sems = refs[23:]
    rows_x, rows_z, cols = geometry[:3]
    grid = Grid(box, pml, *geometry)
    last = rows_x - 1
    own = pl.ds(0, rows_z)
    even = is_even("gz")
    tile[...] = jnp.zeros(tile.shape, jnp.float32)
    for x in range(rows_x):
        for k in range(SLOTS):
            fill_tile(tile, rows_far, rows_near, even, k, x)

    def coefs(x, carry):
        sigma = grid.sigma(x)
        ca[x], cb[x], loss, inverse = grid.electric(
            x,
            full_plane(fields[4], tile, 12, x),
            full_plane(fields[5], tile, 13, x),
            rows_near[pl.ds(rows_x * ROWS + x, 1), :],
            sigma,
        )
        da[x], db[x] = grid.magnetic(sigma)
        weight = (inverse * inverse * (grid.mask_zy * grid.mask_x(x)))[:rows_z]
        by_e[x] = 2.0 * loss[:rows_z] * weight
        by_r[x] = -TIME_STEP * weight
        return carry

    lax.fori_loop(0, rows_x, coefs, 0, unroll=UNROLL)
    zero = jnp.zeros(grid.shape, jnp.float32)
    cb[rows_x] = zero
    for k in (1, 2):
        ele[k, rows_x] = zero
        adj_ele[k, rows_x] = zero

    def first(x, carry):
        prev_h, prev_m = carry
        at_last = jnp.full(grid.shape, x) == last
        ahead = jnp.minimum(x + 1, last)
        e, h, p, q = [triple(fields, tile, g, x) for g in range(4)]
        a, b, c, d = ca[x], cb[x], da[x], db[x]
        e_y = jnp.where(at_last, 0.0, full_plane(fields[0], tile, 1, ahead))
        e_z = jnp.where(at_last, 0.0, full_plane(fields[0], tile, 2, ahead))
        new_h = [c * v - d * w for v, w in zip(h, plus(e, e_y, e_z))]
        curl = minus(new_h, *prev_h)
        b_ahead = cb[x + 1]
        u_y = b_ahead * full_plane(fields[2], tile, 7, ahead)
        u_z = b_ahead * full_plane(fields[2], tile, 8, ahead)
        new_m = [v + w for v, w in zip(q, plus([b * v for v in p], u_y, u_z))]
        scaled = [d * v for v in new_m]
        adj_curl = minus(scaled, *prev_m)
        dot_e, dot_r = 0.0, 0.0
        for k in range(3):
            mag[k, x] = new_h[k]
            adj_mag[k, x] = new_m[k]
            ele[k, x] = a * e[k] + b * curl[k]
            new_p = a * p[k] - adj_curl[k]
            adj_ele[k, x] = new_p
            dot_e = dot_e + new_p[:rows_z] * e[k][:rows_z]
            dot_r = dot_r + new_p[:rows_z] * curl[k][:rows_z]
        sums[x] = by_e[x] * dot_e + by_r[x] * dot_r

        @pl.when((x == 0) | (x == last))
        def _():
            at = jnp.where(x == 0, 0, 3)
            for k in range(3):
                edge[at + k] = curl[k]

        return new_h[1:], scaled[1:]

    lax.fori_loop(0, rows_x, first, ([zero, zero], [zero, zero]), unroll=UNROLL)

    def out_copies(x):
        return [
            pltpu.make_async_copy(ref.at[:, pl.ds(x, 1)], full.at[:, pl.ds(x, 1)], sems.at[i, x])
            for i, (ref, full) in enumerate(((out_e, full_e), (out_h, full_h)))
        ]

    def second(x, carry):
        prev_h, prev_m = carry
        e = [ele[k, x] for k in range(3)]
        p1 = [adj_ele[k, x] for k in range(3)]
        a, b, c, d = ca[x], cb[x], da[x], db[x]
        new_h = [
            c * mag[k, x] - d * w for k, w in enumerate(plus(e, ele[1, x + 1], ele[2, x + 1]))
        ]
        curl = minus(new_h, *prev_h)
        b_ahead = cb[x + 1]
        u = [b * v for v in p1]
        ahead = plus(u, b_ahead * adj_ele[1, x + 1], b_ahead * adj_ele[2, x + 1])
        new_m = [c * adj_mag[k, x] + w for k, w in enumerate(ahead)]
        scaled = [d * v for v in new_m]
        adj_curl = minus(scaled, *prev_m)
        dot_e, dot_r = 0.0, 0.0
        for k in range(3):
            out_h[k, x] = c[:rows_z] * new_m[k][:rows_z]
            out_e[k, x] = a[:rows_z] * p1[k][:rows_z] - adj_curl[k][:rows_z]
            p = fields[2][k, x]
            dot_e = dot_e + p * e[k][:rows_z]
            dot_r = dot_r + p * curl[k][:rows_z]
        terms = sums[x] + by_e[x] * dot_e + by_r[x] * dot_r
        total = terms[0:8]
        for start in range(8, rows_z, 8):
            total = total + terms[start : start + 8]
        grad[pl.ds(x, 1), :] = jnp.sum(total, axis=0, keepdims=True)

        @pl.when((x > 1) & (x < last - 1))
        def _():
            for copy in out_copies(x):
                copy.start()

        return new_h[1:], scaled[1:]

    lax.fori_loop(0, rows_x, second, ([zero, zero], [zero, zero]), unroll=UNROLL)

    kept = [ele[1, 0], ele[2, 0]] + [adj_ele[k, 0] for k in range(3)]
    kept += [mag[1, last], mag[2, last], db[last] * adj_mag[1, last], db[last] * adj_mag[2, last]]
    kept += [adj_ele[k, last] for k in range(3)]
    kept += [ref[x] for x in (0, last) for ref in (ca, cb, da, db)] + [da[last - 1], db[last - 1]]
    kept += [full_plane(fields[0], tile, k, 0) for k in (1, 2)]
    kept += [cb[0] * full_plane(fields[2], tile, k, 0) for k in (7, 8)]
    for k, value in enumerate(kept):
        edge[6 + k] = value
    start = 6 + len(kept)
    for k, value in enumerate((by_e[0], by_r[0], by_r[1], by_r[last - 1], by_e[last], by_r[last])):
        edge[start + k, own, :] = value
    for i, x in enumerate((0, 1, last - 1, last)):
        for k in range(3):
            edge_e[k, i] = out_e[k, x]
            edge_h[k, i] = out_h[k, x]
    for x in range(2, last - 1):
        for copy in out_copies(x):
            copy.wait()


def response(geometry, box, pml, *refs):
    e_ref, p_ref, edge, local_e, local_h, local_grad, far, near = refs[:8]
    edge_e, edge_h, shares, buffers, tile, grad = refs[8:]
    rows_x, rows_z, cols = geometry[:3]
    last = rows_x - 1
    grid = Grid(box, pml, *geometry)
    even = is_even("xy")
    buffers[0] = jnp.where(even, far[...], near[...])
    buffers[1] = jnp.where(even, near[...], far[...])
    grad[...] = jnp.zeros(grad.shape, jnp.float32)
    grad[pl.ds(0, rows_x), :] = local_grad[...]
    for side, rows in enumerate((NEXT_ROWS, PREV_ROWS)):
        for k in range(PLANES):
            tile[side, k] = jnp.zeros(tile.shape[2:], jnp.float32)
        for i, (k, r) in enumerate(rows):
            row = buffers[side, pl.ds(PLANES * rows_z + i, 1), :]
            tile[side, k, pl.ds(r if r >= 0 else EXT + r, 1), :] = row

    def unpack(side):
        return [
            jnp.concatenate([buffers[side, pl.ds(k * rows_z, rows_z), :], tile[side, k]], axis=0)
            for k in range(PLANES)
        ]

    def own(v):
        return v[:rows_z]

    def weight(k):
        return edge[32 + k, pl.ds(0, rows_z), :]

    def add_rows(x, terms):
        total = terms[0:8]
        for start in range(8, rows_z, 8):
            total = total + terms[start : start + 8]
        grad[pl.ds(x, 1), :] += jnp.sum(total, axis=0, keepdims=True)

    def write(ref, local, i, change, scale=1.0):
        for k in range(3):
            ref[k, i] = local[k, i] if change[k] is None else local[k, i] + own(change[k])

    h_y, h_z, h2_y, h2_z, cb_b, m_y, m_z, m2_y, m2_z = unpack(0)
    at = jnp.full(grid.shape, grid.x_start)
    da_b, db_b = grid.magnetic(grid.sigma(-1), at > 0)
    ca_f, cb_f, da_f, db_f = (edge[18 + k] for k in range(4))
    e_y, e_z, u_y, u_z = (edge[28 + k] for k in range(4))
    dh_y, dh_z = db_b * e_z, -(db_b * e_y)
    h_y, h_z = h_y + dh_y, h_z + dh_z
    d_ele = (cb_f * h_z, -(cb_f * h_y))
    ele_y, ele_z = edge[6] + d_ele[0], edge[7] + d_ele[1]
    back = [cb_b * v for v in minus_yz(dh_y, dh_z)]
    h2_y = h2_y + da_b * dh_y - db_b * plus_y(back, ele_z)
    h2_z = h2_z + da_b * dh_z - db_b * plus_z(back, ele_y)
    dm_y, dm_z = -u_z, u_y
    n_y, n_z = db_b * (m_y + dm_y), db_b * (m_z + dm_z)
    d_p = (-n_z, n_y)
    p_y, p_z = edge[9] + d_p[0], edge[10] + d_p[1]
    back = [-(cb_b * v) for v in minus_yz(db_b * dm_y, db_b * dm_z)]
    m2_y = m2_y + da_b * dm_y + plus_y(back, cb_f * p_z)
    m2_z = m2_z + da_b * dm_z + plus_z(back, cb_f * p_y)
    d_h2 = [-(db_f * v) for v in plus_yz(*d_ele)]
    d_m2 = plus_yz(cb_f * d_p[0], cb_f * d_p[1])
    d_r2 = minus(d_h2, h2_y, h2_z)
    d_n2 = [db_f * v for v in d_m2]
    curl = minus(d_n2, db_b * m2_y, db_b * m2_z)
    write(edge_e, local_e, 0, (-curl[0], ca_f * d_p[0] - curl[1], ca_f * d_p[1] - curl[2]))
    write(edge_e, local_e, 1, (None, -d_n2[2], d_n2[1]))
    write(edge_h, local_h, 0, [da_f * v for v in d_m2])
    write(edge_h, local_h, 1, (None, None, None))
    p2 = [p_ref[k, 0] for k in range(3)]
    along_e = sum(
        own(d_p[k - 1]) * e_ref[k, 0] + p2[k] * own(d_ele[k - 1]) for k in (1, 2)
    )
    along_r = dot(p2, [own(v) for v in d_r2])
    along_r = along_r + own(d_p[0] * edge[1] + d_p[1] * edge[2] + p_y * h_z - p_z * h_y)
    add_rows(0, weight(0) * along_e + weight(1) * along_r)
    add_rows(1, weight(2) * (p_ref[1, 1] * own(d_h2[2]) - p_ref[2, 1] * own(d_h2[1])))

    e_y, e_z, e1_y, e1_z, cb_n, u_y, u_z, p_y, p_z = unpack(1)
    ca_l, cb_l, da_l, db_l = (edge[22 + k] for k in range(4))
    da_k, db_k = edge[26], edge[27]
    dh_y, dh_z = db_l * e_z, -(db_l * e_y)
    dm_y, dm_z = -u_z, u_y
    dn_y, dn_z = db_l * dm_y, db_l * dm_z
    d_r1 = minus_yz(dh_y, dh_z)
    d_ele = [cb_l * v for v in d_r1]
    d_p = [-v for v in minus_yz(dn_y, dn_z)]
    e1_y = e1_y + cb_n * (edge[12] + dh_z)
    e1_z = e1_z - cb_n * (edge[11] + dh_y)
    p_y = p_y - (edge[14] + dn_z)
    p_z = p_z + (edge[13] + dn_y)
    d_h2 = [-(db_l * v) for v in plus(d_ele, e1_y, e1_z)]
    d_h2 = [d_h2[0], d_h2[1] + da_l * dh_y, d_h2[2] + da_l * dh_z]
    d_u = [cb_l * v for v in d_p]
    d_m2 = plus(d_u, cb_n * p_y, cb_n * p_z)
    d_m2 = [d_m2[0], d_m2[1] + da_l * dm_y, d_m2[2] + da_l * dm_z]
    k_h2 = (db_k * d_ele[2], -(db_k * d_ele[1]))
    k_m2 = (-d_u[2], d_u[1])
    k_n2 = (db_k * k_m2[0], db_k * k_m2[1])
    k_r2 = minus_yz(*k_h2)
    d_r2 = minus(d_h2, *k_h2)
    write(edge_e, local_e, 2, [-v for v in minus_yz(*k_n2)])
    curl = minus([db_l * v for v in d_m2], *k_n2)
    write(edge_e, local_e, 3, [ca_l * v - c for v, c in zip(d_p, curl)])
    write(edge_h, local_h, 2, (None, da_k * k_m2[0], da_k * k_m2[1]))
    write(edge_h, local_h, 3, [da_l * v for v in d_m2])
    p2 = [p_ref[k, last] for k in range(3)]
    along_e = dot([own(v) for v in d_p], [e_ref[k, last] for k in range(3)])
    along_e = along_e + dot(p2, [own(v) for v in d_ele])
    along_r = dot(p2, [own(v) for v in d_r2])
    for k in range(3):
        new_p = own(edge[15 + k] + d_p[k])
        along_r = along_r + own(d_p[k] * edge[3 + k]) + new_p * own(d_r1[k])
    add_rows(last, weight(4) * along_e + weight(5) * along_r)
    p2 = [p_ref[k, last - 1] for k in range(3)]
    add_rows(last - 1, weight(3) * dot(p2, [own(v) for v in k_r2]))

    shares[...] = jnp.transpose(grad[...])


def finish(parts, edge_e, edge_h, in_e, in_h, out_e, out_h, out, sems):
    last = out_e.shape[1] - 2
    copies = []
    for i, (edge, full) in enumerate(((edge_e, out_e), (edge_h, out_h))):
        for side, start in enumerate((0, last)):
            copy = pltpu.make_async_copy(
                edge.at[:, pl.ds(2 * side, 2)], full.at[:, pl.ds(start, 2)], sems.at[2 * i + side]
            )
            copy.start()
            copies.append(copy)
    share, rows_x = out.shape
    total = parts[pl.ds(0, share), :]
    for j in range(1, parts.shape[0] // share):
        total = total + parts[pl.ds(j * share, share), :]
    out[...] = total[:, :rows_x]
    for copy in copies:
        copy.wait()


def shards(
    e_check, h_check, adj_e_end, adj_h_end, background, conductivity, pattern, design_box, pml_width
):
    rows_x, rows_z, cols = background.shape
    size_x, size_z = lax.axis_size("xy"), lax.axis_size("gz")
    geometry = (rows_x, rows_z, cols, rows_x * size_x, rows_z * size_z)
    fields = (e_check, h_check, adj_e_end, adj_h_end, background, conductivity)
    f32 = jnp.float32
    params = pltpu.CompilerParams(vmem_limit_bytes=VMEM_LIMIT)

    def array(*shape):
        return jax.ShapeDtypeStruct(shape, f32)

    def tiles(ref):
        return pltpu.VMEM(ref.shape[:-2] + (EXT, cols), f32)

    rows_far, rows_near = pl.pallas_call(
        edge_rows,
        out_shape=(array(rows_x * ROWS, cols), array(rows_x * ROWS + rows_x, cols)),
        in_specs=[HBM] * 7,
        out_specs=[VMEM] * 2,
        scratch_shapes=[tiles(ref) for ref in fields for _ in range(2)]
        + [pltpu.SemaphoreType.DMA((13,))],
        compiler_params=pltpu.CompilerParams(vmem_limit_bytes=FIRST_VMEM_LIMIT),
        name="edge_rows",
    )(*fields, pattern)
    rows_far, rows_near = swap_both(rows_far, rows_near, "gz")

    def planes(*lead):
        return pltpu.VMEM(lead + (rows_z + EXT, cols), f32)

    size = PLANES * rows_z + SINGLE_ROWS
    message = pltpu.VMEM((size, cols), f32)
    tile = pltpu.VMEM((SLOTS, rows_x, EXT, cols), f32)
    far, near = pl.pallas_call(
        functools.partial(edge_planes, geometry),
        out_shape=(array(size, cols),) * 2,
        in_specs=[SMEM] * 2 + [VMEM] * 8,
        out_specs=[VMEM] * 2,
        scratch_shapes=[tile, message, message, planes(PLANES)],
        compiler_params=params,
        name="edge_planes",
    )(design_box, pml_width, *fields, rows_far, rows_near)
    far, near = swap_both(far, near, "xy")

    count = rows_x + 1
    local_e, local_h, local_grad, edge, edge_e, edge_h = pl.pallas_call(
        functools.partial(sweep, geometry),
        out_shape=(
            array(*e_check.shape),
            array(*e_check.shape),
            array(rows_x, cols),
            array(EDGE_PLANES, rows_z + EXT, cols),
            array(3, 4, rows_z, cols),
            array(3, 4, rows_z, cols),
        ),
        in_specs=[SMEM] * 2 + [VMEM] * 8,
        out_specs=[HBM] * 2 + [VMEM] * 4,
        scratch_shapes=[tile]
        + [planes(3, count)] * 4
        + [planes(count)] * 4
        + [pltpu.VMEM((rows_x, rows_z, cols), f32)] * 3
        + [pltpu.VMEM((3, rows_x, rows_z, cols), f32)] * 2
        + [pltpu.SemaphoreType.DMA((2, rows_x))],
        compiler_params=params,
        cost_estimate=pl.CostEstimate(flops=50000000, bytes_accessed=8000000, transcendentals=0),
        name="sweep",
    )(design_box, pml_width, *fields, rows_far, rows_near)

    edge_e, edge_h, shares = pl.pallas_call(
        functools.partial(response, geometry),
        out_shape=(array(*edge_e.shape), array(*edge_h.shape), array(cols, cols)),
        in_specs=[SMEM] * 2 + [VMEM] * 8,
        out_specs=[VMEM] * 3,
        scratch_shapes=[
            pltpu.VMEM((2, size, cols), f32),
            pltpu.VMEM((2, PLANES, EXT, cols), f32),
            pltpu.VMEM((cols, cols), f32),
        ],
        compiler_params=params,
        name="response",
    )(design_box, pml_width, e_check, adj_e_end, edge, edge_e, edge_h, local_grad, far, near)

    parts = lax.all_to_all(shares, "gz", split_axis=0, concat_axis=0, tiled=True)
    back_e, back_h, pattern_grad = pl.pallas_call(
        finish,
        out_shape=(array(*e_check.shape), array(*e_check.shape), array(cols // size_z, rows_x)),
        in_specs=[VMEM] * 3 + [HBM] * 2,
        out_specs=[HBM] * 2 + [VMEM],
        scratch_shapes=[pltpu.SemaphoreType.DMA((4,))],
        input_output_aliases={3: 0, 4: 1},
        compiler_params=pltpu.CompilerParams(vmem_limit_bytes=8 * 1024 * 1024),
        name="finish",
    )(parts, edge_e, edge_h, local_e, local_h)
    return (back_e, back_h, pattern_grad.T)


def solution(mesh):
    field = P(None, "xy", "gz", None)
    cell = P("xy", "gz", None)
    return jax.shard_map(
        shards,
        mesh=mesh,
        in_specs=(field, field, field, field, cell, cell, P("xy", None), P(), P()),
        out_specs=(field, field, P("xy", "gz")),
        check_vma=False,
    )
```

time: 50.8 us -> 46.1 us (0.907)
  the two profiles are of different devices: /device:TPU:227 before, /device:TPU:225 now
where the time goes in v3:
time: 46.1 us; the launch traced here: 45.8 us
  blocking collectives  15.6 us (34%)
  starting transfers between devices  13.5 us (29%)
  Pallas kernels  11.6 us (25%)
  waiting for transfers between devices  4.27 us (9%)
  between operations  0.82 us (2%)
    all_to_all x1, blocking collectives, shards(): lax.all_to_all(shares, 'gz', split_axis=0, concat_axis=0, tiled=True)  15.6 us
    ppermute x4, starting transfers between devices, swapped(): return lax.ppermute(shard, axis, pairs)  13.5 us
    pallas_call x1, Pallas kernels, shards(): pl.pallas_call(functools.partial(sweep, geometry), out_shape=(array(*e_ch...  5.75 us
    ppermute x4, waiting for transfers between devices, swapped(): return lax.ppermute(shard, axis, pairs)  4.27 us
    pallas_call x1, Pallas kernels, shards(): pl.pallas_call(edge_rows, out_shape=(array(rows_x * ROWS, cols), array(ro...  2.68 us
    pallas_call x1, Pallas kernels, shards(): pl.pallas_call(finish, out_shape=(array(*e_check.shape), array(*e_check.s...  1.33 us
    pallas_call x1, Pallas kernels, shards(): pl.pallas_call(functools.partial(response, geometry), out_shape=(array(*e...  0.96 us
  transfers between devices with their start and end apart: 4, of which 1 were waited for; matrix products, arithmetic and copies ran while one was open for 0% of the time, Pallas kernels for 13%

profile of v3, /device:TPU:225, one launch (start us, length us, event | category | flops | bytes accessed | tf_op | source)
XLA Modules:
  0.0 45.8 jit_solution(10285804254815914114)
XLA Ops:
  0.6 0.0 copy-start.1
  0.6 0.0 copy-start
  0.7 0.0 copy-start.5
  0.7 0.0 copy-start.4
  0.7 0.0 copy-start.3
  0.7 0.0 copy-start.2
  0.7 2.7 %edge_rows.1 = (f32[416,128]{1,0:T(8,128)}, f32[432,128]{1,0:T(8,128)}) custom-call(f32[3,16,24,128]{3,2,1,0:T(8,128)} %refs_0_.7, f32[3,16,24,128]{3,2,1,0:T(8,128)} %refs_1_.6, f32[3,16,24,128]{3,2,1,0:T(8,128)} %refs_1_.7, f32[3,16,24,128]{3,2,1,0:T(8,128)} %refs_3_.5, f32[16,24,128]{2,1,0:T(8,128)} %refs_4_.5, f32[16,24,128]{2,1,0:T(8,128)} %refs_5_.5, ...), custom_call_target="tpu_custom_call" | custom-call | tf_op jit(solution)/shard_map/edge_rows/pallas_call | solution.py:593
  3.4 0.0 copy-start.6
  3.4 0.0 copy-start.7
  3.4 2.6 %collective-permute-start.1 = (f32[432,128]{1,0:T(8,128)}, f32[432,128]{1,0:T(8,128)S(1)}, u32[]{:S(2)}, u32[]{:S(2)}) collective-permute-start(f32[432,128]{1,0:T(8,128)} %get-tuple-element.20), channel_id=1, source_target_pairs={{0,1},{1,0},{2,3},{3,2},{4,5},{5,4},{6,7},{7,6},{8,9},{9,8},{10,11... | collective-permute-start | bytes 663560 | tf_op jit(solution)/shard_map/ppermute | solution.py:41
  6.0 3.1 %collective-permute-start = (f32[416,128]{1,0:T(8,128)}, f32[416,128]{1,0:T(8,128)S(1)}, u32[]{:S(2)}, u32[]{:S(2)}) collective-permute-start(f32[416,128]{1,0:T(8,128)} %get-tuple-element.19), channel_id=1, source_target_pairs={{1,2},{2,1},{3,4},{4,3},{5,6},{6,5},{7,8},{8,7},{9,10},{10,9},{11,... | collective-permute-start | bytes 638984 | tf_op jit(solution)/shard_map/ppermute | solution.py:41
  9.1 4.3 %collective-permute-done.refs_6_ = f32[416,128]{1,0:T(8,128)S(1)} collective-permute-done((f32[416,128]{1,0:T(8,128)}, f32[416,128]{1,0:T(8,128)S(1)}, u32[]{:S(2)}, u32[]{:S(2)}) %collective-permute-start) | collective-permute-done | bytes 213024 | tf_op jit(solution)/shard_map/ppermute | solution.py:41
  13.4 0.0 collective-permute-done.1.refs_7_
  13.4 0.0 copy-done.1
  13.4 0.0 copy-done
  13.4 0.0 copy-done.5
  13.4 0.0 copy-done.4
  13.4 0.0 copy-done.3
  13.4 0.0 copy-done.2
  13.4 0.0 copy-done.6
  13.4 0.0 copy-done.7
  13.4 0.8 %edge_planes.1 = (f32[232,128]{1,0:T(8,128)S(1)}, f32[232,128]{1,0:T(8,128)S(1)}) custom-call(s32[6]{0:T(128)S(1)} %copy-done.6, s32[3]{0:T(128)S(1)} %copy-done.7, f32[3,16,24,128]{3,2,1,0:T(8,128)S(1)} %copy-done, f32[3,16,24,128]{3,2,1,0:T(8,128)S(1)} %copy-done.2, f32[3,16,24,128]{3,2,1,0:T(8,128)S(1)} %copy-done.1, f32[3,16,24,128]{3,2,1,0:T(8,128)S(1)} %copy-done.3, ...), custom_call_target="tpu_custom_call" | custom-call | tf_op jit(solution)/shard_map/edge_planes/pallas_call | solution.py:611
  14.3 2.7 %collective-permute-start.2 = (f32[232,128]{1,0:T(8,128)S(1)}, f32[232,128]{1,0:T(8,128)S(1)}, u32[]{:S(2)}, u32[]{:S(2)}) collective-permute-start(f32[232,128]{1,0:T(8,128)S(1)} %get-tuple-element.25), channel_id=1, source_target_pairs={{16,32},{32,16},{48,64},{64,48},{80,96},{96,80},{112,128},{128,112... | collective-permute-start | bytes 356360 | tf_op jit(solution)/shard_map/ppermute | solution.py:41
  17.0 5.2 %collective-permute-start.3 = (f32[232,128]{1,0:T(8,128)S(1)}, f32[232,128]{1,0:T(8,128)S(1)}, u32[]{:S(2)}, u32[]{:S(2)}) collective-permute-start(f32[232,128]{1,0:T(8,128)S(1)} %get-tuple-element.26), channel_id=1, source_target_pairs={{0,16},{16,0},{32,48},{48,32},{64,80},{80,64},{96,112},{112,96},{1... | collective-permute-start | bytes 356360 | tf_op jit(solution)/shard_map/ppermute | solution.py:41
  22.1 5.8 %sweep.1 = (f32[3,16,24,128]{3,2,1,0:T(8,128)}, f32[3,16,24,128]{3,2,1,0:T(8,128)}, f32[16,128]{1,0:T(8,128)S(1)}, f32[38,32,128]{2,1,0:T(8,128)S(1)}, f32[3,4,2...) custom-call(s32[6]{0:T(128)S(1)} %copy-done.6, s32[3]{0:T(128)S(1)} %copy-done.7, f32[3,16,24,128]{3,2,1,0:T(8,128)S(1)} %copy-done, ...), custom_call_target="tpu_custom_call" | custom-call | flops 50000000 | bytes 8000000 | tf_op jit(solution)/shard_map/sweep/pallas_call | solution.py:623
  27.9 0.0 collective-permute-done.2.refs_6_
  27.9 0.0 collective-permute-done.3.refs_7_
  27.9 1.0 %response.1 = (f32[3,4,24,128]{3,2,1,0:T(8,128)S(1)}, f32[3,4,24,128]{3,2,1,0:T(8,128)S(1)}, f32[128,128]{1,0:T(8,128)S(1)}) custom-call(s32[6]{0:T(128)S(1)} %copy-done.6, s32[3]{0:T(128)S(1)} %copy-done.7, f32[3,16,24,128]{3,2,1,0:T(8,128)S(1)} %copy-done, f32[3,16,24,128]{3,2,1,0:T(8,128)S(1)} %copy-done.1, f32[38,32,128]{2,1,0:T(8,128)S(1)} %get-tuple-element.21.refs_2_, ...), custom_call_target="tpu_custom_call" | custom-call | tf_op jit(solution)/shard_map/response/pallas_call | solution.py:646
  28.9 15.6 %all_to_all.11 = f32[16,8,128]{2,1,0:T(8,128)S(1)} all-to-all(f32[16,8,128]{2,1,0:T(8,128)S(1)} %bitcast.4), channel_id=1, replica_groups=mesh['xy'=32,'gz'=16] {'gz'}, dimensions={0} | all-to-all | bytes 131072 | tf_op jit(solution)/shard_map/all_to_all | solution.py:660
  44.5 1.3 %finish.1 = (f32[3,16,24,128]{3,2,1,0:T(8,128)}, f32[3,16,24,128]{3,2,1,0:T(8,128)}, f32[8,16]{1,0:T(8,128)}) custom-call(f32[128,128]{1,0:T(8,128)S(1)} %bitcast.3, f32[3,4,24,128]{3,2,1,0:T(8,128)S(1)} %get-tuple-element.28.edge_e, f32[3,4,24,128]{3,2,1,0:T(8,128)S(1)} %get-tuple-element.29.edge_h, ...), custom_call_target="tpu_custom_call", output_to_operand_aliasing={{0}: (3, {}), {1}: (4, {})} | custom-call | tf_op jit(solution)/shard_map/finish/pallas_call | solution.py:661
Async XLA Ops:
  0.6 12.7 %copy-start.1 = (f32[3,16,24,128]{3,2,1,0:T(8,128)S(1)}, f32[3,16,24,128]{3,2,1,0:T(8,128)}, u32[]{:S(2)}) copy-start(f32[3,16,24,128]{3,2,1,0:T(8,128)} %refs_1_.7) | copy-start | bytes 1769476
  0.6 12.7 %copy-start = (f32[3,16,24,128]{3,2,1,0:T(8,128)S(1)}, f32[3,16,24,128]{3,2,1,0:T(8,128)}, u32[]{:S(2)}) copy-start(f32[3,16,24,128]{3,2,1,0:T(8,128)} %refs_0_.7) | copy-start | bytes 1769476
  0.7 12.7 %copy-start.5 = (f32[16,24,128]{2,1,0:T(8,128)S(1)}, f32[16,24,128]{2,1,0:T(8,128)}, u32[]{:S(2)}) copy-start(f32[16,24,128]{2,1,0:T(8,128)} %refs_5_.5) | copy-start | bytes 589828
  0.7 12.7 %copy-start.4 = (f32[16,24,128]{2,1,0:T(8,128)S(1)}, f32[16,24,128]{2,1,0:T(8,128)}, u32[]{:S(2)}) copy-start(f32[16,24,128]{2,1,0:T(8,128)} %refs_4_.5) | copy-start | bytes 589828
  0.7 12.7 %copy-start.3 = (f32[3,16,24,128]{3,2,1,0:T(8,128)S(1)}, f32[3,16,24,128]{3,2,1,0:T(8,128)}, u32[]{:S(2)}) copy-start(f32[3,16,24,128]{3,2,1,0:T(8,128)} %refs_3_.5) | copy-start | bytes 1769476
  0.7 12.7 %copy-start.2 = (f32[3,16,24,128]{3,2,1,0:T(8,128)S(1)}, f32[3,16,24,128]{3,2,1,0:T(8,128)}, u32[]{:S(2)}) copy-start(f32[3,16,24,128]{3,2,1,0:T(8,128)} %refs_1_.6) | copy-start | bytes 1769476
  3.4 10.0 %copy-start.6 = (s32[6]{0:T(128)S(1)}, s32[6]{0:T(128)}, u32[]{:S(2)}) copy-start(s32[6]{0:T(128)} %box.5) | copy-start | bytes 76
  3.4 10.0 %copy-start.7 = (s32[3]{0:T(128)S(1)}, s32[3]{0:T(128)}, u32[]{:S(2)}) copy-start(s32[3]{0:T(128)} %pml.5) | copy-start | bytes 40
  3.4 10.0 %collective-permute-start.1 = (f32[432,128]{1,0:T(8,128)}, f32[432,128]{1,0:T(8,128)S(1)}, u32[]{:S(2)}, u32[]{:S(2)}) collective-permute-start(f32[432,128]{1,0:T(8,128)} %get-tuple-element.20), channel_id=1, source_target_pairs={{0,1},{1,0},{2,3},{3,2},{4,5},{5,4},{6,7},{7,6},{8,9},{9,8},{10,11... | collective-permute-start | bytes 663560 | tf_op jit(solution)/shard_map/ppermute | solution.py:41
  6.0 7.4 %collective-permute-start = (f32[416,128]{1,0:T(8,128)}, f32[416,128]{1,0:T(8,128)S(1)}, u32[]{:S(2)}, u32[]{:S(2)}) collective-permute-start(f32[416,128]{1,0:T(8,128)} %get-tuple-element.19), channel_id=1, source_target_pairs={{1,2},{2,1},{3,4},{4,3},{5,6},{6,5},{7,8},{8,7},{9,10},{10,9},{11,... | collective-permute-start | bytes 638984 | tf_op jit(solution)/shard_map/ppermute | solution.py:41
  14.3 13.6 %collective-permute-start.2 = (f32[232,128]{1,0:T(8,128)S(1)}, f32[232,128]{1,0:T(8,128)S(1)}, u32[]{:S(2)}, u32[]{:S(2)}) collective-permute-start(f32[232,128]{1,0:T(8,128)S(1)} %get-tuple-element.25), channel_id=1, source_target_pairs={{16,32},{32,16},{48,64},{64,48},{80,96},{96,80},{112,128},{128,112... | collective-permute-start | bytes 356360 | tf_op jit(solution)/shard_map/ppermute | solution.py:41
  17.0 11.0 %collective-permute-start.3 = (f32[232,128]{1,0:T(8,128)S(1)}, f32[232,128]{1,0:T(8,128)S(1)}, u32[]{:S(2)}, u32[]{:S(2)}) collective-permute-start(f32[232,128]{1,0:T(8,128)S(1)} %get-tuple-element.26), channel_id=1, source_target_pairs={{0,16},{16,0},{32,48},{48,32},{64,80},{80,64},{96,112},{112,96},{1... | collective-permute-start | bytes 356360 | tf_op jit(solution)/shard_map/ppermute | solution.py:41

commit v4 on v3

--- a/solution.py
+++ b/solution.py
@@ -13,13 +13,13 @@
 EXT = 8
 UNROLL = 4
 VMEM_LIMIT = 32 * 1024 * 1024
-FIRST_VMEM_LIMIT = 60 * 1024 * 1024
 
 FIRST_ROWS = (2, 2, 1, 1, 1, 1, 2, 2, 1, 1, 1, 1, 2, 2)
 LAST_ROWS = (2, 2, 2, 2, 2, 1, 2, 2, 2, 2, 2, 1, 2, 2)
 FIRST_AT = tuple(sum(FIRST_ROWS[:k]) for k in range(14))
 LAST_AT = tuple(sum(LAST_ROWS[:k]) for k in range(14))
 ROWS = max(sum(FIRST_ROWS), sum(LAST_ROWS))
+PERIOD = 4
 SLOTS = 14
 PLANES = 9
 NEXT_ROWS = tuple((k, r) for k in (0, 1, 5, 6) for r in (0, -1)) + ((4, 0),)
@@ -50,43 +50,44 @@
     return lax.rem(lax.axis_index(axis), 2) == 0
 
 
-def edge_rows(*refs):
-    fields, pattern, outs, scratch = refs[:6], refs[6], refs[7:9], refs[9:]
-    far_out, near_out = outs
-    tiles, sems = scratch[:12], scratch[12]
-    rows_z = fields[4].shape[1]
+def rows_of(ref, group):
+    return ref.at[pl.ds(pl.multiple_of(group * (PERIOD * ROWS), 8), PERIOD * ROWS)]
+
+
+def load_fields(*refs):
+    sources, copies_of, (far, near) = refs[:9], refs[9:18], refs[18:20]
+    first, last, sems = refs[20:]
+    rows_x, rows_z = sources[4].shape[:2]
     copies = []
-    for k, ref in enumerate(fields):
-        for side, start in enumerate((0, rows_z - EXT)):
-            src = ref.at[:, :, pl.ds(start, EXT), :] if k < 4 else ref.at[:, pl.ds(start, EXT), :]
-            copy = pltpu.make_async_copy(src, tiles[2 * k + side], sems.at[2 * k + side])
-            copy.start()
-            copies.append(copy)
-    rows_x = fields[4].shape[0]
-    copy = pltpu.make_async_copy(pattern, near_out.at[pl.ds(rows_x * ROWS, rows_x)], sems.at[12])
-    copy.start()
-    copies.append(copy)
-    for copy in copies:
+    for i, (source, target) in enumerate(zip(sources, copies_of)):
+        copy = pltpu.make_async_copy(source, target, sems.at[i])
+        copy.start()
+        copies.append(copy)
+
+    for i in range(6):
+        copies[i].wait()
+        field = copies_of[i]
+
+        def pack(group, carry):
+            first_rows, last_rows = rows_of(first, group), rows_of(last, group)
+            for n in range(PERIOD):
+                x = group * PERIOD + n
+                for k in range(3 * i, 3 * i + 3) if i < 4 else (8 + i,):
+                    at = (k % 3, x) if i < 4 else (x,)
+                    count, start = FIRST_ROWS[k], n * ROWS + FIRST_AT[k]
+                    rows = field[(*at, slice(0, count), slice(None))]
+                    first_rows[start : start + count, :] = rows
+                    count, start = LAST_ROWS[k], n * ROWS + LAST_AT[k]
+                    rows = field[(*at, slice(rows_z - count, rows_z), slice(None))]
+                    last_rows[start : start + count, :] = rows
+            return carry
+
+        lax.fori_loop(0, rows_x // PERIOD, pack, 0)
+    for copy in copies[6:]:
         copy.wait()
-
-    def write(first_out, last_out):
-        for x in range(rows_x):
-            for k in range(SLOTS):
-                group = k // 3 if k < 12 else k - 8
-                at = (k % 3, x) if k < 12 else (x,)
-                low, high = tiles[2 * group], tiles[2 * group + 1]
-                count, start = FIRST_ROWS[k], x * ROWS + FIRST_AT[k]
-                first_out[start : start + count, :] = low[(*at, slice(0, count), slice(None))]
-                count, start = LAST_ROWS[k], x * ROWS + LAST_AT[k]
-                last_out[start : start + count, :] = high[(*at, slice(EXT - count, EXT), slice(None))]
-
-    @pl.when(is_even("gz"))
-    def _():
-        write(far_out, near_out)
-
-    @pl.when(~is_even("gz"))
-    def _():
-        write(near_out, far_out)
+    even = is_even("gz")
+    far[...] = jnp.where(even, first[...], last[...])
+    near[...] = jnp.where(even, last[...], first[...])
 
 
 def lane_index(shape):
@@ -200,18 +201,19 @@
     return jnp.concatenate([own, tile_ref[k, x]], axis=0)
 
 
-def fill_tile(tile_ref, far, near, even, k, x):
-    for count, at, start in (
-        (FIRST_ROWS[k], FIRST_AT[k], 0),
-        (LAST_ROWS[k], LAST_AT[k], EXT - LAST_ROWS[k]),
-    ):
-        rows = pl.ds(x * ROWS + at, count)
-        own, other = (near, far) if start == 0 else (far, near)
-        tile_ref[k, x, pl.ds(start, count), :] = jnp.where(even, own[rows, :], other[rows, :])
-
-
-def field_ref(fields, k):
-    return fields[k // 3] if k < 12 else fields[k - 8]
+def fill_tiles(tile_ref, far, near, even, group, planes):
+    far, near = rows_of(far, group), rows_of(near, group)
+    for n in planes:
+        x = group * PERIOD + n
+        for k in range(SLOTS):
+            tile_ref[k, x] = jnp.zeros(tile_ref.shape[2:], jnp.float32)
+            for count, at, start in (
+                (FIRST_ROWS[k], FIRST_AT[k], 0),
+                (LAST_ROWS[k], LAST_AT[k], EXT - LAST_ROWS[k]),
+            ):
+                rows = pl.ds(n * ROWS + at, count)
+                own, other = (near, far) if start == 0 else (far, near)
+                tile_ref[k, x, pl.ds(start, count), :] = jnp.where(even, own[rows, :], other[rows, :])
 
 
 def triple(fields, tile_ref, group, x):
@@ -219,15 +221,13 @@
 
 
 def edge_planes(geometry, box, pml, *refs):
-    fields, (rows_far, rows_near), (far, near) = refs[:6], refs[6:8], refs[8:10]
-    tile, buffers, planes = refs[10], refs[11:13], refs[13]
+    fields, pattern, (rows_far, rows_near) = refs[:6], refs[6], refs[7:9]
+    far, near, tile, buffers, planes = refs[9], refs[10], refs[11], refs[12:14], refs[14]
     rows_x, rows_z = geometry[:2]
     grid = Grid(box, pml, *geometry)
     even = is_even("gz")
-    for x in (0, 1, rows_x - 2, rows_x - 1):
-        for k in range(SLOTS):
-            tile[k, x] = jnp.zeros(tile.shape[2:], jnp.float32)
-            fill_tile(tile, rows_far, rows_near, even, k, x)
+    fill_tiles(tile, rows_far, rows_near, even, 0, (0, 1))
+    fill_tiles(tile, rows_far, rows_near, even, rows_x // PERIOD - 1, (PERIOD - 2, PERIOD - 1))
 
     def coefs(x):
         sigma = grid.sigma(x)
@@ -235,7 +235,7 @@
             x,
             full_plane(fields[4], tile, 12, x),
             full_plane(fields[5], tile, 13, x),
-            rows_near[pl.ds(rows_x * ROWS + x, 1), :],
+            pattern[pl.ds(x, 1), :],
             sigma,
         )
         return (coef_a, coef_b) + grid.magnetic(sigma)
@@ -300,19 +300,21 @@
 
 
 def sweep(geometry, box, pml, *refs):
-    fields, (rows_far, rows_near) = refs[:6], refs[6:8]
-    full_e, full_h, grad, edge, edge_e, edge_h = refs[8:14]
-    tile, mag, adj_mag, ele, adj_ele, ca, cb, da, db = refs[14:23]
-    by_e, by_r, sums, out_e, out_h, sems = refs[23:]
+    fields, pattern, (rows_far, rows_near) = refs[:6], refs[6], refs[7:9]
+    full_e, full_h, grad, edge, edge_e, edge_h = refs[9:15]
+    tile, mag, adj_mag, ele, adj_ele, ca, cb, da, db = refs[15:24]
+    by_e, by_r, sums, out_e, out_h, sems = refs[24:]
     rows_x, rows_z, cols = geometry[:3]
     grid = Grid(box, pml, *geometry)
     last = rows_x - 1
     own = pl.ds(0, rows_z)
     even = is_even("gz")
-    tile[...] = jnp.zeros(tile.shape, jnp.float32)
-    for x in range(rows_x):
-        for k in range(SLOTS):
-            fill_tile(tile, rows_far, rows_near, even, k, x)
+
+    def fill(group, carry):
+        fill_tiles(tile, rows_far, rows_near, even, group, range(PERIOD))
+        return carry
+
+    lax.fori_loop(0, rows_x // PERIOD, fill, 0)
 
     def coefs(x, carry):
         sigma = grid.sigma(x)
@@ -320,7 +322,7 @@
             x,
             full_plane(fields[4], tile, 12, x),
             full_plane(fields[5], tile, 13, x),
-            rows_near[pl.ds(rows_x * ROWS + x, 1), :],
+            pattern[pl.ds(x, 1), :],
             sigma,
         )
         da[x], db[x] = grid.magnetic(sigma)
@@ -362,20 +364,14 @@
             dot_e = dot_e + new_p[:rows_z] * e[k][:rows_z]
             dot_r = dot_r + new_p[:rows_z] * curl[k][:rows_z]
         sums[x] = by_e[x] * dot_e + by_r[x] * dot_r
-
-        @pl.when((x == 0) | (x == last))
-        def _():
-            at = jnp.where(x == 0, 0, 3)
-            for k in range(3):
-                edge[at + k] = curl[k]
-
         return new_h[1:], scaled[1:]
 
     lax.fori_loop(0, rows_x, first, ([zero, zero], [zero, zero]), unroll=UNROLL)
 
-    def out_copies(x):
+    def out_copies(group):
+        part = pl.ds(group * UNROLL, UNROLL)
         return [
-            pltpu.make_async_copy(ref.at[:, pl.ds(x, 1)], full.at[:, pl.ds(x, 1)], sems.at[i, x])
+            pltpu.make_async_copy(ref.at[:, part], full.at[:, part], sems.at[i, group])
             for i, (ref, full) in enumerate(((out_e, full_e), (out_h, full_h)))
         ]
 
@@ -406,16 +402,22 @@
         for start in range(8, rows_z, 8):
             total = total + terms[start : start + 8]
         grad[pl.ds(x, 1), :] = jnp.sum(total, axis=0, keepdims=True)
-
-        @pl.when((x > 1) & (x < last - 1))
-        def _():
-            for copy in out_copies(x):
-                copy.start()
-
         return new_h[1:], scaled[1:]
 
-    lax.fori_loop(0, rows_x, second, ([zero, zero], [zero, zero]), unroll=UNROLL)
-
+    def second_group(group, carry):
+        for i in range(UNROLL):
+            carry = second(group * UNROLL + i, carry)
+        for copy in out_copies(group):
+            copy.start()
+        return carry
+
+    groups = rows_x // UNROLL
+    lax.fori_loop(0, groups, second_group, ([zero, zero], [zero, zero]))
+
+    first_curl = minus([mag[k, 0] for k in range(3)], 0.0, 0.0)
+    last_curl = minus([mag[k, last] for k in range(3)], mag[1, last - 1], mag[2, last - 1])
+    for k in range(3):
+        edge[k], edge[3 + k] = first_curl[k], last_curl[k]
     kept = [ele[1, 0], ele[2, 0]] + [adj_ele[k, 0] for k in range(3)]
     kept += [mag[1, last], mag[2, last], db[last] * adj_mag[1, last], db[last] * adj_mag[2, last]]
     kept += [adj_ele[k, last] for k in range(3)]
@@ -431,8 +433,8 @@
         for k in range(3):
             edge_e[k, i] = out_e[k, x]
             edge_h[k, i] = out_h[k, x]
-    for x in range(2, last - 1):
-        for copy in out_copies(x):
+    for group in range(groups):
+        for copy in out_copies(group):
             copy.wait()
 
 
@@ -587,19 +589,17 @@
     def array(*shape):
         return jax.ShapeDtypeStruct(shape, f32)
 
-    def tiles(ref):
-        return pltpu.VMEM(ref.shape[:-2] + (EXT, cols), f32)
-
-    rows_far, rows_near = pl.pallas_call(
-        edge_rows,
-        out_shape=(array(rows_x * ROWS, cols), array(rows_x * ROWS + rows_x, cols)),
-        in_specs=[HBM] * 7,
-        out_specs=[VMEM] * 2,
-        scratch_shapes=[tiles(ref) for ref in fields for _ in range(2)]
-        + [pltpu.SemaphoreType.DMA((13,))],
-        compiler_params=pltpu.CompilerParams(vmem_limit_bytes=FIRST_VMEM_LIMIT),
-        name="edge_rows",
-    )(*fields, pattern)
+    message = pltpu.VMEM((rows_x * ROWS, cols), f32)
+    inputs = fields + (pattern, design_box, pml_width)
+    *inputs, design_box, pml_width, rows_far, rows_near = pl.pallas_call(
+        load_fields,
+        out_shape=tuple(pltpu.VMEM(ref.shape, ref.dtype) for ref in inputs) + (message,) * 2,
+        in_specs=[HBM] * 9,
+        out_specs=[VMEM] * 11,
+        scratch_shapes=[message] * 2 + [pltpu.SemaphoreType.DMA((9,))],
+        compiler_params=pltpu.CompilerParams(vmem_limit_bytes=8 * 1024 * 1024),
+        name="load_fields",
+    )(*(pltpu.with_memory_space_constraint(ref, pltpu.HBM) for ref in inputs))
     rows_far, rows_near = swap_both(rows_far, rows_near, "gz")
 
     def planes(*lead):
@@ -611,12 +611,12 @@
     far, near = pl.pallas_call(
         functools.partial(edge_planes, geometry),
         out_shape=(array(size, cols),) * 2,
-        in_specs=[SMEM] * 2 + [VMEM] * 8,
+        in_specs=[SMEM] * 2 + [VMEM] * 9,
         out_specs=[VMEM] * 2,
         scratch_shapes=[tile, message, message, planes(PLANES)],
         compiler_params=params,
         name="edge_planes",
-    )(design_box, pml_width, *fields, rows_far, rows_near)
+    )(design_box, pml_width, *inputs, rows_far, rows_near)
     far, near = swap_both(far, near, "xy")
 
     count = rows_x + 1
@@ -630,18 +630,18 @@
             array(3, 4, rows_z, cols),
             array(3, 4, rows_z, cols),
         ),
-        in_specs=[SMEM] * 2 + [VMEM] * 8,
+        in_specs=[SMEM] * 2 + [VMEM] * 9,
         out_specs=[HBM] * 2 + [VMEM] * 4,
         scratch_shapes=[tile]
         + [planes(3, count)] * 4
         + [planes(count)] * 4
         + [pltpu.VMEM((rows_x, rows_z, cols), f32)] * 3
         + [pltpu.VMEM((3, rows_x, rows_z, cols), f32)] * 2
-        + [pltpu.SemaphoreType.DMA((2, rows_x))],
+        + [pltpu.SemaphoreType.DMA((2, rows_x // UNROLL))],
         compiler_params=params,
         cost_estimate=pl.CostEstimate(flops=50000000, bytes_accessed=8000000, transcendentals=0),
         name="sweep",
-    )(design_box, pml_width, *fields, rows_far, rows_near)
+    )(design_box, pml_width, *inputs, rows_far, rows_near)
 
     edge_e, edge_h, shares = pl.pallas_call(
         functools.partial(response, geometry),
@@ -655,7 +655,7 @@
         ],
         compiler_params=params,
         name="response",
-    )(design_box, pml_width, e_check, adj_e_end, edge, edge_e, edge_h, local_grad, far, near)
+    )(design_box, pml_width, inputs[0], inputs[2], edge, edge_e, edge_h, local_grad, far, near)
 
     parts = lax.all_to_all(shares, "gz", split_axis=0, concat_axis=0, tiled=True)
     back_e, back_h, pattern_grad = pl.pallas_call(

time: 46.1 us -> 41.5 us (0.900)
  waiting for transfers between devices: 4.27 us -> 1.59 us
  Pallas kernels: 11.6 us -> 9.24 us
  blocking collectives: 15.6 us -> 16.2 us
    ppermute x4, waiting for transfers between devices: 4.27 us -> 1.59 us  [swapped(): return lax.ppermute(shard, axis, pairs)]
    pallas_call x1, Pallas kernels: 5.75 us -> 4.25 us  [shards(): pl.pallas_call(functools.partial(sweep, geometry), out_shape=(array(*e_ch...]
    pallas_call x1, Pallas kernels: 2.68 us -> 1.85 us  [shards(): pl.pallas_call(load_fields, out_shape=tuple((pltpu.VMEM(ref.shape, ref.dt...]
    all_to_all x1, blocking collectives: 15.6 us -> 16.2 us  [shards(): lax.all_to_all(shares, 'gz', split_axis=0, concat_axis=0, tiled=True)]
  transfers between devices with their start and end apart: 4 -> 4, of which waited for: 1 -> 1; matrix products, arithmetic and copies ran while one was open for 0% -> 0% of each run, Pallas kernels for 13% -> 10%
where the time goes in v4:
time: 41.5 us; the launch traced here: 41.2 us
  blocking collectives  16.2 us (39%)
  starting transfers between devices  13.5 us (33%)
  Pallas kernels  9.24 us (22%)
  waiting for transfers between devices  1.59 us (4%)
  between operations  0.71 us (2%)
    all_to_all x1, blocking collectives, shards(): lax.all_to_all(shares, 'gz', split_axis=0, concat_axis=0, tiled=True)  16.2 us
    ppermute x4, starting transfers between devices, swapped(): return lax.ppermute(shard, axis, pairs)  13.5 us
    pallas_call x1, Pallas kernels, shards(): pl.pallas_call(functools.partial(sweep, geometry), out_shape=(array(*e_ch...  4.25 us
    pallas_call x1, Pallas kernels, shards(): pl.pallas_call(load_fields, out_shape=tuple((pltpu.VMEM(ref.shape, ref.dt...  1.85 us
    ppermute x4, waiting for transfers between devices, swapped(): return lax.ppermute(shard, axis, pairs)  1.59 us
    pallas_call x1, Pallas kernels, shards(): pl.pallas_call(finish, out_shape=(array(*e_check.shape), array(*e_check.s...  1.33 us
    pallas_call x1, Pallas kernels, shards(): pl.pallas_call(functools.partial(response, geometry), out_shape=(array(*e...  0.98 us
    pallas_call x1, Pallas kernels, shards(): pl.pallas_call(functools.partial(edge_planes, geometry), out_shape=(array...  0.83 us
  transfers between devices with their start and end apart: 4, of which 1 were waited for; matrix products, arithmetic and copies ran while one was open for 0% of the time, Pallas kernels for 10%

profile of v4, /device:TPU:225, one launch (start us, length us, event | category | flops | bytes accessed | tf_op | source)
XLA Modules:
  0.0 41.2 jit_solution(3513839240551061076)
XLA Ops:
  0.6 1.8 %load_fields.1 = (f32[3,16,24,128]{3,2,1,0:T(8,128)S(1)}, f32[3,16,24,128]{3,2,1,0:T(8,128)S(1)}, f32[3,16,24,128]{3,2,1,0:T(8,128)S(1)}, f32[3,16,24,128]{3,2,1...) custom-call(f32[3,16,24,128]{3,2,1,0:T(8,128)} %refs_0_.1, ...), custom_call_target="tpu_custom_call" | custom-call | tf_op jit(solution)/shard_map/load_fields/pallas_call | solution.py:594
  2.5 3.8 %collective-permute-start = (f32[416,128]{1,0:T(8,128)S(1)}, f32[416,128]{1,0:T(8,128)S(1)}, u32[]{:S(2)}, u32[]{:S(2)}) collective-permute-start(f32[416,128]{1,0:T(8,128)S(1)} %get-tuple-element.37), channel_id=1, source_target_pairs={{1,2},{2,1},{3,4},{4,3},{5,6},{6,5},{7,8},{8,7},{9,10},{10,9},{11,... | collective-permute-start | bytes 638984 | tf_op jit(solution)/shard_map/ppermute | solution.py:41
  6.3 1.9 %collective-permute-start.1 = (f32[416,128]{1,0:T(8,128)S(1)}, f32[416,128]{1,0:T(8,128)S(1)}, u32[]{:S(2)}, u32[]{:S(2)}) collective-permute-start(f32[416,128]{1,0:T(8,128)S(1)} %get-tuple-element.38), channel_id=1, source_target_pairs={{0,1},{1,0},{2,3},{3,2},{4,5},{5,4},{6,7},{7,6},{8,9},{9,8},{10,11... | collective-permute-start | bytes 638984 | tf_op jit(solution)/shard_map/ppermute | solution.py:41
  8.2 1.6 %collective-permute-done.refs_7_ = f32[416,128]{1,0:T(8,128)S(1)} collective-permute-done((f32[416,128]{1,0:T(8,128)S(1)}, f32[416,128]{1,0:T(8,128)S(1)}, u32[]{:S(2)}, u32[]{:S(2)}) %collective-permute-start) | collective-permute-done | bytes 213024 | tf_op jit(solution)/shard_map/ppermute | solution.py:41
  9.8 0.0 collective-permute-done.1.refs_8_
  9.8 0.8 %edge_planes.1 = (f32[232,128]{1,0:T(8,128)S(1)}, f32[232,128]{1,0:T(8,128)S(1)}) custom-call(s32[6]{0:T(128)S(1)} %get-tuple-element.28.box, s32[3]{0:T(128)S(1)} %get-tuple-element.29.pml, f32[3,16,24,128]{3,2,1,0:T(8,128)S(1)} %get-tuple-element.30.refs_0_, f32[3,16,24,128]{3,2,1,0:T(8,128)S(1)} %get-tuple-element.32.refs_1_, ...), custom_call_target="tpu_custom_call" | custom-call | tf_op jit(solution)/shard_map/edge_planes/pallas_call | solution.py:611
  10.6 2.7 %collective-permute-start.2 = (f32[232,128]{1,0:T(8,128)S(1)}, f32[232,128]{1,0:T(8,128)S(1)}, u32[]{:S(2)}, u32[]{:S(2)}) collective-permute-start(f32[232,128]{1,0:T(8,128)S(1)} %get-tuple-element.43), channel_id=1, source_target_pairs={{16,32},{32,16},{48,64},{64,48},{80,96},{96,80},{112,128},{128,112... | collective-permute-start | bytes 356360 | tf_op jit(solution)/shard_map/ppermute | solution.py:41
  13.3 5.2 %collective-permute-start.3 = (f32[232,128]{1,0:T(8,128)S(1)}, f32[232,128]{1,0:T(8,128)S(1)}, u32[]{:S(2)}, u32[]{:S(2)}) collective-permute-start(f32[232,128]{1,0:T(8,128)S(1)} %get-tuple-element.44), channel_id=1, source_target_pairs={{0,16},{16,0},{32,48},{48,32},{64,80},{80,64},{96,112},{112,96},{1... | collective-permute-start | bytes 356360 | tf_op jit(solution)/shard_map/ppermute | solution.py:41
  18.5 4.2 %sweep.1 = (f32[3,16,24,128]{3,2,1,0:T(8,128)}, f32[3,16,24,128]{3,2,1,0:T(8,128)}, f32[16,128]{1,0:T(8,128)S(1)}, f32[38,32,128]{2,1,0:T(8,128)S(1)}, f32[3,4,2...) custom-call(s32[6]{0:T(128)S(1)} %get-tuple-element.28.box, s32[3]{0:T(128)S(1)} %get-tuple-element.29.pml, ...), custom_call_target="tpu_custom_call" | custom-call | flops 50000000 | bytes 8000000 | tf_op jit(solution)/shard_map/sweep/pallas_call | solution.py:623
  22.7 0.0 collective-permute-done.2.refs_6_
  22.7 0.0 collective-permute-done.3.refs_7_
  22.8 1.0 %response.1 = (f32[3,4,24,128]{3,2,1,0:T(8,128)S(1)}, f32[3,4,24,128]{3,2,1,0:T(8,128)S(1)}, f32[128,128]{1,0:T(8,128)S(1)}) custom-call(s32[6]{0:T(128)S(1)} %get-tuple-element.28.box, s32[3]{0:T(128)S(1)} %get-tuple-element.29.pml, f32[3,16,24,128]{3,2,1,0:T(8,128)S(1)} %get-tuple-element.30.refs_0_, ...), custom_call_target="tpu_custom_call" | custom-call | tf_op jit(solution)/shard_map/response/pallas_call | solution.py:646
  23.7 16.2 %all_to_all.11 = f32[16,8,128]{2,1,0:T(8,128)S(1)} all-to-all(f32[16,8,128]{2,1,0:T(8,128)S(1)} %bitcast.4), channel_id=1, replica_groups=mesh['xy'=32,'gz'=16] {'gz'}, dimensions={0} | all-to-all | bytes 131072 | tf_op jit(solution)/shard_map/all_to_all | solution.py:660
  39.9 1.3 %finish.1 = (f32[3,16,24,128]{3,2,1,0:T(8,128)}, f32[3,16,24,128]{3,2,1,0:T(8,128)}, f32[8,16]{1,0:T(8,128)}) custom-call(f32[128,128]{1,0:T(8,128)S(1)} %bitcast.3, f32[3,4,24,128]{3,2,1,0:T(8,128)S(1)} %get-tuple-element.46.edge_e, f32[3,4,24,128]{3,2,1,0:T(8,128)S(1)} %get-tuple-element.47.edge_h, ...), custom_call_target="tpu_custom_call", output_to_operand_aliasing={{0}: (3, {}), {1}: (4, {})} | custom-call | tf_op jit(solution)/shard_map/finish/pallas_call | solution.py:661
Async XLA Ops:
  2.5 7.3 %collective-permute-start = (f32[416,128]{1,0:T(8,128)S(1)}, f32[416,128]{1,0:T(8,128)S(1)}, u32[]{:S(2)}, u32[]{:S(2)}) collective-permute-start(f32[416,128]{1,0:T(8,128)S(1)} %get-tuple-element.37), channel_id=1, source_target_pairs={{1,2},{2,1},{3,4},{4,3},{5,6},{6,5},{7,8},{8,7},{9,10},{10,9},{11,... | collective-permute-start | bytes 638984 | tf_op jit(solution)/shard_map/ppermute | solution.py:41
  6.3 3.5 %collective-permute-start.1 = (f32[416,128]{1,0:T(8,128)S(1)}, f32[416,128]{1,0:T(8,128)S(1)}, u32[]{:S(2)}, u32[]{:S(2)}) collective-permute-start(f32[416,128]{1,0:T(8,128)S(1)} %get-tuple-element.38), channel_id=1, source_target_pairs={{0,1},{1,0},{2,3},{3,2},{4,5},{5,4},{6,7},{7,6},{8,9},{9,8},{10,11... | collective-permute-start | bytes 638984 | tf_op jit(solution)/shard_map/ppermute | solution.py:41
  10.6 12.1 %collective-permute-start.2 = (f32[232,128]{1,0:T(8,128)S(1)}, f32[232,128]{1,0:T(8,128)S(1)}, u32[]{:S(2)}, u32[]{:S(2)}) collective-permute-start(f32[232,128]{1,0:T(8,128)S(1)} %get-tuple-element.43), channel_id=1, source_target_pairs={{16,32},{32,16},{48,64},{64,48},{80,96},{96,80},{112,128},{128,112... | collective-permute-start | bytes 356360 | tf_op jit(solution)/shard_map/ppermute | solution.py:41
  13.3 9.5 %collective-permute-start.3 = (f32[232,128]{1,0:T(8,128)S(1)}, f32[232,128]{1,0:T(8,128)S(1)}, u32[]{:S(2)}, u32[]{:S(2)}) collective-permute-start(f32[232,128]{1,0:T(8,128)S(1)} %get-tuple-element.44), channel_id=1, source_target_pairs={{0,16},{16,0},{32,48},{48,32},{64,80},{80,64},{96,112},{112,96},{1... | collective-permute-start | bytes 356360 | tf_op jit(solution)/shard_map/ppermute | solution.py:41

commit v5 on v4

--- a/solution.py
+++ b/solution.py
@@ -295,8 +295,10 @@
 
     even = is_even("xy")
     to_next, to_prev = buffers[0][...], buffers[1][...]
+    size = to_next.shape[0]
     far[...] = jnp.where(even, to_prev, to_next)
-    near[...] = jnp.where(even, to_next, to_prev)
+    near[pl.ds(0, size), :] = jnp.where(even, to_next, to_prev)
+    near[pl.ds(size, 8), :] = jnp.zeros((8, to_next.shape[1]), jnp.float32)
 
 
 def sweep(geometry, box, pml, *refs):
@@ -445,8 +447,9 @@
     last = rows_x - 1
     grid = Grid(box, pml, *geometry)
     even = is_even("xy")
-    buffers[0] = jnp.where(even, far[...], near[...])
-    buffers[1] = jnp.where(even, near[...], far[...])
+    close = near[pl.ds(0, far.shape[0]), :]
+    buffers[0] = jnp.where(even, far[...], close)
+    buffers[1] = jnp.where(even, close, far[...])
     grad[...] = jnp.zeros(grad.shape, jnp.float32)
     grad[pl.ds(0, rows_x), :] = local_grad[...]
     for side, rows in enumerate((NEXT_ROWS, PREV_ROWS)):
@@ -557,7 +560,8 @@
     shares[...] = jnp.transpose(grad[...])
 
 
-def finish(parts, edge_e, edge_h, in_e, in_h, out_e, out_h, out, sems):
+def finish(parts, edge_e, edge_h, in_e, in_h, out_e, out_h, out, total, sems):
+    share, rows_x = out.shape
     last = out_e.shape[1] - 2
     copies = []
     for i, (edge, full) in enumerate(((edge_e, out_e), (edge_h, out_h))):
@@ -567,12 +571,13 @@
             )
             copy.start()
             copies.append(copy)
-    share, rows_x = out.shape
-    total = parts[pl.ds(0, share), :]
-    for j in range(1, parts.shape[0] // share):
-        total = total + parts[pl.ds(j * share, share), :]
-    out[...] = total[:, :rows_x]
-    for copy in copies:
+    rows = [parts[pl.ds(j * share, share), :] for j in range(parts.shape[0] // share)]
+    while len(rows) > 1:
+        rows = [a + b for a, b in zip(rows[::2], rows[1::2])] + rows[len(rows) // 2 * 2 :]
+    total[...] = rows[0][:, :rows_x]
+    copy = pltpu.make_async_copy(total, out, sems.at[4])
+    copy.start()
+    for copy in copies + [copy]:
         copy.wait()
 
 
@@ -610,7 +615,7 @@
     tile = pltpu.VMEM((SLOTS, rows_x, EXT, cols), f32)
     far, near = pl.pallas_call(
         functools.partial(edge_planes, geometry),
-        out_shape=(array(size, cols),) * 2,
+        out_shape=(array(size, cols), array(size + 8, cols)),
         in_specs=[SMEM] * 2 + [VMEM] * 9,
         out_specs=[VMEM] * 2,
         scratch_shapes=[tile, message, message, planes(PLANES)],
@@ -662,8 +667,11 @@
         finish,
         out_shape=(array(*e_check.shape), array(*e_check.shape), array(cols // size_z, rows_x)),
         in_specs=[VMEM] * 3 + [HBM] * 2,
-        out_specs=[HBM] * 2 + [VMEM],
-        scratch_shapes=[pltpu.SemaphoreType.DMA((4,))],
+        out_specs=[HBM] * 3,
+        scratch_shapes=[
+            pltpu.VMEM((cols // size_z, rows_x), f32),
+            pltpu.SemaphoreType.DMA((5,)),
+        ],
         input_output_aliases={3: 0, 4: 1},
         compiler_params=pltpu.CompilerParams(vmem_limit_bytes=8 * 1024 * 1024),
         name="finish",

time: 41.5 us -> 40.2 us (0.969)
  the two profiles are of different devices: /device:TPU:225 before, /device:TPU:385 now
where the time goes in v5:
time: 40.2 us; the launch traced here: 39.9 us
  blocking collectives  15.8 us (39%)
  starting transfers between devices  12.6 us (31%)
  Pallas kernels  8.66 us (22%)
  waiting for transfers between devices  2.09 us (5%)
  between operations  0.69 us (2%)
    all_to_all x1, blocking collectives, shards(): lax.all_to_all(shares, 'gz', split_axis=0, concat_axis=0, tiled=True)  15.8 us
    ppermute x4, starting transfers between devices, swapped(): return lax.ppermute(shard, axis, pairs)  12.6 us
    pallas_call x1, Pallas kernels, shards(): pl.pallas_call(functools.partial(sweep, geometry), out_shape=(array(*e_ch...  4.25 us
    ppermute x4, waiting for transfers between devices, swapped(): return lax.ppermute(shard, axis, pairs)  2.09 us
    pallas_call x1, Pallas kernels, shards(): pl.pallas_call(load_fields, out_shape=tuple((pltpu.VMEM(ref.shape, ref.dt...  1.85 us
    pallas_call x1, Pallas kernels, shards(): pl.pallas_call(functools.partial(response, geometry), out_shape=(array(*e...  0.98 us
    pallas_call x1, Pallas kernels, shards(): pl.pallas_call(functools.partial(edge_planes, geometry), out_shape=(array...  0.83 us
  transfers between devices with their start and end apart: 4, of which 2 were waited for; matrix products, arithmetic and copies ran while one was open for 0% of the time, Pallas kernels for 11%

profile of v5, /device:TPU:385, one launch (start us, length us, event | category | flops | bytes accessed | tf_op | source)
XLA Modules:
  0.0 39.9 jit_solution(12579318897047331084)
XLA Ops:
  0.6 1.8 %load_fields.1 = (f32[3,16,24,128]{3,2,1,0:T(8,128)S(1)}, f32[3,16,24,128]{3,2,1,0:T(8,128)S(1)}, f32[3,16,24,128]{3,2,1,0:T(8,128)S(1)}, f32[3,16,24,128]{3,2,1...) custom-call(f32[3,16,24,128]{3,2,1,0:T(8,128)} %refs_0_.1, ...), custom_call_target="tpu_custom_call" | custom-call | tf_op jit(solution)/shard_map/load_fields/pallas_call | solution.py:599
  2.5 3.8 %collective-permute-start = (f32[416,128]{1,0:T(8,128)S(1)}, f32[416,128]{1,0:T(8,128)S(1)}, u32[]{:S(2)}, u32[]{:S(2)}) collective-permute-start(f32[416,128]{1,0:T(8,128)S(1)} %get-tuple-element.37), channel_id=1, source_target_pairs={{1,2},{2,1},{3,4},{4,3},{5,6},{6,5},{7,8},{8,7},{9,10},{10,9},{11,... | collective-permute-start | bytes 638984 | tf_op jit(solution)/shard_map/ppermute | solution.py:41
  6.3 1.9 %collective-permute-start.1 = (f32[416,128]{1,0:T(8,128)S(1)}, f32[416,128]{1,0:T(8,128)S(1)}, u32[]{:S(2)}, u32[]{:S(2)}) collective-permute-start(f32[416,128]{1,0:T(8,128)S(1)} %get-tuple-element.38), channel_id=1, source_target_pairs={{0,1},{1,0},{2,3},{3,2},{4,5},{5,4},{6,7},{7,6},{8,9},{9,8},{10,11... | collective-permute-start | bytes 638984 | tf_op jit(solution)/shard_map/ppermute | solution.py:41
  8.2 1.6 %collective-permute-done.refs_7_ = f32[416,128]{1,0:T(8,128)S(1)} collective-permute-done((f32[416,128]{1,0:T(8,128)S(1)}, f32[416,128]{1,0:T(8,128)S(1)}, u32[]{:S(2)}, u32[]{:S(2)}) %collective-permute-start) | collective-permute-done | bytes 213024 | tf_op jit(solution)/shard_map/ppermute | solution.py:41
  9.8 0.0 collective-permute-done.1.refs_8_
  9.8 0.8 %edge_planes.1 = (f32[232,128]{1,0:T(8,128)S(1)}, f32[240,128]{1,0:T(8,128)S(1)}) custom-call(s32[6]{0:T(128)S(1)} %get-tuple-element.28.box, s32[3]{0:T(128)S(1)} %get-tuple-element.29.pml, f32[3,16,24,128]{3,2,1,0:T(8,128)S(1)} %get-tuple-element.30.refs_0_, f32[3,16,24,128]{3,2,1,0:T(8,128)S(1)} %get-tuple-element.32.refs_1_, ...), custom_call_target="tpu_custom_call" | custom-call | tf_op jit(solution)/shard_map/edge_planes/pallas_call | solution.py:616
  10.6 3.1 %collective-permute-start.3 = (f32[240,128]{1,0:T(8,128)S(1)}, f32[240,128]{1,0:T(8,128)S(1)}, u32[]{:S(2)}, u32[]{:S(2)}) collective-permute-start(f32[240,128]{1,0:T(8,128)S(1)} %get-tuple-element.44), channel_id=1, source_target_pairs={{0,16},{16,0},{32,48},{48,32},{64,80},{80,64},{96,112},{112,96},{1... | collective-permute-start | bytes 368648 | tf_op jit(solution)/shard_map/ppermute | solution.py:41
  13.7 3.8 %collective-permute-start.2 = (f32[232,128]{1,0:T(8,128)S(1)}, f32[232,128]{1,0:T(8,128)S(1)}, u32[]{:S(2)}, u32[]{:S(2)}) collective-permute-start(f32[232,128]{1,0:T(8,128)S(1)} %get-tuple-element.43), channel_id=1, source_target_pairs={{16,32},{32,16},{48,64},{64,48},{80,96},{96,80},{112,128},{128,112... | collective-permute-start | bytes 356360 | tf_op jit(solution)/shard_map/ppermute | solution.py:41
  17.6 4.2 %sweep.1 = (f32[3,16,24,128]{3,2,1,0:T(8,128)}, f32[3,16,24,128]{3,2,1,0:T(8,128)}, f32[16,128]{1,0:T(8,128)S(1)}, f32[38,32,128]{2,1,0:T(8,128)S(1)}, f32[3,4,2...) custom-call(s32[6]{0:T(128)S(1)} %get-tuple-element.28.box, s32[3]{0:T(128)S(1)} %get-tuple-element.29.pml, ...), custom_call_target="tpu_custom_call" | custom-call | flops 50000000 | bytes 8000000 | tf_op jit(solution)/shard_map/sweep/pallas_call | solution.py:628
  21.8 0.5 %collective-permute-done.2.refs_6_ = f32[232,128]{1,0:T(8,128)S(1)} collective-permute-done((f32[232,128]{1,0:T(8,128)S(1)}, f32[232,128]{1,0:T(8,128)S(1)}, u32[]{:S(2)}, u32[]{:S(2)}) %collective-permute-start.2) | collective-permute-done | bytes 118816 | tf_op jit(solution)/shard_map/ppermute | solution.py:41
  22.3 0.0 collective-permute-done.3.refs_7_
  22.3 1.0 %response.1 = (f32[3,4,24,128]{3,2,1,0:T(8,128)S(1)}, f32[3,4,24,128]{3,2,1,0:T(8,128)S(1)}, f32[128,128]{1,0:T(8,128)S(1)}) custom-call(s32[6]{0:T(128)S(1)} %get-tuple-element.28.box, s32[3]{0:T(128)S(1)} %get-tuple-element.29.pml, f32[3,16,24,128]{3,2,1,0:T(8,128)S(1)} %get-tuple-element.30.refs_0_, ...), custom_call_target="tpu_custom_call" | custom-call | tf_op jit(solution)/shard_map/response/pallas_call | solution.py:651
  23.3 15.8 %all_to_all.11 = f32[16,8,128]{2,1,0:T(8,128)S(1)} all-to-all(f32[16,8,128]{2,1,0:T(8,128)S(1)} %bitcast.4), channel_id=1, replica_groups=mesh['xy'=32,'gz'=16] {'gz'}, dimensions={0} | all-to-all | bytes 131072 | tf_op jit(solution)/shard_map/all_to_all | solution.py:665
  39.2 0.8 %finish.1 = (f32[3,16,24,128]{3,2,1,0:T(8,128)}, f32[3,16,24,128]{3,2,1,0:T(8,128)}, f32[8,16]{1,0:T(8,128)}) custom-call(f32[128,128]{1,0:T(8,128)S(1)} %bitcast.3, f32[3,4,24,128]{3,2,1,0:T(8,128)S(1)} %get-tuple-element.46.edge_e, f32[3,4,24,128]{3,2,1,0:T(8,128)S(1)} %get-tuple-element.47.edge_h, ...), custom_call_target="tpu_custom_call", output_to_operand_aliasing={{0}: (3, {}), {1}: (4, {})} | custom-call | tf_op jit(solution)/shard_map/finish/pallas_call | solution.py:666
Async XLA Ops:
  2.5 7.3 %collective-permute-start = (f32[416,128]{1,0:T(8,128)S(1)}, f32[416,128]{1,0:T(8,128)S(1)}, u32[]{:S(2)}, u32[]{:S(2)}) collective-permute-start(f32[416,128]{1,0:T(8,128)S(1)} %get-tuple-element.37), channel_id=1, source_target_pairs={{1,2},{2,1},{3,4},{4,3},{5,6},{6,5},{7,8},{8,7},{9,10},{10,9},{11,... | collective-permute-start | bytes 638984 | tf_op jit(solution)/shard_map/ppermute | solution.py:41
  6.3 3.5 %collective-permute-start.1 = (f32[416,128]{1,0:T(8,128)S(1)}, f32[416,128]{1,0:T(8,128)S(1)}, u32[]{:S(2)}, u32[]{:S(2)}) collective-permute-start(f32[416,128]{1,0:T(8,128)S(1)} %get-tuple-element.38), channel_id=1, source_target_pairs={{0,1},{1,0},{2,3},{3,2},{4,5},{5,4},{6,7},{7,6},{8,9},{9,8},{10,11... | collective-permute-start | bytes 638984 | tf_op jit(solution)/shard_map/ppermute | solution.py:41
  10.6 11.7 %collective-permute-start.3 = (f32[240,128]{1,0:T(8,128)S(1)}, f32[240,128]{1,0:T(8,128)S(1)}, u32[]{:S(2)}, u32[]{:S(2)}) collective-permute-start(f32[240,128]{1,0:T(8,128)S(1)} %get-tuple-element.44), channel_id=1, source_target_pairs={{0,16},{16,0},{32,48},{48,32},{64,80},{80,64},{96,112},{112,96},{1... | collective-permute-start | bytes 368648 | tf_op jit(solution)/shard_map/ppermute | solution.py:41
  13.7 8.6 %collective-permute-start.2 = (f32[232,128]{1,0:T(8,128)S(1)}, f32[232,128]{1,0:T(8,128)S(1)}, u32[]{:S(2)}, u32[]{:S(2)}) collective-permute-start(f32[232,128]{1,0:T(8,128)S(1)} %get-tuple-element.43), channel_id=1, source_target_pairs={{16,32},{32,16},{48,64},{64,48},{80,96},{96,80},{112,128},{128,112... | collective-permute-start | bytes 356360 | tf_op jit(solution)/shard_map/ppermute | solution.py:41

commit v6 on v5

--- a/solution.py
+++ b/solution.py
@@ -58,11 +58,10 @@
     sources, copies_of, (far, near) = refs[:9], refs[9:18], refs[18:20]
     first, last, sems = refs[20:]
     rows_x, rows_z = sources[4].shape[:2]
-    copies = []
-    for i, (source, target) in enumerate(zip(sources, copies_of)):
-        copy = pltpu.make_async_copy(source, target, sems.at[i])
-        copy.start()
-        copies.append(copy)
+    copies = [None] * len(sources)
+    for i in (6, 7, 8, 0, 1, 2, 3, 4, 5):
+        copies[i] = pltpu.make_async_copy(sources[i], copies_of[i], sems.at[i])
+        copies[i].start()
 
     for i in range(6):
         copies[i].wait()
@@ -407,10 +406,13 @@
         return new_h[1:], scaled[1:]
 
     def second_group(group, carry):
+        @pl.when(group > 0)
+        def _():
+            for copy in out_copies(group - 1):
+                copy.start()
+
         for i in range(UNROLL):
             carry = second(group * UNROLL + i, carry)
-        for copy in out_copies(group):
-            copy.start()
         return carry
 
     groups = rows_x // UNROLL
@@ -431,37 +433,39 @@
     start = 6 + len(kept)
     for k, value in enumerate((by_e[0], by_r[0], by_r[1], by_r[last - 1], by_e[last], by_r[last])):
         edge[start + k, own, :] = value
-    for i, x in enumerate((0, 1, last - 1, last)):
+    for i, x in enumerate((0, 1, *range(rows_x - UNROLL, rows_x))):
         for k in range(3):
             edge_e[k, i] = out_e[k, x]
             edge_h[k, i] = out_h[k, x]
-    for group in range(groups):
+    for group in range(groups - 1):
         for copy in out_copies(group):
             copy.wait()
 
 
 def response(geometry, box, pml, *refs):
     e_ref, p_ref, edge, local_e, local_h, local_grad, far, near = refs[:8]
-    edge_e, edge_h, shares, buffers, tile, grad = refs[8:]
+    edge_e, edge_h, shares, tile, grad = refs[8:]
     rows_x, rows_z, cols = geometry[:3]
     last = rows_x - 1
     grid = Grid(box, pml, *geometry)
     even = is_even("xy")
-    close = near[pl.ds(0, far.shape[0]), :]
-    buffers[0] = jnp.where(even, far[...], close)
-    buffers[1] = jnp.where(even, close, far[...])
-    grad[...] = jnp.zeros(grad.shape, jnp.float32)
-    grad[pl.ds(0, rows_x), :] = local_grad[...]
+
+    def received(side, at, count):
+        rows = pl.ds(at, count)
+        pair = (far[rows, :], near[rows, :])
+        return jnp.where(even, pair[side], pair[1 - side])
+
+    grad[...] = local_grad[...]
     for side, rows in enumerate((NEXT_ROWS, PREV_ROWS)):
         for k in range(PLANES):
             tile[side, k] = jnp.zeros(tile.shape[2:], jnp.float32)
         for i, (k, r) in enumerate(rows):
-            row = buffers[side, pl.ds(PLANES * rows_z + i, 1), :]
+            row = received(side, PLANES * rows_z + i, 1)
             tile[side, k, pl.ds(r if r >= 0 else EXT + r, 1), :] = row
 
     def unpack(side):
         return [
-            jnp.concatenate([buffers[side, pl.ds(k * rows_z, rows_z), :], tile[side, k]], axis=0)
+            jnp.concatenate([received(side, k * rows_z, rows_z), tile[side, k]], axis=0)
             for k in range(PLANES)
         ]
 
@@ -541,11 +545,15 @@
     k_n2 = (db_k * k_m2[0], db_k * k_m2[1])
     k_r2 = minus_yz(*k_h2)
     d_r2 = minus(d_h2, *k_h2)
-    write(edge_e, local_e, 2, [-v for v in minus_yz(*k_n2)])
+    kept, before_last, at_last = range(2, UNROLL), UNROLL, UNROLL + 1
+    for i in kept:
+        write(edge_e, local_e, i, (None, None, None))
+        write(edge_h, local_h, i, (None, None, None))
+    write(edge_e, local_e, before_last, [-v for v in minus_yz(*k_n2)])
     curl = minus([db_l * v for v in d_m2], *k_n2)
-    write(edge_e, local_e, 3, [ca_l * v - c for v, c in zip(d_p, curl)])
-    write(edge_h, local_h, 2, (None, da_k * k_m2[0], da_k * k_m2[1]))
-    write(edge_h, local_h, 3, [da_l * v for v in d_m2])
+    write(edge_e, local_e, at_last, [ca_l * v - c for v, c in zip(d_p, curl)])
+    write(edge_h, local_h, before_last, (None, da_k * k_m2[0], da_k * k_m2[1]))
+    write(edge_h, local_h, at_last, [da_l * v for v in d_m2])
     p2 = [p_ref[k, last] for k in range(3)]
     along_e = dot([own(v) for v in d_p], [e_ref[k, last] for k in range(3)])
     along_e = along_e + dot(p2, [own(v) for v in d_ele])
@@ -557,17 +565,18 @@
     p2 = [p_ref[k, last - 1] for k in range(3)]
     add_rows(last - 1, weight(3) * dot(p2, [own(v) for v in k_r2]))
 
-    shares[...] = jnp.transpose(grad[...])
+    shares[...] = jnp.zeros(shares.shape, jnp.float32)
+    shares[:, :rows_x] = jnp.transpose(grad[...])
 
 
 def finish(parts, edge_e, edge_h, in_e, in_h, out_e, out_h, out, total, sems):
     share, rows_x = out.shape
-    last = out_e.shape[1] - 2
+    tail = out_e.shape[1] - UNROLL
     copies = []
     for i, (edge, full) in enumerate(((edge_e, out_e), (edge_h, out_h))):
-        for side, start in enumerate((0, last)):
+        for side, (at, start, count) in enumerate(((0, 0, 2), (2, tail, UNROLL))):
             copy = pltpu.make_async_copy(
-                edge.at[:, pl.ds(2 * side, 2)], full.at[:, pl.ds(start, 2)], sems.at[2 * i + side]
+                edge.at[:, pl.ds(at, count)], full.at[:, pl.ds(start, count)], sems.at[2 * i + side]
             )
             copy.start()
             copies.append(copy)
@@ -632,8 +641,8 @@
             array(*e_check.shape),
             array(rows_x, cols),
             array(EDGE_PLANES, rows_z + EXT, cols),
-            array(3, 4, rows_z, cols),
-            array(3, 4, rows_z, cols),
+            array(3, 2 + UNROLL, rows_z, cols),
+            array(3, 2 + UNROLL, rows_z, cols),
         ),
         in_specs=[SMEM] * 2 + [VMEM] * 9,
         out_specs=[HBM] * 2 + [VMEM] * 4,
@@ -654,9 +663,8 @@
         in_specs=[SMEM] * 2 + [VMEM] * 8,
         out_specs=[VMEM] * 3,
         scratch_shapes=[
-            pltpu.VMEM((2, size, cols), f32),
             pltpu.VMEM((2, PLANES, EXT, cols), f32),
-            pltpu.VMEM((cols, cols), f32),
+            pltpu.VMEM((rows_x, cols), f32),
         ],
         compiler_params=params,
         name="response",

time: 40.2 us -> 40.3 us (level)
  transfers between devices with their start and end apart: 4 -> 4, of which waited for: 2 -> 2; matrix products, arithmetic and copies ran while one was open for 0% -> 0% of each run, Pallas kernels for 11% -> 10%
where the time goes in v6:
time: 40.3 us; the launch traced here: 40 us
  blocking collectives  15.8 us (39%)
  starting transfers between devices  12.6 us (31%)
  Pallas kernels  8.54 us (21%)
  waiting for transfers between devices  2.31 us (6%)
  between operations  0.69 us (2%)
    all_to_all x1, blocking collectives, shards(): lax.all_to_all(shares, 'gz', split_axis=0, concat_axis=0, tiled=True)  15.8 us
    ppermute x4, starting transfers between devices, swapped(): return lax.ppermute(shard, axis, pairs)  12.6 us
    pallas_call x1, Pallas kernels, shards(): pl.pallas_call(functools.partial(sweep, geometry), out_shape=(array(*e_ch...  4.03 us
    ppermute x4, waiting for transfers between devices, swapped(): return lax.ppermute(shard, axis, pairs)  2.31 us
    pallas_call x1, Pallas kernels, shards(): pl.pallas_call(load_fields, out_shape=tuple((pltpu.VMEM(ref.shape, ref.dt...  1.89 us
    pallas_call x1, Pallas kernels, shards(): pl.pallas_call(functools.partial(response, geometry), out_shape=(array(*e...  0.98 us
    pallas_call x1, Pallas kernels, shards(): pl.pallas_call(functools.partial(edge_planes, geometry), out_shape=(array...  0.83 us
  transfers between devices with their start and end apart: 4, of which 2 were waited for; matrix products, arithmetic and copies ran while one was open for 0% of the time, Pallas kernels for 10%

profile of v6, /device:TPU:385, one launch (start us, length us, event | category | flops | bytes accessed | tf_op | source)
XLA Modules:
  0.0 40.0 jit_solution(13068355696180238150)
XLA Ops:
  0.6 1.9 %load_fields.1 = (f32[3,16,24,128]{3,2,1,0:T(8,128)S(1)}, f32[3,16,24,128]{3,2,1,0:T(8,128)S(1)}, f32[3,16,24,128]{3,2,1,0:T(8,128)S(1)}, f32[3,16,24,128]{3,2,1...) custom-call(f32[3,16,24,128]{3,2,1,0:T(8,128)} %refs_0_.1, ...), custom_call_target="tpu_custom_call" | custom-call | tf_op jit(solution)/shard_map/load_fields/pallas_call | solution.py:608
  2.5 3.8 %collective-permute-start = (f32[416,128]{1,0:T(8,128)S(1)}, f32[416,128]{1,0:T(8,128)S(1)}, u32[]{:S(2)}, u32[]{:S(2)}) collective-permute-start(f32[416,128]{1,0:T(8,128)S(1)} %get-tuple-element.37), channel_id=1, source_target_pairs={{1,2},{2,1},{3,4},{4,3},{5,6},{6,5},{7,8},{8,7},{9,10},{10,9},{11,... | collective-permute-start | bytes 638984 | tf_op jit(solution)/shard_map/ppermute | solution.py:41
  6.3 1.9 %collective-permute-start.1 = (f32[416,128]{1,0:T(8,128)S(1)}, f32[416,128]{1,0:T(8,128)S(1)}, u32[]{:S(2)}, u32[]{:S(2)}) collective-permute-start(f32[416,128]{1,0:T(8,128)S(1)} %get-tuple-element.38), channel_id=1, source_target_pairs={{0,1},{1,0},{2,3},{3,2},{4,5},{5,4},{6,7},{7,6},{8,9},{9,8},{10,11... | collective-permute-start | bytes 638984 | tf_op jit(solution)/shard_map/ppermute | solution.py:41
  8.2 1.6 %collective-permute-done.refs_7_ = f32[416,128]{1,0:T(8,128)S(1)} collective-permute-done((f32[416,128]{1,0:T(8,128)S(1)}, f32[416,128]{1,0:T(8,128)S(1)}, u32[]{:S(2)}, u32[]{:S(2)}) %collective-permute-start) | collective-permute-done | bytes 213024 | tf_op jit(solution)/shard_map/ppermute | solution.py:41
  9.8 0.0 collective-permute-done.1.refs_8_
  9.8 0.8 %edge_planes.1 = (f32[232,128]{1,0:T(8,128)S(1)}, f32[240,128]{1,0:T(8,128)S(1)}) custom-call(s32[6]{0:T(128)S(1)} %get-tuple-element.28.box, s32[3]{0:T(128)S(1)} %get-tuple-element.29.pml, f32[3,16,24,128]{3,2,1,0:T(8,128)S(1)} %get-tuple-element.30.refs_0_, f32[3,16,24,128]{3,2,1,0:T(8,128)S(1)} %get-tuple-element.32.refs_1_, ...), custom_call_target="tpu_custom_call" | custom-call | tf_op jit(solution)/shard_map/edge_planes/pallas_call | solution.py:625
  10.7 3.1 %collective-permute-start.3 = (f32[240,128]{1,0:T(8,128)S(1)}, f32[240,128]{1,0:T(8,128)S(1)}, u32[]{:S(2)}, u32[]{:S(2)}) collective-permute-start(f32[240,128]{1,0:T(8,128)S(1)} %get-tuple-element.44), channel_id=1, source_target_pairs={{0,16},{16,0},{32,48},{48,32},{64,80},{80,64},{96,112},{112,96},{1... | collective-permute-start | bytes 368648 | tf_op jit(solution)/shard_map/ppermute | solution.py:41
  13.8 3.8 %collective-permute-start.2 = (f32[232,128]{1,0:T(8,128)S(1)}, f32[232,128]{1,0:T(8,128)S(1)}, u32[]{:S(2)}, u32[]{:S(2)}) collective-permute-start(f32[232,128]{1,0:T(8,128)S(1)} %get-tuple-element.43), channel_id=1, source_target_pairs={{16,32},{32,16},{48,64},{64,48},{80,96},{96,80},{112,128},{128,112... | collective-permute-start | bytes 356360 | tf_op jit(solution)/shard_map/ppermute | solution.py:41
  17.6 4.0 %sweep.1 = (f32[3,16,24,128]{3,2,1,0:T(8,128)}, f32[3,16,24,128]{3,2,1,0:T(8,128)}, f32[16,128]{1,0:T(8,128)S(1)}, f32[38,32,128]{2,1,0:T(8,128)S(1)}, f32[3,6,2...) custom-call(s32[6]{0:T(128)S(1)} %get-tuple-element.28.box, s32[3]{0:T(128)S(1)} %get-tuple-element.29.pml, ...), custom_call_target="tpu_custom_call" | custom-call | flops 50000000 | bytes 8000000 | tf_op jit(solution)/shard_map/sweep/pallas_call | solution.py:637
  21.7 0.7 %collective-permute-done.2.refs_6_ = f32[232,128]{1,0:T(8,128)S(1)} collective-permute-done((f32[232,128]{1,0:T(8,128)S(1)}, f32[232,128]{1,0:T(8,128)S(1)}, u32[]{:S(2)}, u32[]{:S(2)}) %collective-permute-start.2) | collective-permute-done | bytes 118816 | tf_op jit(solution)/shard_map/ppermute | solution.py:41
  22.4 0.0 collective-permute-done.3.refs_7_
  22.4 1.0 %response.1 = (f32[3,6,24,128]{3,2,1,0:T(8,128)S(1)}, f32[3,6,24,128]{3,2,1,0:T(8,128)S(1)}, f32[128,128]{1,0:T(8,128)S(1)}) custom-call(s32[6]{0:T(128)S(1)} %get-tuple-element.28.box, s32[3]{0:T(128)S(1)} %get-tuple-element.29.pml, f32[3,16,24,128]{3,2,1,0:T(8,128)S(1)} %get-tuple-element.30.refs_0_, ...), custom_call_target="tpu_custom_call" | custom-call | tf_op jit(solution)/shard_map/response/pallas_call | solution.py:660
  23.4 15.8 %all_to_all.11 = f32[16,8,128]{2,1,0:T(8,128)S(1)} all-to-all(f32[16,8,128]{2,1,0:T(8,128)S(1)} %bitcast.4), channel_id=1, replica_groups=mesh['xy'=32,'gz'=16] {'gz'}, dimensions={0} | all-to-all | bytes 131072 | tf_op jit(solution)/shard_map/all_to_all | solution.py:673
  39.2 0.8 %finish.1 = (f32[3,16,24,128]{3,2,1,0:T(8,128)}, f32[3,16,24,128]{3,2,1,0:T(8,128)}, f32[8,16]{1,0:T(8,128)}) custom-call(f32[128,128]{1,0:T(8,128)S(1)} %bitcast.3, f32[3,6,24,128]{3,2,1,0:T(8,128)S(1)} %get-tuple-element.46.edge_e, f32[3,6,24,128]{3,2,1,0:T(8,128)S(1)} %get-tuple-element.47.edge_h, ...), custom_call_target="tpu_custom_call", output_to_operand_aliasing={{0}: (3, {}), {1}: (4, {})} | custom-call | tf_op jit(solution)/shard_map/finish/pallas_call | solution.py:674
Async XLA Ops:
  2.5 7.3 %collective-permute-start = (f32[416,128]{1,0:T(8,128)S(1)}, f32[416,128]{1,0:T(8,128)S(1)}, u32[]{:S(2)}, u32[]{:S(2)}) collective-permute-start(f32[416,128]{1,0:T(8,128)S(1)} %get-tuple-element.37), channel_id=1, source_target_pairs={{1,2},{2,1},{3,4},{4,3},{5,6},{6,5},{7,8},{8,7},{9,10},{10,9},{11,... | collective-permute-start | bytes 638984 | tf_op jit(solution)/shard_map/ppermute | solution.py:41
  6.3 3.5 %collective-permute-start.1 = (f32[416,128]{1,0:T(8,128)S(1)}, f32[416,128]{1,0:T(8,128)S(1)}, u32[]{:S(2)}, u32[]{:S(2)}) collective-permute-start(f32[416,128]{1,0:T(8,128)S(1)} %get-tuple-element.38), channel_id=1, source_target_pairs={{0,1},{1,0},{2,3},{3,2},{4,5},{5,4},{6,7},{7,6},{8,9},{9,8},{10,11... | collective-permute-start | bytes 638984 | tf_op jit(solution)/shard_map/ppermute | solution.py:41
  10.7 11.7 %collective-permute-start.3 = (f32[240,128]{1,0:T(8,128)S(1)}, f32[240,128]{1,0:T(8,128)S(1)}, u32[]{:S(2)}, u32[]{:S(2)}) collective-permute-start(f32[240,128]{1,0:T(8,128)S(1)} %get-tuple-element.44), channel_id=1, source_target_pairs={{0,16},{16,0},{32,48},{48,32},{64,80},{80,64},{96,112},{112,96},{1... | collective-permute-start | bytes 368648 | tf_op jit(solution)/shard_map/ppermute | solution.py:41
  13.8 8.6 %collective-permute-start.2 = (f32[232,128]{1,0:T(8,128)S(1)}, f32[232,128]{1,0:T(8,128)S(1)}, u32[]{:S(2)}, u32[]{:S(2)}) collective-permute-start(f32[232,128]{1,0:T(8,128)S(1)} %get-tuple-element.43), channel_id=1, source_target_pairs={{16,32},{32,16},{48,64},{64,48},{80,96},{96,80},{112,128},{128,112... | collective-permute-start | bytes 356360 | tf_op jit(solution)/shard_map/ppermute | solution.py:41

commit v7 on v5

--- a/solution.py
+++ b/solution.py
@@ -61,7 +61,7 @@
     copies = []
     for i, (source, target) in enumerate(zip(sources, copies_of)):
         copy = pltpu.make_async_copy(source, target, sems.at[i])
-        copy.start()
+        copy.start(priority=i % 2)
         copies.append(copy)
 
     for i in range(6):

time: 40.2 us -> 40.2 us (level)
  no operation moved by 1% of the time
where the time goes in v7:
time: 40.2 us; the launch traced here: 40 us
  blocking collectives  15.8 us (39%)
  starting transfers between devices  12.6 us (31%)
  Pallas kernels  8.73 us (22%)
  waiting for transfers between devices  2.09 us (5%)
  between operations  0.69 us (2%)
    all_to_all x1, blocking collectives, shards(): lax.all_to_all(shares, 'gz', split_axis=0, concat_axis=0, tiled=True)  15.8 us
    ppermute x4, starting transfers between devices, swapped(): return lax.ppermute(shard, axis, pairs)  12.6 us
    pallas_call x1, Pallas kernels, shards(): pl.pallas_call(functools.partial(sweep, geometry), out_shape=(array(*e_ch...  4.25 us
    ppermute x4, waiting for transfers between devices, swapped(): return lax.ppermute(shard, axis, pairs)  2.09 us
    pallas_call x1, Pallas kernels, shards(): pl.pallas_call(load_fields, out_shape=tuple((pltpu.VMEM(ref.shape, ref.dt...  1.92 us
    pallas_call x1, Pallas kernels, shards(): pl.pallas_call(functools.partial(response, geometry), out_shape=(array(*e...  0.98 us
    pallas_call x1, Pallas kernels, shards(): pl.pallas_call(functools.partial(edge_planes, geometry), out_shape=(array...  0.83 us
  transfers between devices with their start and end apart: 4, of which 2 were waited for; matrix products, arithmetic and copies ran while one was open for 0% of the time, Pallas kernels for 11%

profile of v7, /device:TPU:385, one launch (start us, length us, event | category | flops | bytes accessed | tf_op | source)
XLA Modules:
  0.0 40.0 jit_solution(3498190119020949591)
XLA Ops:
  0.6 1.9 %load_fields.1 = (f32[3,16,24,128]{3,2,1,0:T(8,128)S(1)}, f32[3,16,24,128]{3,2,1,0:T(8,128)S(1)}, f32[3,16,24,128]{3,2,1,0:T(8,128)S(1)}, f32[3,16,24,128]{3,2,1...) custom-call(f32[3,16,24,128]{3,2,1,0:T(8,128)} %refs_0_.1, ...), custom_call_target="tpu_custom_call" | custom-call | tf_op jit(solution)/shard_map/load_fields/pallas_call | solution.py:599
  2.6 3.8 %collective-permute-start = (f32[416,128]{1,0:T(8,128)S(1)}, f32[416,128]{1,0:T(8,128)S(1)}, u32[]{:S(2)}, u32[]{:S(2)}) collective-permute-start(f32[416,128]{1,0:T(8,128)S(1)} %get-tuple-element.37), channel_id=1, source_target_pairs={{1,2},{2,1},{3,4},{4,3},{5,6},{6,5},{7,8},{8,7},{9,10},{10,9},{11,... | collective-permute-start | bytes 638984 | tf_op jit(solution)/shard_map/ppermute | solution.py:41
  6.3 1.9 %collective-permute-start.1 = (f32[416,128]{1,0:T(8,128)S(1)}, f32[416,128]{1,0:T(8,128)S(1)}, u32[]{:S(2)}, u32[]{:S(2)}) collective-permute-start(f32[416,128]{1,0:T(8,128)S(1)} %get-tuple-element.38), channel_id=1, source_target_pairs={{0,1},{1,0},{2,3},{3,2},{4,5},{5,4},{6,7},{7,6},{8,9},{9,8},{10,11... | collective-permute-start | bytes 638984 | tf_op jit(solution)/shard_map/ppermute | solution.py:41
  8.3 1.6 %collective-permute-done.refs_7_ = f32[416,128]{1,0:T(8,128)S(1)} collective-permute-done((f32[416,128]{1,0:T(8,128)S(1)}, f32[416,128]{1,0:T(8,128)S(1)}, u32[]{:S(2)}, u32[]{:S(2)}) %collective-permute-start) | collective-permute-done | bytes 213024 | tf_op jit(solution)/shard_map/ppermute | solution.py:41
  9.8 0.0 collective-permute-done.1.refs_8_
  9.8 0.8 %edge_planes.1 = (f32[232,128]{1,0:T(8,128)S(1)}, f32[240,128]{1,0:T(8,128)S(1)}) custom-call(s32[6]{0:T(128)S(1)} %get-tuple-element.28.box, s32[3]{0:T(128)S(1)} %get-tuple-element.29.pml, f32[3,16,24,128]{3,2,1,0:T(8,128)S(1)} %get-tuple-element.30.refs_0_, f32[3,16,24,128]{3,2,1,0:T(8,128)S(1)} %get-tuple-element.32.refs_1_, ...), custom_call_target="tpu_custom_call" | custom-call | tf_op jit(solution)/shard_map/edge_planes/pallas_call | solution.py:616
  10.7 3.1 %collective-permute-start.3 = (f32[240,128]{1,0:T(8,128)S(1)}, f32[240,128]{1,0:T(8,128)S(1)}, u32[]{:S(2)}, u32[]{:S(2)}) collective-permute-start(f32[240,128]{1,0:T(8,128)S(1)} %get-tuple-element.44), channel_id=1, source_target_pairs={{0,16},{16,0},{32,48},{48,32},{64,80},{80,64},{96,112},{112,96},{1... | collective-permute-start | bytes 368648 | tf_op jit(solution)/shard_map/ppermute | solution.py:41
  13.8 3.8 %collective-permute-start.2 = (f32[232,128]{1,0:T(8,128)S(1)}, f32[232,128]{1,0:T(8,128)S(1)}, u32[]{:S(2)}, u32[]{:S(2)}) collective-permute-start(f32[232,128]{1,0:T(8,128)S(1)} %get-tuple-element.43), channel_id=1, source_target_pairs={{16,32},{32,16},{48,64},{64,48},{80,96},{96,80},{112,128},{128,112... | collective-permute-start | bytes 356360 | tf_op jit(solution)/shard_map/ppermute | solution.py:41
  17.6 4.2 %sweep.1 = (f32[3,16,24,128]{3,2,1,0:T(8,128)}, f32[3,16,24,128]{3,2,1,0:T(8,128)}, f32[16,128]{1,0:T(8,128)S(1)}, f32[38,32,128]{2,1,0:T(8,128)S(1)}, f32[3,4,2...) custom-call(s32[6]{0:T(128)S(1)} %get-tuple-element.28.box, s32[3]{0:T(128)S(1)} %get-tuple-element.29.pml, ...), custom_call_target="tpu_custom_call" | custom-call | flops 50000000 | bytes 8000000 | tf_op jit(solution)/shard_map/sweep/pallas_call | solution.py:628
  21.9 0.5 %collective-permute-done.2.refs_6_ = f32[232,128]{1,0:T(8,128)S(1)} collective-permute-done((f32[232,128]{1,0:T(8,128)S(1)}, f32[232,128]{1,0:T(8,128)S(1)}, u32[]{:S(2)}, u32[]{:S(2)}) %collective-permute-start.2) | collective-permute-done | bytes 118816 | tf_op jit(solution)/shard_map/ppermute | solution.py:41
  22.4 0.0 collective-permute-done.3.refs_7_
  22.4 1.0 %response.1 = (f32[3,4,24,128]{3,2,1,0:T(8,128)S(1)}, f32[3,4,24,128]{3,2,1,0:T(8,128)S(1)}, f32[128,128]{1,0:T(8,128)S(1)}) custom-call(s32[6]{0:T(128)S(1)} %get-tuple-element.28.box, s32[3]{0:T(128)S(1)} %get-tuple-element.29.pml, f32[3,16,24,128]{3,2,1,0:T(8,128)S(1)} %get-tuple-element.30.refs_0_, ...), custom_call_target="tpu_custom_call" | custom-call | tf_op jit(solution)/shard_map/response/pallas_call | solution.py:651
  23.4 15.8 %all_to_all.11 = f32[16,8,128]{2,1,0:T(8,128)S(1)} all-to-all(f32[16,8,128]{2,1,0:T(8,128)S(1)} %bitcast.4), channel_id=1, replica_groups=mesh['xy'=32,'gz'=16] {'gz'}, dimensions={0} | all-to-all | bytes 131072 | tf_op jit(solution)/shard_map/all_to_all | solution.py:665
  39.2 0.8 %finish.1 = (f32[3,16,24,128]{3,2,1,0:T(8,128)}, f32[3,16,24,128]{3,2,1,0:T(8,128)}, f32[8,16]{1,0:T(8,128)}) custom-call(f32[128,128]{1,0:T(8,128)S(1)} %bitcast.3, f32[3,4,24,128]{3,2,1,0:T(8,128)S(1)} %get-tuple-element.46.edge_e, f32[3,4,24,128]{3,2,1,0:T(8,128)S(1)} %get-tuple-element.47.edge_h, ...), custom_call_target="tpu_custom_call", output_to_operand_aliasing={{0}: (3, {}), {1}: (4, {})} | custom-call | tf_op jit(solution)/shard_map/finish/pallas_call | solution.py:666
Async XLA Ops:
  2.6 7.3 %collective-permute-start = (f32[416,128]{1,0:T(8,128)S(1)}, f32[416,128]{1,0:T(8,128)S(1)}, u32[]{:S(2)}, u32[]{:S(2)}) collective-permute-start(f32[416,128]{1,0:T(8,128)S(1)} %get-tuple-element.37), channel_id=1, source_target_pairs={{1,2},{2,1},{3,4},{4,3},{5,6},{6,5},{7,8},{8,7},{9,10},{10,9},{11,... | collective-permute-start | bytes 638984 | tf_op jit(solution)/shard_map/ppermute | solution.py:41
  6.3 3.5 %collective-permute-start.1 = (f32[416,128]{1,0:T(8,128)S(1)}, f32[416,128]{1,0:T(8,128)S(1)}, u32[]{:S(2)}, u32[]{:S(2)}) collective-permute-start(f32[416,128]{1,0:T(8,128)S(1)} %get-tuple-element.38), channel_id=1, source_target_pairs={{0,1},{1,0},{2,3},{3,2},{4,5},{5,4},{6,7},{7,6},{8,9},{9,8},{10,11... | collective-permute-start | bytes 638984 | tf_op jit(solution)/shard_map/ppermute | solution.py:41
  10.7 11.7 %collective-permute-start.3 = (f32[240,128]{1,0:T(8,128)S(1)}, f32[240,128]{1,0:T(8,128)S(1)}, u32[]{:S(2)}, u32[]{:S(2)}) collective-permute-start(f32[240,128]{1,0:T(8,128)S(1)} %get-tuple-element.44), channel_id=1, source_target_pairs={{0,16},{16,0},{32,48},{48,32},{64,80},{80,64},{96,112},{112,96},{1... | collective-permute-start | bytes 368648 | tf_op jit(solution)/shard_map/ppermute | solution.py:41
  13.8 8.6 %collective-permute-start.2 = (f32[232,128]{1,0:T(8,128)S(1)}, f32[232,128]{1,0:T(8,128)S(1)}, u32[]{:S(2)}, u32[]{:S(2)}) collective-permute-start(f32[232,128]{1,0:T(8,128)S(1)} %get-tuple-element.43), channel_id=1, source_target_pairs={{16,32},{32,16},{48,64},{64,48},{80,96},{96,80},{112,128},{128,112... | collective-permute-start | bytes 356360 | tf_op jit(solution)/shard_map/ppermute | solution.py:41
